TPU v7x, 32 devices: a whole 2x2x4 slice. The times are simulated.
32 devices in a mesh: dp: 16 (over z, y, x), mp: 2 (over core).
Axes of the slice: x: 2, y: 2, z: 4, core: 2. Of those that a mesh axis runs over, the one named last changes fastest.
Arguments:
- features: bfloat16 [4096, 768], P('dp', 'mp'), may hold values from -0.21875 to 0.21875
- labels: int32 [4096], P('dp'), may hold values from 0 to 16383, as said below
- queries: bfloat16 [4096, 768], P('dp', 'mp'), may hold values from -240 to 240
- bank: float32 [16384, 768], P('dp', 'mp'), may hold values from -0.21875 to 0.21875
- old_conc: float32 [16384], P('dp'), may hold values from 0.4 to 0.6
- neg_index: int32 [1024], replicated, may hold values from 0 to 16383, as said below
Outputs:
- new_bank: float32 [16384, 768], P('dp', 'mp')
- new_conc: float32 [16384], P('dp')
- loss: float32 [4096], P('dp')
- grad: float32 [4096, 768], P('dp', 'mp')
Inputs may be any that keep to these rules, and one draw needn't show every extreme that they name: In each aligned block of 256 rows, at most 48 labels fall in any one range of 1024 consecutive prototypes starting at a multiple of 1024; one such range receives exactly 48 labels from every block. `neg_index`: entries j * 64 to (j + 1) * 64 - 1 are distinct prototypes of the range j * 1024 to (j + 1) * 1024 - 1.
All inputs are finite; a program needn't handle non-finite values.
Results may differ from a plain program's by a relative error of at most 0.0074.
Values may be sent and summed in bfloat16 or wider, within the bound.
No kernel may reach another device: no remote copies, remote signals or barrier semaphores. Data moves between devices by JAX's collectives and lax.ppermute only.
A program may use at most 64 MiB of HBM per device.

v0:
```python
import jax
import jax.numpy as jnp
from jax import lax
from jax.sharding import PartitionSpec as P


def combined_all(value, axis, combine):
    everything = jax.tree.map(lambda part: lax.all_gather(part, axis), value)
    first = jax.tree.map(lambda part: part[0], everything)

    def turn(k, so_far):
        return combine(so_far, jax.tree.map(lambda part: part[k], everything))

    return lax.fori_loop(1, lax.axis_size(axis), turn, first)


def merge_softmax(first, second):
    top = jnp.maximum(first[0], second[0])
    total = first[1] * jnp.exp(first[0] - top) + second[1] * jnp.exp(second[0] - top)
    return (top, total)


def body(features, labels, queries, bank, old_conc, neg_index):
    dp_count = lax.axis_size("dp")
    dp_self = lax.axis_index("dp")
    owned = bank.shape[0]
    feat_rows = features.shape[0]
    capacity = 3 * feat_rows // dp_count
    slot_total = dp_count * capacity
    owners = labels // owned
    local = labels - owners * owned
    table = (owners[:, None] == jnp.arange(dp_count, dtype=jnp.int32)[None, :]).astype(jnp.int32)
    running = jnp.cumsum(table, axis=0)
    ranks = jnp.take_along_axis(running, owners[:, None], axis=1)[:, 0] - 1
    slot_of = owners * capacity + ranks
    send_rows = jnp.zeros((slot_total, features.shape[1]), jnp.bfloat16).at[slot_of].set(features)
    send_ids = jnp.full((slot_total,), owned, jnp.int32).at[slot_of].set(local)
    got_rows = lax.all_to_all(send_rows, "dp", split_axis=0, concat_axis=0, tiled=True)
    got_ids = lax.all_to_all(send_ids, "dp", split_axis=0, concat_axis=0, tiled=True)
    onehot = (jnp.arange(owned, dtype=jnp.int32)[:, None] == got_ids[None, :]).astype(jnp.bfloat16)
    sums = jnp.dot(onehot, got_rows, preferred_element_type=jnp.float32)
    counts = jnp.sum(onehot, axis=1, dtype=jnp.float32)
    touched = counts > 0
    safe_counts = jnp.maximum(counts, 1.0)
    blended = 0.5 * bank + 0.5 * sums / safe_counts[:, None]
    new_bank = jnp.where(touched[:, None], blended, bank)
    valid = got_ids < owned
    safe_ids = jnp.minimum(got_ids, owned - 1)
    differ = got_rows.astype(jnp.float32) - new_bank[safe_ids]
    squared = lax.psum(jnp.sum(differ * differ, axis=1), "mp")
    dist = jnp.where(valid, jnp.sqrt(squared + 0.25), 0.0)
    dist_sums = jax.ops.segment_sum(dist, safe_ids, num_segments=owned)
    new_conc = jnp.where(touched, dist_sums / (safe_counts * jnp.log(safe_counts + 10.0)), old_conc)
    scaled = (new_bank / new_conc[:, None]).astype(jnp.bfloat16)
    returned = lax.all_to_all(scaled[safe_ids], "dp", split_axis=0, concat_axis=0, tiled=True)
    pos_rows = returned[slot_of]
    neg_count = neg_index.shape[0] // dp_count
    wanted = lax.dynamic_slice_in_dim(neg_index, dp_self * neg_count, neg_count) - dp_self * owned
    mine = scaled[wanted]
    own_full = lax.all_to_all(mine, "mp", split_axis=0, concat_axis=1, tiled=True)
    neg_full = lax.all_gather(own_full, "dp", axis=0, tiled=True)
    pos_part = jnp.sum(queries.astype(jnp.float32) * pos_rows.astype(jnp.float32), axis=1)
    query_full = lax.all_gather(queries, "mp", axis=1, tiled=True)
    negative = lax.dot_general(
        query_full, neg_full, (((1,), (1,)), ((), ())), preferred_element_type=jnp.float32
    )
    positive = lax.psum(pos_part, "mp")
    local_top = jnp.max(negative, axis=1)
    local_total = jnp.sum(jnp.exp(negative - local_top[:, None]), axis=1)
    merged_top, merged_total = combined_all((local_top, local_total), "mp", merge_softmax)
    top = jnp.maximum(merged_top, positive)
    exppos = jnp.exp(positive - top)
    total = merged_total * jnp.exp(merged_top - top) + exppos
    weight = (jnp.exp(negative - top[:, None]) / total[:, None]).astype(jnp.bfloat16)
    grad_terms = jnp.dot(weight, neg_full, preferred_element_type=jnp.float32)
    grad_negs = lax.psum_scatter(grad_terms, "mp", scatter_dimension=1, tiled=True)
    loss = jnp.log(total) + top - positive
    grad = grad_negs + (exppos / total - 1.0)[:, None] * pos_rows.astype(jnp.float32)
    return (new_bank, new_conc, loss, grad)


def solution(mesh):
    placed = (P("dp", "mp"), P("dp"), P("dp", "mp"), P("dp", "mp"), P("dp"), P())
    return jax.shard_map(
        body,
        mesh=mesh,
        in_specs=placed,
        out_specs=(P("dp", "mp"), P("dp"), P("dp"), P("dp", "mp")),
        check_vma=False,
    )
```

profile of v0, /device:TPU:0, one launch (start us, length us, event | category | flops | bytes accessed | tf_op | source)
XLA Modules:
  0.0 149.8 jit_solution(2523006609633418479)
XLA Ops:
  7.2 0.7 multiply_subtract_fusion
  8.8 2.4 %gather_fusion.4 = s32[256]{0:T(256)S(1)} fusion(s32[256,16]{0,1:T(8,128)S(1)} %bitcast_bitcast_fusion, s32[256]{0:T(256)S(1)} %bitcast.36), kind=kCustom, calls=%fused_computation.4 | custom fusion | bytes 4096 | tf_op jit(solution)/shard_map/jit(take_along_axis)/gather | solution.py:34
  11.2 1.4 scatter_custom_fusion
  12.6 0.7 all_to_all.36
  13.3 8.3 %all-to-all-start = ((s32[16,48,1]{1,2,0:T(1,128)}), s32[16,48,1]{1,2,0:T(1,128)S(1)}, u32[]{:S(2)}, u32[]{:S(2)}) async-start(s32[16,48,1]{1,2,0:T(1,128)} %bitcast.5), calls=%async_computation | async-start | bytes 16384 | tf_op jit(solution)/shard_map/all_to_all | solution.py:39
  21.6 0.6 pad_clamp_fusion
  22.2 0.8 compare_select_fusion.3
  23.6 2.7 %scatter_custom_fusion.1 = bf16[768,384]{1,0:T(8,128)(2,1)} fusion(s32[256]{0:T(256)S(1)} %compare_select_fusion.1, bf16[256,384]{1,0:T(8,128)(2,1)} %param.6, bf16[]{:T(256)} %constant.49.clone.1), kind=kCustom, calls=%fused_computation.22 | custom fusion | bytes 590336 | tf_op jit(solution)/shard_map/scatter | solution.py:36
  26.3 2.5 %all-to-all-done = s32[16,48,1]{1,2,0:T(1,128)S(1)} async-done(((s32[16,48,1]{1,2,0:T(1,128)}), s32[16,48,1]{1,2,0:T(1,128)S(1)}, u32[]{:S(2)}, u32[]{:S(2)}) %all-to-all-start) | async-done | bytes 3104 | tf_op jit(solution)/shard_map/all_to_all | solution.py:39
  28.8 4.4 %all-to-all-start.1 = ((bf16[16,48,384]{2,1,0:T(8,128)(2,1)}), bf16[16,48,384]{2,1,0:T(8,128)(2,1)S(1)}, u32[]{:S(2)}, u32[]{:S(2)}) async-start(bf16[16,48,384]{2,1,0:T(8,128)(2,1)} %bitcast.6), calls=%async_computation.1 | async-start | bytes 1179648 | tf_op jit(solution)/shard_map/all_to_all | solution.py:38
  33.2 2.2 %all_gather.19 = bf16[256,768]{1,0:T(8,128)(2,1)} all-gather(bf16[256,384]{1,0:T(8,128)(2,1)S(1)} %copy-done.2), channel_id=1, replica_groups=mesh['dp'=16,'mp'=2] {'mp'}, dimensions={1}, use_global_device_ids=true | all-gather | bytes 589824 | tf_op jit(solution)/shard_map/all_gather | solution.py:63
  36.0 0.7 fusion.21
  36.7 0.7 reshape.156
  37.9 11.0 %all-to-all-done.1 = bf16[16,48,384]{2,1,0:T(8,128)(2,1)S(1)} async-done(((bf16[16,48,384]{2,1,0:T(8,128)(2,1)}), bf16[16,48,384]{2,1,0:T(8,128)(2,1)S(1)}, u32[]{:S(2)}, u32[]{:S(2)}) %all-to-all-start.1) | async-done | bytes 589856 | tf_op jit(solution)/shard_map/all_to_all | solution.py:38
  49.0 2.5 %add_select_fusion = f32[1024,384]{1,0:T(8,128)S(1)} fusion(f32[1024,384]{1,0:T(8,128)} %param.9, bf16[768,384]{1,0:T(8,128)(2,1)S(1)} %bitcast.39, s32[768]{0:T(1024)S(1)} %eq.37, f32[1024]{0:T(1024)S(1)} %broadcast_maximum_fusion, pred[1024]{0:T(1024)(128)(4,1)S(1)} %broadcast_compare_fusion), kind=kOutput, calls=%fused_computation.13 | convolution fusion | flops 606732288 | bytes 3743744 | tf_op jit(solution)/shard_map/dot_general | solution.py:41
  51.5 2.1 %gather_fusion = f32[768,384]{1,0:T(8,128)S(1)} fusion(f32[1024,384]{1,0:T(8,128)S(1)} %add_select_fusion, s32[1024]{0:T(1024)S(1)} %pad_clamp_fusion.2), kind=kCustom, calls=%fused_computation | custom fusion | bytes 2362368 | tf_op jit(solution)/shard_map/gather | solution.py:49
  53.9 2.5 %psum.14 = f32[768]{0:T(1024)S(1)} all-reduce(f32[768]{0:T(1024)S(1)} %reduce_sum.40), channel_id=1, replica_groups=mesh['dp'=16,'mp'=2] {'mp'}, use_global_device_ids=true, to_apply=%region_6.7 | all-reduce | flops 768 | bytes 6144 | tf_op jit(solution)/shard_map/psum | solution.py:50
  56.4 0.7 sqrt_select_fusion
  57.1 6.0 %scatter_custom_fusion.2 = f32[1024]{0:T(1024)S(1)} fusion(s32[768]{0:T(1024)} %reshape.156, f32[768]{0:T(1024)S(1)} %sqrt_select_fusion, f32[]{:T(128)} %constant.44.clone.1), kind=kCustom, calls=%fused_computation.45 | custom fusion | flops 768 | bytes 4608 | tf_op jit(solution)/shard_map/scatter-add | solution.py:52
  63.1 0.7 divide_select_fusion
  64.0 3.2 %gather_fusion.2 = bf16[768,384]{1,0:T(8,128)(2,1)} fusion(bf16[1024,384]{1,0:T(8,128)(2,1)S(1)} %divide_convert_fusion, s32[1024]{0:T(1024)S(1)} %pad_clamp_fusion.2), kind=kCustom, calls=%fused_computation.2 | custom fusion | bytes 1182720 | tf_op jit(solution)/shard_map/gather | solution.py:55
  67.2 1.0 gather_fusion.1
  68.2 3.8 %all_to_all.52 = bf16[2,32,384]{2,1,0:T(8,128)(2,1)S(1)} all-to-all(bf16[2,32,384]{2,1,0:T(8,128)(2,1)S(1)} %bitcast.42), channel_id=1, replica_groups=mesh['dp'=16,'mp'=2] {'mp'}, dimensions={0} | all-to-all | bytes 98304 | tf_op jit(solution)/shard_map/all_to_all | solution.py:60
  72.0 4.1 %all-to-all-start.3 = ((bf16[16,48,384]{2,1,0:T(8,128)(2,1)}), bf16[16,48,384]{2,1,0:T(8,128)(2,1)S(1)}, u32[]{:S(2)}, u32[]{:S(2)}) async-start(bf16[16,48,384]{2,1,0:T(8,128)(2,1)} %bitcast.17), calls=%async_computation.3 | async-start | bytes 1179648 | tf_op jit(solution)/shard_map/all_to_all | solution.py:55
  76.2 48.9 %all_gather.18 = bf16[512,768]{1,0:T(8,128)(2,1)S(1)} all-gather(bf16[32,768]{1,0:T(8,128)(2,1)S(1)} %bitcast.40), channel_id=1, replica_groups=mesh['dp'=16,'mp'=2] {'dp'}, dimensions={0}, use_global_device_ids=true | all-gather | bytes 835584 | tf_op jit(solution)/shard_map/all_gather | solution.py:61
  125.6 1.8 %all-gather.2 = f32[2,1,256]{2,1,0:T(1,128)S(1)} all-gather(f32[1,1,256]{2,1,0:T(1,128)S(1)} %bitcast.46), channel_id=2, replica_groups=mesh['dp'=16,'mp'=2] {'mp'}, dimensions={0}, use_global_device_ids=true | all-gather | bytes 3072 | tf_op jit(solution)/shard_map/all_gather | solution.py:8
  127.4 1.8 %all-gather.3 = f32[2,1,256]{2,1,0:T(1,128)S(1)} all-gather(f32[1,1,256]{2,1,0:T(1,128)S(1)} %bitcast.45), channel_id=3, replica_groups=mesh['dp'=16,'mp'=2] {'mp'}, dimensions={0}, use_global_device_ids=true | all-gather | bytes 3072 | tf_op jit(solution)/shard_map/all_gather | solution.py:8
  129.2 1.3 gather_fusion.3
  130.6 2.5 %psum.15 = f32[256]{0:T(256)S(1)} all-reduce(f32[256]{0:T(256)S(1)} %fusion.3), channel_id=1, replica_groups=mesh['dp'=16,'mp'=2] {'mp'}, use_global_device_ids=true, to_apply=%region_11.12 | all-reduce | flops 256 | bytes 2048 | tf_op jit(solution)/shard_map/psum | solution.py:67
  133.1 1.3 fusion.7
  135.0 6.2 %reduce-scatter.2.cloned.1.call-done = f32[256,384]{1,0:T(8,128)} async-done(((f32[256,768]{1,0:T(8,128)}), f32[256,384]{1,0:T(8,128)}) %reduce-scatter.2.cloned.1.call-update) | async-done | bytes 393232 | tf_op jit(solution)/shard_map/reduce_scatter | solution.py:76
  141.1 1.8 %fusion.4 = f32[256,384]{1,0:T(8,128)} fusion(f32[256,384]{1,0:T(8,128)} %reduce-scatter.2.cloned.1.call-done, bf16[256,384]{1,0:T(8,128)(2,1)S(1)} %gather_fusion.3, f32[256]{0:T(256)S(1)} %get-tuple-element.24), kind=kLoop, calls=%fused_computation.21 | loop fusion | flops 294912 | bytes 984064 | tf_op jit(solution)/shard_map/add | solution.py:78
  (44 shorter events, 4.5 us)
Async XLA Ops:
  7.9 25.4 %copy-start.2 = (bf16[256,384]{1,0:T(8,128)(2,1)S(1)}, bf16[256,384]{1,0:T(8,128)(2,1)}, u32[]{:S(2)}) copy-start(bf16[256,384]{1,0:T(8,128)(2,1)} %param.8) | copy-start | bytes 589828
  13.3 15.5 %all-to-all-start = ((s32[16,48,1]{1,2,0:T(1,128)}), s32[16,48,1]{1,2,0:T(1,128)S(1)}, u32[]{:S(2)}, u32[]{:S(2)}) async-start(s32[16,48,1]{1,2,0:T(1,128)} %bitcast.5), calls=%async_computation | async-start | bytes 16384 | tf_op jit(solution)/shard_map/all_to_all | solution.py:39
  28.8 20.1 %all-to-all-start.1 = ((bf16[16,48,384]{2,1,0:T(8,128)(2,1)}), bf16[16,48,384]{2,1,0:T(8,128)(2,1)S(1)}, u32[]{:S(2)}, u32[]{:S(2)}) async-start(bf16[16,48,384]{2,1,0:T(8,128)(2,1)} %bitcast.6), calls=%async_computation.1 | async-start | bytes 1179648 | tf_op jit(solution)/shard_map/all_to_all | solution.py:38
  37.5 11.5 %copy-start.4 = (s32[768]{0:T(1024)}, s32[768]{0:T(1024)S(1)}, u32[]{:S(2)}) copy-start(s32[768]{0:T(1024)S(1)} %eq.37) | copy-start | bytes 9220
  51.4 12.3 %copy-start = (f32[1024,384]{1,0:T(8,128)}, f32[1024,384]{1,0:T(8,128)S(1)}, u32[]{:S(2)}) copy-start(f32[1024,384]{1,0:T(8,128)S(1)} %add_select_fusion) | copy-start | bytes 4718596
  63.8 3.5 %copy-start.3 = (f32[1024]{0:T(1024)}, f32[1024]{0:T(1024)S(1)}, u32[]{:S(2)}) copy-start(f32[1024]{0:T(1024)S(1)} %divide_select_fusion) | copy-start | bytes 12292
  67.2 57.8 %copy-start.1 = (bf16[256,768]{1,0:T(8,128)(2,1)S(1)}, bf16[256,768]{1,0:T(8,128)(2,1)}, u32[]{:S(2)}) copy-start(bf16[256,768]{1,0:T(8,128)(2,1)} %all_gather.19) | copy-start | bytes 1179652
  72.0 57.2 %all-to-all-start.3 = ((bf16[16,48,384]{2,1,0:T(8,128)(2,1)}), bf16[16,48,384]{2,1,0:T(8,128)(2,1)S(1)}, u32[]{:S(2)}, u32[]{:S(2)}) async-start(bf16[16,48,384]{2,1,0:T(8,128)(2,1)} %bitcast.17), calls=%async_computation.3 | async-start | bytes 1179648 | tf_op jit(solution)/shard_map/all_to_all | solution.py:55
  76.1 65.0 %reduce-scatter.2.cloned.1.call-start = ((), (), s32[]{:S(2)}) async-start(), calls=%async_computation.5 | async-start | bytes 1179648 | tf_op jit(solution)/shard_map/reduce_scatter | solution.py:76
Sparse Core Ops, SparseCore 0:
  134.5 6.5 reduce-scatter.1
where the time goes:
time: 151 us; the launch traced here: 150 us
  blocking collectives  63.3 us (42%)
  waiting for transfers between devices  19.7 us (13%)
  starting transfers between devices  16.9 us (11%)
  local copies, waits for them, and re-layouts  16.5 us (11%)
  other arithmetic  15 us (10%)
  between operations  14.2 us (9%)
  matrix products  4.18 us (3%)
    all_gather x1, blocking collectives, body(): neg_full = lax.all_gather(own_full, 'dp', axis=0, tiled=True)  48.9 us
    all_to_all x1, waiting for transfers between devices, body(): lax.all_to_all(send_rows, 'dp', split_axis=0, concat_axis=0, tiled=True)  11 us
    all_to_all x1, starting transfers between devices, body(): lax.all_to_all(send_ids, 'dp', split_axis=0, concat_axis=0, tiled=True)  8.31 us
    reduce_scatter x1, waiting for transfers between devices, body(): lax.psum_scatter(grad_terms, 'mp', scatter_dimension=1, tiled=True)  6.17 us
    scatter-add x1, other arithmetic, body(): dist_sums = jax.ops.segment_sum(dist, safe_ids, num_segments=owned)  5.99 us
    all_to_all x1, starting transfers between devices, body(): lax.all_to_all(send_rows, 'dp', split_axis=0, concat_axis=0, tiled=True)  4.4 us
    all_to_all x1, starting transfers between devices, body(): lax.all_to_all(scaled[safe_ids], 'dp', split_axis=0, concat_axis=0, tiled...  4.15 us
    all_to_all x1, blocking collectives, body(): lax.all_to_all(mine, 'mp', split_axis=0, concat_axis=1, tiled=True)  3.77 us
  transfers between devices with their start and end apart: 4, of which 3 were waited for; matrix products, arithmetic and copies ran while one was open for 6% of the time, Pallas kernels for 0%

commit v1 on v0

v1 whole, which is shorter than its diff:
```python
import functools

import jax
import jax.numpy as jnp
from jax import lax
from jax.experimental import pallas as pl
from jax.experimental.pallas import tpu as pltpu
from jax.sharding import PartitionSpec as P

F32 = jnp.float32
BF16 = jnp.bfloat16
I32 = jnp.int32
LANES = 128


def call(kernel, outs, *args, flops=0, in_smem=()):
    moved = sum(a.size * a.dtype.itemsize for a in args) + sum(o.size * o.dtype.itemsize for o in outs)
    specs = [
        pl.BlockSpec(memory_space=pltpu.SMEM if k in in_smem else pltpu.VMEM) for k in range(len(args))
    ]
    return pl.pallas_call(
        kernel,
        out_shape=list(outs),
        in_specs=specs,
        out_specs=[pl.BlockSpec(memory_space=pltpu.VMEM) for _ in outs],
        compiler_params=pltpu.CompilerParams(vmem_limit_bytes=40 * 2**20),
        cost_estimate=pl.CostEstimate(flops=flops, bytes_accessed=moved, transcendentals=0),
    )(*args)


def shape(dims, dtype):
    return jax.ShapeDtypeStruct(dims, dtype)


def nt(a, b):
    return lax.dot_general(a, b, (((1,), (1,)), ((), ())), preferred_element_type=F32)


def nn(a, b):
    return jnp.dot(a, b, preferred_element_type=F32)


def to_col(row):
    return jnp.transpose(jnp.broadcast_to(row, (LANES, row.shape[1])))


def to_row(col):
    return jnp.transpose(jnp.broadcast_to(col, (col.shape[0], LANES)))[0:1, :]


def upper(rows):
    before = lax.broadcasted_iota(I32, (rows, rows), 0)
    return jnp.where(before <= lax.broadcasted_iota(I32, (rows, rows), 1), 1.0, 0.0).astype(BF16)


def pack_kernel(owners, owned, capacity, label_ref, feat_ref, send_ref, slot_ref):
    rows = label_ref.shape[1]
    label = label_ref[...]
    start = lax.broadcasted_iota(I32, (owners, rows), 0) * owned
    mine = (label >= start) & (label < start + owned)
    table = jnp.where(mine, 1.0, 0.0)
    running = nn(table.astype(BF16), upper(rows))
    place = running - 1.0 + (lax.broadcasted_iota(I32, (owners, rows), 0) * capacity).astype(F32)
    slot = jnp.sum(jnp.where(mine, place, 0.0), axis=0, keepdims=True).astype(I32)
    slot_ref[...] = slot
    pick = jnp.where(lax.broadcasted_iota(I32, (owners * capacity, rows), 0) == slot, 1.0, 0.0).astype(BF16)
    send_ref[...] = nn(pick, feat_ref[...]).astype(BF16)


def ids_kernel(owned, capacity, self_ref, label_ref, row_ref, col_ref):
    owners, rows = label_ref.shape
    slots = row_ref.shape[1]
    me = self_ref[0]
    local = label_ref[...] - me * owned
    mine = (local >= 0) & (local < owned)
    rank = nn(jnp.where(mine, 1.0, 0.0).astype(BF16), upper(rows)) - 1.0
    rank = jnp.where(mine, rank, -1.0)
    value = local.astype(F32) + 1.0
    lane = lax.broadcasted_iota(I32, (owners, LANES), 1)
    table = jnp.zeros((owners, LANES), F32)
    for j in range(capacity):
        found = jnp.sum(jnp.where(rank == float(j), value, 0.0), axis=1, keepdims=True)
        table = jnp.where(lane == j, found, table)
    high = jnp.floor(table * (1.0 / 32.0))
    low = table - 32.0 * high
    place = lax.broadcasted_iota(I32, (LANES, slots), 1).astype(F32)
    within = place - capacity * jnp.floor((place + 0.5) * (1.0 / capacity))
    spread = jnp.where(within == lax.broadcasted_iota(I32, (LANES, slots), 0).astype(F32), 1.0, 0.0).astype(BF16)
    wide = 32.0 * nn(high.astype(BF16), spread) + nn(low.astype(BF16), spread)
    first = (lax.broadcasted_iota(I32, (owners, slots), 0) ^ me) * capacity
    spot = lax.broadcasted_iota(I32, (owners, slots), 1)
    own_block = (spot >= first) & (spot < first + capacity)
    ids = jnp.sum(jnp.where(own_block, wide, 0.0), axis=0, keepdims=True)
    ids = jnp.where(ids > 0.5, ids - 1.0, float(owned))
    row_ref[...] = ids.astype(I32)
    col_ref[...] = to_col(ids).astype(I32)


def blend(bank, sums, counts):
    safe = jnp.maximum(counts, 1.0)
    return jnp.where(counts > 0, 0.5 * bank + 0.5 * sums / safe, bank)


def mean_kernel(row_ref, col_ref, neg_ref, got_ref, bank_ref, new_ref, pack_ref):
    slots, width = got_ref.shape
    negs = neg_ref.shape[0]
    half = negs // 2
    ids = row_ref[...]
    got = got_ref[...]
    same = jnp.where(col_ref[:, 0:1] == ids, 1.0, 0.0)
    new = blend(bank_ref[0:slots, :], nn(same.astype(BF16), got), jnp.sum(same, axis=1, keepdims=True))
    new_ref[0:slots, :] = new
    differ = got.astype(F32) - new
    squared = to_row(jnp.sum(differ * differ, axis=1, keepdims=True))
    same = jnp.where(neg_ref[:, 0:1] == ids, 1.0, 0.0)
    new = blend(bank_ref[slots:, :], nn(same.astype(BF16), got), jnp.sum(same, axis=1, keepdims=True))
    new_ref[slots:, :] = new[0:half]
    pack_ref[0:half, :] = new[half:]
    for k in range(slots // width):
        pack_ref[half + k : half + k + 1, :] = squared[:, k * width : (k + 1) * width]


def concentration(same, dist, old):
    counts = jnp.sum(jnp.where(same, 1.0, 0.0), axis=1, keepdims=True)
    total = jnp.sum(jnp.where(same, dist, 0.0), axis=1, keepdims=True)
    safe = jnp.maximum(counts, 1.0)
    return jnp.where(counts > 0, total / (safe * jnp.log(safe + 10.0)), old)


def scale_kernel(row_ref, col_ref, neg_ref, old_ref, new_ref, pack_ref, other_ref, slot_ref, full_ref, dist_ref):
    slots, width = slot_ref.shape
    half = full_ref.shape[0]
    ids = row_ref[...]
    tail = slice(half, half + slots // width)
    squared = pack_ref[tail, :] + other_ref[tail, :]
    squared = jnp.concatenate([squared[k : k + 1, :] for k in range(slots // width)], axis=1)
    dist = jnp.sqrt(squared + 0.25)
    dist_ref[...] = dist
    conc = concentration(col_ref[:, 0:1] == ids, dist, 1.0)
    slot_ref[...] = (new_ref[0:slots, :] / conc).astype(BF16)
    conc = concentration(neg_ref[0:half, 0:1] == ids, dist, old_ref[:, 0:1])
    full_ref[:, 0:width] = (new_ref[slots:, :] / conc).astype(BF16)
    full_ref[:, width:] = (other_ref[0:half, :] / conc).astype(BF16)


def owner_kernel(row_ref, col_ref, dist_ref, got_ref, bank_ref, old_ref, new_ref, conc_ref):
    block = bank_ref.shape[0]
    slots = got_ref.shape[0]
    base = pl.program_id(0) * block
    same = jnp.where(lax.broadcasted_iota(I32, (block, slots), 0) + base == row_ref[...], 1.0, 0.0)
    sums = nn(same.astype(BF16), got_ref[...])
    new_ref[...] = blend(bank_ref[...], sums, jnp.sum(same, axis=1, keepdims=True))
    turned = lax.broadcasted_iota(I32, (slots, block), 1) + base == col_ref[:, 0:1]
    counts = jnp.sum(jnp.where(turned, 1.0, 0.0), axis=0, keepdims=True)
    total = jnp.sum(jnp.where(turned, to_col(dist_ref[...])[:, 0:1], 0.0), axis=0, keepdims=True)
    safe = jnp.maximum(counts, 1.0)
    conc_ref[...] = jnp.where(counts > 0, total / (safe * jnp.log(safe + 10.0)), old_ref[...])


def owner_call(row, col, dist, got, bank, old):
    owned, width = bank.shape
    slots = got.shape[0]
    block = 256
    whole = lambda k: (0, 0)
    return pl.pallas_call(
        owner_kernel,
        grid=(owned // block,),
        in_specs=[
            pl.BlockSpec((1, slots), whole),
            pl.BlockSpec((slots, LANES), whole),
            pl.BlockSpec((1, slots), whole),
            pl.BlockSpec((slots, width), whole),
            pl.BlockSpec((block, width), lambda k: (k, 0)),
            pl.BlockSpec((1, block), lambda k: (0, k)),
        ],
        out_specs=[pl.BlockSpec((block, width), lambda k: (k, 0)), pl.BlockSpec((1, block), lambda k: (0, k))],
        out_shape=[shape((owned, width), F32), shape((1, owned), F32)],
        compiler_params=pltpu.CompilerParams(vmem_limit_bytes=40 * 2**20),
        cost_estimate=pl.CostEstimate(
            flops=2 * owned * slots * width, bytes_accessed=8 * owned * width, transcendentals=0
        ),
    )(row, col, dist, got, bank, old)


def flash_kernel(width, mine_ref, other_ref, *refs):
    parts, (keep_ref, stats_ref, send_ref) = refs[:-3], refs[-3:]
    rows = mine_ref.shape[0]
    mine, other = mine_ref[...], other_ref[...]
    logits = [nt(mine, p[:, 0:width]) + nt(other, p[:, width:]) for p in parts]
    top = functools.reduce(jnp.maximum, [jnp.max(l, axis=1, keepdims=True) for l in logits])
    total = jnp.zeros((rows, 1), F32)
    grad = jnp.zeros((rows, 2 * width), F32)
    for l, p in zip(logits, parts):
        weight = jnp.exp(l - top)
        total = total + jnp.sum(weight, axis=1, keepdims=True)
        grad = grad + nn(weight.astype(BF16), p[...])
    keep_ref[...] = grad[:, 0:width]
    send_ref[0:rows, :] = grad[:, width:]
    stats = jnp.concatenate([to_row(top), to_row(total)], axis=0)
    stats_ref[0:2, :] = stats
    send_ref[rows : rows + 2, 0:rows] = stats


def positive_kernel(slot_ref, back_ref, query_ref, rows_ref, part_ref):
    rows, slots = query_ref.shape[0], back_ref.shape[0]
    slot = to_col(slot_ref[...].astype(F32))[:, 0:1].astype(I32)
    pick = jnp.where(lax.broadcasted_iota(I32, (rows, slots), 1) == slot, 1.0, 0.0).astype(BF16)
    found = nn(pick, back_ref[...])
    rows_ref[...] = found.astype(BF16)
    part = to_row(jnp.sum(query_ref[...].astype(F32) * found, axis=1, keepdims=True))
    part_ref[...] = jnp.broadcast_to(part, part_ref.shape)


def final_kernel(self_ref, part_ref, far_ref, stats_ref, keep_ref, sent_ref, rows_ref, loss_ref, grad_ref):
    rows = keep_ref.shape[0]
    first = self_ref[0] == 0
    here, there = stats_ref[0:2, :], sent_ref[rows : rows + 2, 0:rows]
    low = jnp.where(first, here, there)
    high = jnp.where(first, there, here)
    positive = part_ref[0:1, :] + far_ref[0:1, :]
    top = jnp.maximum(jnp.maximum(low[0:1], high[0:1]), positive)
    exppos = jnp.exp(positive - top)
    total = low[1:2] * jnp.exp(low[0:1] - top) + high[1:2] * jnp.exp(high[0:1] - top) + exppos
    loss_ref[...] = jnp.log(total) + top - positive
    mine = to_col(jnp.exp(here[0:1] - top) / total)[:, 0:1]
    other = to_col(jnp.exp(there[0:1] - top) / total)[:, 0:1]
    pull = to_col(exppos / total - 1.0)[:, 0:1]
    grad_ref[...] = keep_ref[...] * mine + sent_ref[0:rows, :] * other + pull * rows_ref[...].astype(F32)


def swap(value):
    return lax.ppermute(value, "mp", [(0, 1), (1, 0)])


def hop(value, count, bits):
    return lax.ppermute(value, "dp", [(k, k ^ bits) for k in range(count)])


def spread(value, count):
    held, done = value, 1
    pieces = [value]
    while done < count:
        step = min(4, count // done)
        stride = count // (done * step)
        pieces = [held] + [hop(held, count, stride * k) for k in range(1, step)]
        done *= step
        if done < count:
            held = jnp.concatenate(pieces, axis=0)
    return pieces


def gathered_labels(labels, count):
    held = labels.reshape(1, -1)
    bit = 1
    while bit < count:
        held = jnp.concatenate([held, hop(held, count, bit)], axis=0)
        bit *= 2
    return held


def body(features, labels, queries, bank, old_conc, neg_index):
    count = lax.axis_size("dp")
    me, core = lax.axis_index("dp"), lax.axis_index("mp")
    owned, width = bank.shape
    rows = features.shape[0]
    capacity = 3 * rows // count
    slots = count * capacity
    negs = neg_index.shape[0] // count
    half = negs // 2
    me_ref, core_ref = me.astype(I32).reshape(1), core.astype(I32).reshape(1)

    label_row = labels.reshape(1, rows)
    send, slot = call(
        functools.partial(pack_kernel, count, owned, capacity),
        (shape((slots, width), BF16), shape((1, rows), I32)),
        label_row, features, flops=2 * slots * rows * width,
    )
    got = lax.all_to_all(send.reshape(count, capacity, width), "dp", split_axis=0, concat_axis=0)
    got = got.reshape(slots, width)

    query_far = swap(queries)
    ids_row, ids_col = call(
        functools.partial(ids_kernel, owned, capacity),
        (shape((1, slots), I32), shape((slots, LANES), I32)),
        me_ref, gathered_labels(labels, count), in_smem=(0,),
    )
    start = me * negs
    near = lax.dynamic_slice_in_dim(neg_index, start + core * half, half) - me * owned
    far = lax.dynamic_slice_in_dim(neg_index, start + (1 - core) * half, half) - me * owned
    both = jnp.concatenate([near, far])
    held = bank[jnp.concatenate([jnp.minimum(ids_row.reshape(slots), owned - 1), both])]
    neg_col = jnp.broadcast_to(both[:, None], (negs, LANES))
    old_col = jnp.broadcast_to(old_conc[near][:, None], (half, LANES))

    extra = 8 * -(-(slots // width) // 8)
    new, pack = call(
        mean_kernel,
        (shape((slots + half, width), F32), shape((half + extra, width), F32)),
        ids_row, ids_col, neg_col, got, held, flops=2 * (slots + negs) * slots * width,
    )
    scaled, full, dist = call(
        scale_kernel,
        (shape((slots, width), BF16), shape((half, 2 * width), BF16), shape((1, slots), F32)),
        ids_row, ids_col, neg_col, old_col, new, pack, swap(pack),
    )
    back = lax.all_to_all(scaled.reshape(count, capacity, width), "dp", split_axis=0, concat_axis=0)
    pieces = spread(full, count)
    new_bank, new_conc = owner_call(ids_row, ids_col, dist, got, bank, old_conc.reshape(1, owned))
    keep, stats, sent = call(
        functools.partial(flash_kernel, width),
        (shape((rows, width), F32), shape((8, rows), F32), shape((rows + 8, width), F32)),
        queries, query_far, *pieces, flops=8 * rows * half * count * width,
    )
    sent = swap(sent)
    found, part = call(
        positive_kernel,
        (shape((rows, width), BF16), shape((8, rows), F32)),
        slot, back.reshape(slots, width), queries, flops=2 * slots * rows * width,
    )
    loss, grad = call(
        final_kernel,
        (shape((1, rows), F32), shape((rows, width), F32)),
        core_ref, part, swap(part), stats, keep, sent, found, in_smem=(0,),
    )
    return (new_bank, new_conc.reshape(owned), loss.reshape(rows), grad)


def solution(mesh):
    placed = (P("dp", "mp"), P("dp"), P("dp", "mp"), P("dp", "mp"), P("dp"), P())
    return jax.shard_map(
        body,
        mesh=mesh,
        in_specs=placed,
        out_specs=(P("dp", "mp"), P("dp"), P("dp"), P("dp", "mp")),
        check_vma=False,
    )
```

time: 151 us -> 91.3 us (0.60)
  blocking collectives: 63.3 us -> 0 us
  other arithmetic: 15 us -> 1.05 us
  between operations: 14.2 us -> 0.83 us
  starting transfers between devices: 16.9 us -> 29.9 us
  Pallas kernels: 0 us -> 11.8 us
  waiting for transfers between devices: 19.7 us -> 30.9 us
  matrix products: 4.18 us -> 0 us
    all_gather x4 -> x0, blocking collectives: 54.7 us -> none  [the longest x1 48.9 us: body(): neg_full = lax.all_gather(own_full, 'dp', axis=0, tiled=True)]
    ppermute x0 -> x14, waiting for transfers between devices: none -> 30.9 us  [the longest x10 30.3 us: hop(): return lax.ppermute(value, 'dp', [(k, k ^ bits) for k in range(count)])]
    ppermute x0 -> x14, starting transfers between devices: none -> 15.7 us  [the longest x10 15.1 us: hop(): return lax.ppermute(value, 'dp', [(k, k ^ bits) for k in range(count)])]
    all_to_all x3 -> x2, waiting for transfers between devices: 13.5 us -> 0.01 us  [the longest x1 0.01 us: body(): lax.all_to_all(send.reshape(count, capacity, width), 'dp', split_axis=0,...]
    unnamed x11 -> x49, local copies, waits for them, and re-layouts: 0.03 us -> 12.6 us
    pallas_call x0 -> x8, Pallas kernels: none -> 11.8 us  [the longest x7 8.81 us: call(): pl.pallas_call(kernel, out_shape=list(outs), in_specs=specs, out_specs=[p...]
    gather x5 -> x2, local copies, waits for them, and re-layouts: 10 us -> 3.53 us  [the longest x1 2.86 us: body(): bank[jnp.concatenate([jnp.minimum(ids_row.reshape(slots), owned - 1), bot...]
    reduce_scatter x1 -> x0, waiting for transfers between devices: 6.17 us -> none  [body(): lax.psum_scatter(grad_terms, 'mp', scatter_dimension=1, tiled=True)]
  transfers between devices with their start and end apart: 4 -> 16, of which waited for: 3 -> 9; matrix products, arithmetic and copies ran while one was open for 6% -> 6% of each run, Pallas kernels for 0% -> 7%
where the time goes in v1:
time: 91.3 us; the launch traced here: 90.7 us
  waiting for transfers between devices  30.9 us (34%)
  starting transfers between devices  29.9 us (33%)
  local copies, waits for them, and re-layouts  16.3 us (18%)
  Pallas kernels  11.8 us (13%)
  other arithmetic  1.05 us (1%)
    ppermute x10, waiting for transfers between devices, hop(): return lax.ppermute(value, 'dp', [(k, k ^ bits) for k in range(count)])  30.3 us
    ppermute x10, starting transfers between devices, hop(): return lax.ppermute(value, 'dp', [(k, k ^ bits) for k in range(count)])  15.1 us
    unnamed x49, local copies, waits for them, and re-layouts  12.6 us
    pallas_call x7, Pallas kernels, call(): pl.pallas_call(kernel, out_shape=list(outs), in_specs=specs, out_specs=[p...  8.81 us
    all_to_all x1, starting transfers between devices, body(): lax.all_to_all(send.reshape(count, capacity, width), 'dp', split_axis=0,...  8.31 us
    all_to_all x1, starting transfers between devices, body(): lax.all_to_all(scaled.reshape(count, capacity, width), 'dp', split_axis=0...  5.86 us
    pallas_call x1, Pallas kernels, owner_call(): pl.pallas_call(owner_kernel, grid=(owned // block,), in_specs=[pl.BlockSp...  3.03 us
    gather x1, local copies, waits for them, and re-layouts, body(): bank[jnp.concatenate([jnp.minimum(ids_row.reshape(slots), owned - 1), bot...  2.86 us
  transfers between devices with their start and end apart: 16, of which 9 were waited for; matrix products, arithmetic and copies ran while one was open for 6% of the time, Pallas kernels for 7%

profile of v1, /device:TPU:0, one launch (start us, length us, event | category | flops | bytes accessed | tf_op | source)
XLA Modules:
  0.0 90.7 jit_solution(2661462505744674977)
XLA Ops:
  1.4 0.9 %copy-done.22 = bf16[256,384]{1,0:T(8,128)(2,1)S(1)} copy-done((bf16[256,384]{1,0:T(8,128)(2,1)S(1)}, bf16[256,384]{1,0:T(8,128)(2,1)}, u32[]{:S(2)}) %copy-start.22) | copy-done | bytes 196632
  2.4 1.3 %shard_map.94 = (bf16[768,384]{1,0:T(8,128)(2,1)}, s32[1,256]{1,0:T(1,128)S(1)}) custom-call(s32[1,256]{1,0:T(1,128)S(1)} %bitcast.18, bf16[256,384]{1,0:T(8,128)(2,1)S(1)} %copy-done.22), custom_call_target="tpu_custom_call" | custom-call | flops 150994944 | bytes 788480 | tf_op jit(solution)/shard_map/pallas_call | solution.py:21
  4.3 8.3 %all-to-all-start = ((bf16[16,48,384]{2,1,0:T(8,128)(2,1)}), bf16[16,48,384]{2,1,0:T(8,128)(2,1)S(1)}, u32[]{:S(2)}, u32[]{:S(2)}) async-start(bf16[16,48,384]{2,1,0:T(8,128)(2,1)} %bitcast.2), calls=%async_computation | async-start | bytes 1179648 | tf_op jit(solution)/shard_map/all_to_all | solution.py:278
  12.6 2.0 %collective-permute-start = (s32[1,256]{1,0:T(1,128)S(1)}, s32[1,256]{1,0:T(1,128)S(1)}, u32[]{:S(2)}, u32[]{:S(2)}) collective-permute-start(s32[1,256]{1,0:T(1,128)S(1)} %bitcast.19), channel_id=1, source_target_pairs={{0,2},{2,0},{4,6},{6,4},{8,10},{10,8},{12,14},{14,12},{16,18},{18,... | collective-permute-start | bytes 3080 | tf_op jit(solution)/shard_map/ppermute | solution.py:236
  14.6 2.7 %collective-permute-done = s32[1,256]{1,0:T(1,128)S(1)} collective-permute-done((s32[1,256]{1,0:T(1,128)S(1)}, s32[1,256]{1,0:T(1,128)S(1)}, u32[]{:S(2)}, u32[]{:S(2)}) %collective-permute-start) | collective-permute-done | bytes 1056 | tf_op jit(solution)/shard_map/ppermute | solution.py:236
  17.3 1.5 %collective-permute-start.1 = (s32[2,256]{1,0:T(2,128)S(1)}, s32[2,256]{1,0:T(2,128)S(1)}, u32[]{:S(2)}, u32[]{:S(2)}) collective-permute-start(s32[2,256]{1,0:T(2,128)S(1)} %pad_add_fusion.2), channel_id=1, source_target_pairs={{0,4},{2,6},{4,0},{6,2},{8,12},{10,14},{12,8},{14,10},{16,20},{18,... | collective-permute-start | bytes 6152 | tf_op jit(solution)/shard_map/ppermute | solution.py:236
  18.8 2.1 %collective-permute-done.1 = s32[2,256]{1,0:T(2,128)S(1)} collective-permute-done((s32[2,256]{1,0:T(2,128)S(1)}, s32[2,256]{1,0:T(2,128)S(1)}, u32[]{:S(2)}, u32[]{:S(2)}) %collective-permute-start.1) | collective-permute-done | bytes 2080 | tf_op jit(solution)/shard_map/ppermute | solution.py:236
  20.9 1.3 %collective-permute-start.2 = (s32[4,256]{1,0:T(4,128)S(1)}, s32[4,256]{1,0:T(4,128)S(1)}, u32[]{:S(2)}, u32[]{:S(2)}) collective-permute-start(s32[4,256]{1,0:T(4,128)S(1)} %pad_add_fusion.1), channel_id=1, source_target_pairs={{0,8},{2,10},{4,12},{6,14},{8,0},{10,2},{12,4},{14,6},{16,24},{18,... | collective-permute-start | bytes 12296 | tf_op jit(solution)/shard_map/ppermute | solution.py:236
  22.2 0.8 compare_select_fusion.1
  23.1 1.5 %collective-permute-done.2 = s32[4,256]{1,0:T(4,128)S(1)} collective-permute-done((s32[4,256]{1,0:T(4,128)S(1)}, s32[4,256]{1,0:T(4,128)S(1)}, u32[]{:S(2)}, u32[]{:S(2)}) %collective-permute-start.2) | collective-permute-done | bytes 4128 | tf_op jit(solution)/shard_map/ppermute | solution.py:236
  24.6 2.3 %collective-permute-start.3 = (s32[8,256]{1,0:T(8,128)S(1)}, s32[8,256]{1,0:T(8,128)S(1)}, u32[]{:S(2)}, u32[]{:S(2)}) collective-permute-start(s32[8,256]{1,0:T(8,128)S(1)} %pad_add_fusion), channel_id=1, source_target_pairs={{0,16},{2,18},{4,20},{6,22},{8,24},{10,26},{12,28},{14,30},{16,0},... | collective-permute-start | bytes 24584 | tf_op jit(solution)/shard_map/ppermute | solution.py:236
  27.0 2.2 %collective-permute-done.3 = s32[8,256]{1,0:T(8,128)S(1)} collective-permute-done((s32[8,256]{1,0:T(8,128)S(1)}, s32[8,256]{1,0:T(8,128)S(1)}, u32[]{:S(2)}, u32[]{:S(2)}) %collective-permute-start.3) | collective-permute-done | bytes 8224 | tf_op jit(solution)/shard_map/ppermute | solution.py:236
  30.8 2.9 %gather_fusion.1 = f32[832,384]{1,0:T(8,128)S(1)} fusion(f32[1024,384]{1,0:T(8,128)S(1)} %copy-done, s32[1024]{0:T(1024)S(1)} %pad_clamp_fusion), kind=kCustom, calls=%fused_computation.1 | custom fusion | bytes 2559232 | tf_op jit(solution)/shard_map/gather | solution.py:291
  33.7 1.0 %copy-done.3 = s32[768,128]{1,0:T(8,128)S(1)} copy-done((s32[768,128]{1,0:T(8,128)S(1)}, s32[768,128]{1,0:T(8,128)}, u32[]{:S(2)}) %copy-start.3) | copy-done | bytes 393240
  34.7 1.3 %shard_map.95 = (f32[800,384]{1,0:T(8,128)S(1)}, f32[40,384]{1,0:T(8,128)S(1)}) custom-call(s32[1,768]{1,0:T(1,128)S(1)} %get-tuple-element.22.row_ref, s32[768,128]{1,0:T(8,128)S(1)} %copy-done.3, s32[64,128]{1,0:T(8,128)S(1)} %broadcast_in_dim.6.neg_ref, bf16[768,384]{1,0:T(8,128)(2,1)S(1)} %bitcast.15, f32[832,384]{1,0:T(8,128)S(1)} %gather_fusion.1), custom_call_target="tpu_custom_call" | custom-call | flops 490733568 | bytes 3587072 | tf_op jit(solution)/shard_map/pallas_call | solution.py:21
  36.1 1.1 %copy-done.6 = f32[800,384]{1,0:T(8,128)} copy-done((f32[800,384]{1,0:T(8,128)}, f32[800,384]{1,0:T(8,128)S(1)}, u32[]{:S(2)}) %copy-start.6) | copy-done | bytes 1228824
  38.5 1.0 %copy-done.4 = s32[768,128]{1,0:T(8,128)S(1)} copy-done((s32[768,128]{1,0:T(8,128)S(1)}, s32[768,128]{1,0:T(8,128)}, u32[]{:S(2)}) %copy-start.4) | copy-done | bytes 393240
  39.5 1.3 %copy-done.7 = f32[800,384]{1,0:T(8,128)S(1)} copy-done((f32[800,384]{1,0:T(8,128)S(1)}, f32[800,384]{1,0:T(8,128)}, u32[]{:S(2)}) %copy-start.7) | copy-done | bytes 1228824
  40.7 1.6 %shard_map.96 = (bf16[768,384]{1,0:T(8,128)(2,1)}, bf16[32,768]{1,0:T(8,128)(2,1)}, f32[1,768]{1,0:T(1,128)S(1)}) custom-call(s32[1,768]{1,0:T(1,128)S(1)} %get-tuple-element.22.row_ref, s32[768,128]{1,0:T(8,128)S(1)} %copy-done.4, s32[64,128]{1,0:T(8,128)S(1)} %broadcast_in_dim.6.neg_ref, f32[32,128]{1,0:T(8,128)S(1)} %broadcast_in_dim.8.old_ref, ...), custom_call_target="tpu_custom_call" | custom-call | bytes 2439168 | tf_op jit(solution)/shard_map/pallas_call | solution.py:21
  42.3 5.9 %all-to-all-start.1 = ((bf16[16,48,384]{2,1,0:T(8,128)(2,1)}), bf16[16,48,384]{2,1,0:T(8,128)(2,1)S(1)}, u32[]{:S(2)}, u32[]{:S(2)}) async-start(bf16[16,48,384]{2,1,0:T(8,128)(2,1)} %bitcast.10), calls=%async_computation.1 | async-start | bytes 1179648 | tf_op jit(solution)/shard_map/all_to_all | solution.py:306
  48.3 2.0 %collective-permute-start.7 = (bf16[32,768]{1,0:T(8,128)(2,1)}, bf16[32,768]{1,0:T(8,128)(2,1)S(1)}, u32[]{:S(2)}, u32[]{:S(2)}) collective-permute-start(bf16[32,768]{1,0:T(8,128)(2,1)} %get-tuple-element.33), channel_id=1, source_target_pairs={{0,8},{2,10},{4,12},{6,14},{8,0},{10,2},{12,4},{14,6},{16,24},{18,... | collective-permute-start | bytes 147464 | tf_op jit(solution)/shard_map/ppermute | solution.py:236
  51.1 2.4 %collective-permute-start.8 = (bf16[32,768]{1,0:T(8,128)(2,1)}, bf16[32,768]{1,0:T(8,128)(2,1)S(1)}, u32[]{:S(2)}, u32[]{:S(2)}) collective-permute-start(bf16[32,768]{1,0:T(8,128)(2,1)} %get-tuple-element.33), channel_id=1, source_target_pairs={{0,16},{2,18},{4,20},{6,22},{8,24},{10,26},{12,28},{14,30},{16,0},... | collective-permute-start | bytes 147464 | tf_op jit(solution)/shard_map/ppermute | solution.py:236
  53.6 6.5 %collective-permute-done.7 = bf16[32,768]{1,0:T(8,128)(2,1)S(1)} collective-permute-done((bf16[32,768]{1,0:T(8,128)(2,1)}, bf16[32,768]{1,0:T(8,128)(2,1)S(1)}, u32[]{:S(2)}, u32[]{:S(2)}) %collective-permute-start.7) | collective-permute-done | bytes 49184 | tf_op jit(solution)/shard_map/ppermute | solution.py:236
  60.0 7.9 %collective-permute-done.8 = bf16[32,768]{1,0:T(8,128)(2,1)S(1)} collective-permute-done((bf16[32,768]{1,0:T(8,128)(2,1)}, bf16[32,768]{1,0:T(8,128)(2,1)S(1)}, u32[]{:S(2)}, u32[]{:S(2)}) %collective-permute-start.8) | collective-permute-done | bytes 49184 | tf_op jit(solution)/shard_map/ppermute | solution.py:236
  68.0 1.5 %collective-permute-start.10 = (bf16[128,768]{1,0:T(8,128)(2,1)S(1)}, bf16[128,768]{1,0:T(8,128)(2,1)S(1)}, u32[]{:S(2)}, u32[]{:S(2)}) collective-permute-start(bf16[128,768]{1,0:T(8,128)(2,1)S(1)} %constant_dynamic-update-slice_fusion.refs_0_), channel_id=1, source_target_pairs={{0,2},{2,0},{4,6},{6,4},{8,10},{10,8},{12,14},{14,12},{16,18},{18,... | collective-permute-start | bytes 589832 | tf_op jit(solution)/shard_map/ppermute | solution.py:236
  69.5 1.5 %collective-permute-start.11 = (bf16[128,768]{1,0:T(8,128)(2,1)S(1)}, bf16[128,768]{1,0:T(8,128)(2,1)S(1)}, u32[]{:S(2)}, u32[]{:S(2)}) collective-permute-start(bf16[128,768]{1,0:T(8,128)(2,1)S(1)} %constant_dynamic-update-slice_fusion.refs_0_), channel_id=1, source_target_pairs={{0,4},{2,6},{4,0},{6,2},{8,12},{10,14},{12,8},{14,10},{16,20},{18,... | collective-permute-start | bytes 589832 | tf_op jit(solution)/shard_map/ppermute | solution.py:236
  71.6 4.0 %collective-permute-done.10.refs_1_ = bf16[128,768]{1,0:T(8,128)(2,1)S(1)} collective-permute-done((bf16[128,768]{1,0:T(8,128)(2,1)S(1)}, bf16[128,768]{1,0:T(8,128)(2,1)S(1)}, u32[]{:S(2)}, u32[]{:S(2)}) %collective-permute-start.10) | collective-permute-done | bytes 196640 | tf_op jit(solution)/shard_map/ppermute | solution.py:236
  75.5 3.3 %collective-permute-done.11.refs_2_ = bf16[128,768]{1,0:T(8,128)(2,1)S(1)} collective-permute-done((bf16[128,768]{1,0:T(8,128)(2,1)S(1)}, bf16[128,768]{1,0:T(8,128)(2,1)S(1)}, u32[]{:S(2)}, u32[]{:S(2)}) %collective-permute-start.11) | collective-permute-done | bytes 196640 | tf_op jit(solution)/shard_map/ppermute | solution.py:236
  78.8 2.2 %shard_map.99 = (f32[256,384]{1,0:T(8,128)S(1)}, f32[8,256]{1,0:T(8,128)S(1)}, f32[264,384]{1,0:T(8,128)}) custom-call(bf16[256,384]{1,0:T(8,128)(2,1)S(1)} %copy-done.10, bf16[256,384]{1,0:T(8,128)(2,1)S(1)} %collective-permute-done.6.other_ref, bf16[128,768]{1,0:T(8,128)(2,1)S(1)} %constant_dynamic-update-slice_fusion.refs_0_, ...), custom_call_target="tpu_custom_call" | custom-call | flops 402653184 | bytes 1986560 | tf_op jit(solution)/shard_map/pallas_call | solution.py:21
  82.4 0.9 %copy-done.11 = bf16[256,384]{1,0:T(8,128)(2,1)S(1)} copy-done((bf16[256,384]{1,0:T(8,128)(2,1)S(1)}, bf16[256,384]{1,0:T(8,128)(2,1)}, u32[]{:S(2)}) %copy-start.11) | copy-done | bytes 196632
  86.5 3.0 %shard_map.97 = (f32[1024,384]{1,0:T(8,128)}, f32[1,1024]{1,0:T(1,128)}) custom-call(s32[1,768]{1,0:T(1,128)S(1)} %copy-done.13, s32[768,128]{1,0:T(8,128)S(1)} %copy-done.5, f32[1,768]{1,0:T(1,128)S(1)} %copy-done.19, bf16[768,384]{1,0:T(8,128)(2,1)S(1)} %bitcast.16, f32[1024,384]{1,0:T(8,128)S(1)} %copy-done, f32[1,1024]{1,0:T(1,128)S(1)} %bitcast.14), custom_call_target="tpu_custom_call" | custom-call | flops 603979776 | bytes 3145728 | tf_op jit(solution)/shard_map/pallas_call | solution.py:165
  89.6 1.1 %shard_map.100 = (f32[1,256]{1,0:T(1,128)}, f32[256,384]{1,0:T(8,128)}) custom-call(s32[1]{0:T(128)} %bitcast.9.self_ref, f32[8,256]{1,0:T(8,128)S(1)} %get-tuple-element.32.part_ref, f32[8,256]{1,0:T(8,128)S(1)} %collective-permute-done.5.far_ref, f32[8,256]{1,0:T(8,128)S(1)} %copy-done.17, f32[256,384]{1,0:T(8,128)S(1)} %copy-done.9, ...), custom_call_target="tpu_custom_call" | custom-call | bytes 1414148 | tf_op jit(solution)/shard_map/pallas_call | solution.py:21
  (72 shorter events, 10.6 us)
Async XLA Ops:
  0.6 30.1 %copy-start = (f32[1024,384]{1,0:T(8,128)S(1)}, f32[1024,384]{1,0:T(8,128)}, u32[]{:S(2)}) copy-start(f32[1024,384]{1,0:T(8,128)} %bank_ref.1) | copy-start | bytes 4718596
  0.6 0.8 copy-start.14
  1.4 0.9 %copy-start.22 = (bf16[256,384]{1,0:T(8,128)(2,1)S(1)}, bf16[256,384]{1,0:T(8,128)(2,1)}, u32[]{:S(2)}) copy-start(bf16[256,384]{1,0:T(8,128)(2,1)} %feat_ref.1) | copy-start | bytes 589828
  2.4 10.2 %copy-start.15 = (s32[256]{0:T(256)S(1)}, s32[256]{0:T(256)}, u32[]{:S(2)}) copy-start(s32[256]{0:T(256)} %param.7) | copy-start | bytes 3076
  4.3 29.4 %all-to-all-start = ((bf16[16,48,384]{2,1,0:T(8,128)(2,1)}), bf16[16,48,384]{2,1,0:T(8,128)(2,1)S(1)}, u32[]{:S(2)}, u32[]{:S(2)}) async-start(bf16[16,48,384]{2,1,0:T(8,128)(2,1)} %bitcast.2), calls=%async_computation | async-start | bytes 1179648 | tf_op jit(solution)/shard_map/all_to_all | solution.py:278
  12.6 4.7 %collective-permute-start = (s32[1,256]{1,0:T(1,128)S(1)}, s32[1,256]{1,0:T(1,128)S(1)}, u32[]{:S(2)}, u32[]{:S(2)}) collective-permute-start(s32[1,256]{1,0:T(1,128)S(1)} %bitcast.19), channel_id=1, source_target_pairs={{0,2},{2,0},{4,6},{6,4},{8,10},{10,8},{12,14},{14,12},{16,18},{18,... | collective-permute-start | bytes 3080 | tf_op jit(solution)/shard_map/ppermute | solution.py:236
  17.3 3.6 %collective-permute-start.1 = (s32[2,256]{1,0:T(2,128)S(1)}, s32[2,256]{1,0:T(2,128)S(1)}, u32[]{:S(2)}, u32[]{:S(2)}) collective-permute-start(s32[2,256]{1,0:T(2,128)S(1)} %pad_add_fusion.2), channel_id=1, source_target_pairs={{0,4},{2,6},{4,0},{6,2},{8,12},{10,14},{12,8},{14,10},{16,20},{18,... | collective-permute-start | bytes 6152 | tf_op jit(solution)/shard_map/ppermute | solution.py:236
  20.9 3.7 %collective-permute-start.2 = (s32[4,256]{1,0:T(4,128)S(1)}, s32[4,256]{1,0:T(4,128)S(1)}, u32[]{:S(2)}, u32[]{:S(2)}) collective-permute-start(s32[4,256]{1,0:T(4,128)S(1)} %pad_add_fusion.1), channel_id=1, source_target_pairs={{0,8},{2,10},{4,12},{6,14},{8,0},{10,2},{12,4},{14,6},{16,24},{18,... | collective-permute-start | bytes 12296 | tf_op jit(solution)/shard_map/ppermute | solution.py:236
  24.6 4.6 %collective-permute-start.3 = (s32[8,256]{1,0:T(8,128)S(1)}, s32[8,256]{1,0:T(8,128)S(1)}, u32[]{:S(2)}, u32[]{:S(2)}) collective-permute-start(s32[8,256]{1,0:T(8,128)S(1)} %pad_add_fusion), channel_id=1, source_target_pairs={{0,16},{2,18},{4,20},{6,22},{8,24},{10,26},{12,28},{14,30},{16,0},... | collective-permute-start | bytes 24584 | tf_op jit(solution)/shard_map/ppermute | solution.py:236
  30.6 7.8 %copy-start.12 = (s32[1,768]{1,0:T(1,128)}, s32[1,768]{1,0:T(1,128)S(1)}, u32[]{:S(2)}) copy-start(s32[1,768]{1,0:T(1,128)S(1)} %get-tuple-element.22.row_ref) | copy-start | bytes 9220
  33.6 3.5 %copy-start.1 = (f32[1024]{0:T(1024)S(1)}, f32[1024]{0:T(1024)}, u32[]{:S(2)}) copy-start(f32[1024]{0:T(1024)} %param.10) | copy-start | bytes 12292
  33.7 1.0 %copy-start.3 = (s32[768,128]{1,0:T(8,128)S(1)}, s32[768,128]{1,0:T(8,128)}, u32[]{:S(2)}) copy-start(s32[768,128]{1,0:T(8,128)} %copy-done.2) | copy-start | bytes 1179652
  36.1 1.1 %copy-start.6 = (f32[800,384]{1,0:T(8,128)}, f32[800,384]{1,0:T(8,128)S(1)}, u32[]{:S(2)}) copy-start(f32[800,384]{1,0:T(8,128)S(1)} %get-tuple-element.25.new_ref) | copy-start | bytes 3686404
  37.1 1.2 %collective-permute-start.4 = (f32[40,384]{1,0:T(8,128)S(1)}, f32[40,384]{1,0:T(8,128)S(1)}, u32[]{:S(2)}, u32[]{:S(2)}) collective-permute-start(f32[40,384]{1,0:T(8,128)S(1)} %get-tuple-element.26.pack_ref), channel_id=1, source_target_pairs={{0,1},{1,0},{2,3},{3,2},{4,5},{5,4},{6,7},{7,6},{8,9},{9,8},{10,11... | collective-permute-start | bytes 184328 | tf_op jit(solution)/shard_map/ppermute | solution.py:232
  38.5 1.0 %copy-start.4 = (s32[768,128]{1,0:T(8,128)S(1)}, s32[768,128]{1,0:T(8,128)}, u32[]{:S(2)}) copy-start(s32[768,128]{1,0:T(8,128)} %copy-done.2) | copy-start | bytes 1179652
  39.5 1.3 %copy-start.7 = (f32[800,384]{1,0:T(8,128)S(1)}, f32[800,384]{1,0:T(8,128)}, u32[]{:S(2)}) copy-start(f32[800,384]{1,0:T(8,128)} %copy-done.6) | copy-start | bytes 3686404
  40.7 7.4 %copy-start.10 = (bf16[256,384]{1,0:T(8,128)(2,1)S(1)}, bf16[256,384]{1,0:T(8,128)(2,1)}, u32[]{:S(2)}) copy-start(bf16[256,384]{1,0:T(8,128)(2,1)} %mine_ref.1) | copy-start | bytes 589828
  42.3 38.7 %copy-start.18 = (f32[1,768]{1,0:T(1,128)}, f32[1,768]{1,0:T(1,128)S(1)}, u32[]{:S(2)}) copy-start(f32[1,768]{1,0:T(1,128)S(1)} %get-tuple-element.27.dist_ref) | copy-start | bytes 9220
  42.3 40.1 %all-to-all-start.1 = ((bf16[16,48,384]{2,1,0:T(8,128)(2,1)}), bf16[16,48,384]{2,1,0:T(8,128)(2,1)S(1)}, u32[]{:S(2)}, u32[]{:S(2)}) async-start(bf16[16,48,384]{2,1,0:T(8,128)(2,1)} %bitcast.10), calls=%async_computation.1 | async-start | bytes 1179648 | tf_op jit(solution)/shard_map/all_to_all | solution.py:306
  48.2 23.4 %collective-permute-start.6 = (bf16[256,384]{1,0:T(8,128)(2,1)S(1)}, bf16[256,384]{1,0:T(8,128)(2,1)S(1)}, u32[]{:S(2)}, u32[]{:S(2)}) collective-permute-start(bf16[256,384]{1,0:T(8,128)(2,1)S(1)} %copy-done.10), channel_id=1, source_target_pairs={{0,1},{1,0},{2,3},{3,2},{4,5},{5,4},{6,7},{7,6},{8,9},{9,8},{10,11... | collective-permute-start | bytes 589832 | tf_op jit(solution)/shard_map/ppermute | solution.py:232
  48.3 11.8 %collective-permute-start.7 = (bf16[32,768]{1,0:T(8,128)(2,1)}, bf16[32,768]{1,0:T(8,128)(2,1)S(1)}, u32[]{:S(2)}, u32[]{:S(2)}) collective-permute-start(bf16[32,768]{1,0:T(8,128)(2,1)} %get-tuple-element.33), channel_id=1, source_target_pairs={{0,8},{2,10},{4,12},{6,14},{8,0},{10,2},{12,4},{14,6},{16,24},{18,... | collective-permute-start | bytes 147464 | tf_op jit(solution)/shard_map/ppermute | solution.py:236
  51.1 34.1 %copy-start.5 = (s32[768,128]{1,0:T(8,128)S(1)}, s32[768,128]{1,0:T(8,128)}, u32[]{:S(2)}) copy-start(s32[768,128]{1,0:T(8,128)} %copy-done.2) | copy-start | bytes 1179652
  51.1 16.9 %collective-permute-start.8 = (bf16[32,768]{1,0:T(8,128)(2,1)}, bf16[32,768]{1,0:T(8,128)(2,1)S(1)}, u32[]{:S(2)}, u32[]{:S(2)}) collective-permute-start(bf16[32,768]{1,0:T(8,128)(2,1)} %get-tuple-element.33), channel_id=1, source_target_pairs={{0,16},{2,18},{4,20},{6,22},{8,24},{10,26},{12,28},{14,30},{16,0},... | collective-permute-start | bytes 147464 | tf_op jit(solution)/shard_map/ppermute | solution.py:236
  53.5 14.5 %collective-permute-start.9 = (bf16[32,768]{1,0:T(8,128)(2,1)}, bf16[32,768]{1,0:T(8,128)(2,1)S(1)}, u32[]{:S(2)}, u32[]{:S(2)}) collective-permute-start(bf16[32,768]{1,0:T(8,128)(2,1)} %get-tuple-element.33), channel_id=1, source_target_pairs={{0,24},{2,26},{4,28},{6,30},{8,16},{10,18},{12,20},{14,22},{16,8},... | collective-permute-start | bytes 147464 | tf_op jit(solution)/shard_map/ppermute | solution.py:236
  68.0 7.5 %collective-permute-start.10 = (bf16[128,768]{1,0:T(8,128)(2,1)S(1)}, bf16[128,768]{1,0:T(8,128)(2,1)S(1)}, u32[]{:S(2)}, u32[]{:S(2)}) collective-permute-start(bf16[128,768]{1,0:T(8,128)(2,1)S(1)} %constant_dynamic-update-slice_fusion.refs_0_), channel_id=1, source_target_pairs={{0,2},{2,0},{4,6},{6,4},{8,10},{10,8},{12,14},{14,12},{16,18},{18,... | collective-permute-start | bytes 589832 | tf_op jit(solution)/shard_map/ppermute | solution.py:236
  69.5 9.3 %collective-permute-start.11 = (bf16[128,768]{1,0:T(8,128)(2,1)S(1)}, bf16[128,768]{1,0:T(8,128)(2,1)S(1)}, u32[]{:S(2)}, u32[]{:S(2)}) collective-permute-start(bf16[128,768]{1,0:T(8,128)(2,1)S(1)} %constant_dynamic-update-slice_fusion.refs_0_), channel_id=1, source_target_pairs={{0,4},{2,6},{4,0},{6,2},{8,12},{10,14},{12,8},{14,10},{16,20},{18,... | collective-permute-start | bytes 589832 | tf_op jit(solution)/shard_map/ppermute | solution.py:236
  71.0 7.8 %collective-permute-start.12 = (bf16[128,768]{1,0:T(8,128)(2,1)S(1)}, bf16[128,768]{1,0:T(8,128)(2,1)S(1)}, u32[]{:S(2)}, u32[]{:S(2)}) collective-permute-start(bf16[128,768]{1,0:T(8,128)(2,1)S(1)} %constant_dynamic-update-slice_fusion.refs_0_), channel_id=1, source_target_pairs={{0,6},{2,4},{4,2},{6,0},{8,14},{10,12},{12,10},{14,8},{16,22},{18,... | collective-permute-start | bytes 589832 | tf_op jit(solution)/shard_map/ppermute | solution.py:236
  82.4 7.2 %collective-permute-start.13 = (f32[264,384]{1,0:T(8,128)}, f32[264,384]{1,0:T(8,128)S(1)}, u32[]{:S(2)}, u32[]{:S(2)}) collective-permute-start(f32[264,384]{1,0:T(8,128)} %get-tuple-element.36), channel_id=1, source_target_pairs={{0,1},{1,0},{2,3},{3,2},{4,5},{5,4},{6,7},{7,6},{8,9},{9,8},{10,11... | collective-permute-start | bytes 1216520 | tf_op jit(solution)/shard_map/ppermute | solution.py:232
  82.4 0.9 %copy-start.11 = (bf16[256,384]{1,0:T(8,128)(2,1)S(1)}, bf16[256,384]{1,0:T(8,128)(2,1)}, u32[]{:S(2)}) copy-start(bf16[256,384]{1,0:T(8,128)(2,1)} %mine_ref.1) | copy-start | bytes 589828
  84.6 4.9 %collective-permute-start.5 = (f32[8,256]{1,0:T(8,128)S(1)}, f32[8,256]{1,0:T(8,128)S(1)}, u32[]{:S(2)}, u32[]{:S(2)}) collective-permute-start(f32[8,256]{1,0:T(8,128)S(1)} %get-tuple-element.32.part_ref), channel_id=1, source_target_pairs={{0,1},{1,0},{2,3},{3,2},{4,5},{5,4},{6,7},{7,6},{8,9},{9,8},{10,11... | collective-permute-start | bytes 24584 | tf_op jit(solution)/shard_map/ppermute | solution.py:232
  86.5 3.0 %copy-start.9 = (f32[256,384]{1,0:T(8,128)S(1)}, f32[256,384]{1,0:T(8,128)}, u32[]{:S(2)}) copy-start(f32[256,384]{1,0:T(8,128)} %copy-done.8) | copy-start | bytes 1179652
  86.5 3.1 %copy-start.17 = (f32[8,256]{1,0:T(8,128)S(1)}, f32[8,256]{1,0:T(8,128)}, u32[]{:S(2)}) copy-start(f32[8,256]{1,0:T(8,128)} %copy-done.16) | copy-start | bytes 24580
  (7 other events, 4.7 us)

commit v2 on v1

v2 whole, which is shorter than its diff:
```python
import functools

import jax
import jax.numpy as jnp
from jax import lax
from jax.experimental import pallas as pl
from jax.experimental.pallas import tpu as pltpu
from jax.sharding import PartitionSpec as P

F32 = jnp.float32
BF16 = jnp.bfloat16
I32 = jnp.int32
LANES = 128
VMEM = 24 * 2**20


def call(kernel, outs, *args, flops=0, smem=(), hbm=(), out_hbm=(), free=(), out_free=(), scratch=()):
    moved = sum(a.size * a.dtype.itemsize for a in args) + sum(o.size * o.dtype.itemsize for o in outs)
    spaces = [pltpu.SMEM if k in smem else pltpu.HBM if k in hbm else pltpu.VMEM for k in range(len(args))]
    out_spaces = [pltpu.HBM if k in out_hbm else pltpu.VMEM for k in range(len(outs))]
    return pl.pallas_call(
        kernel,
        out_shape=[o if k in out_free else space(o.shape, o.dtype) for k, (o, space) in enumerate(zip(outs, out_spaces))],
        in_specs=[pl.BlockSpec(memory_space=space) for space in spaces],
        out_specs=[pl.BlockSpec(memory_space=space) for space in out_spaces],
        scratch_shapes=list(scratch),
        compiler_params=pltpu.CompilerParams(vmem_limit_bytes=VMEM),
        cost_estimate=pl.CostEstimate(flops=flops, bytes_accessed=moved, transcendentals=0),
    )(*[placed(a, space, k in free) for k, (a, space) in enumerate(zip(args, spaces))])


def placed(value, space, free=False):
    return value if free or space is pltpu.SMEM else pltpu.with_memory_space_constraint(value, space)


def shape(dims, dtype):
    return jax.ShapeDtypeStruct(dims, dtype)


def nt(a, b):
    return lax.dot_general(a, b, (((1,), (1,)), ((), ())), preferred_element_type=F32)


def nn(a, b):
    return jnp.dot(a, b, preferred_element_type=F32)


def iota(dims, axis):
    return lax.broadcasted_iota(I32, dims, axis)


def onehot(mask):
    return jnp.where(mask, 1.0, 0.0).astype(BF16)


def to_col(row):
    return jnp.transpose(jnp.broadcast_to(row, (LANES, row.shape[1])))


def to_row(col):
    return jnp.transpose(jnp.broadcast_to(col, (col.shape[0], LANES)))[0:1, :]


def id_col(ids):
    return to_col(ids.astype(F32))[:, 0:1].astype(I32)


def ranks_of(label, owners, owned):
    rows = label.shape[1]
    start = iota((owners, rows), 0) * owned
    mine = (label >= start) & (label < start + owned)
    before = onehot(iota((rows, rows), 0) <= iota((rows, rows), 1))
    running = nn(onehot(mine), before)
    return mine, jnp.sum(jnp.where(mine, running, 0.0), axis=0, keepdims=True) - 1.0


def slot_of(mine, rank, stride):
    owner = jnp.sum(jnp.where(mine, iota(mine.shape, 0).astype(F32), 0.0), axis=0, keepdims=True)
    return (owner * stride + rank).astype(I32)


def pack_kernel(owners, owned, capacity, label_ref, feat_ref, send_ref, label_buf, feat_buf, send_buf, sems):
    slots, width = send_buf.shape
    rows = label_buf.shape[1]
    stride = slots // owners
    labels = pltpu.make_async_copy(label_ref, label_buf, sems.at[0])
    feats = pltpu.make_async_copy(feat_ref, feat_buf, sems.at[1])
    labels.start()
    feats.start()
    labels.wait()
    label = label_buf[...]
    mine, rank = ranks_of(label, owners, owned)
    slot = slot_of(mine, rank, stride)
    value = jnp.where(mine, (label - iota((owners, rows), 0) * owned + 1).astype(F32), 0.0)
    high = jnp.floor(value * (1.0 / 32.0))
    low = value - 32.0 * high
    place = onehot(to_col(rank)[:, 0:1] == iota((rows, LANES), 1).astype(F32))
    ids = jnp.concatenate(
        [nn(high.astype(BF16), place), nn(low.astype(BF16), place), jnp.zeros((owners, width - 2 * LANES), F32)], axis=1
    ).astype(BF16)
    feats.wait()
    half = slots // 2
    copies = []
    for k in range(2):
        at = slice(k * half, (k + 1) * half)
        spot = iota((half, rows), 0) + k * half
        last = iota((half, owners), 0) + k * half == iota((half, owners), 1) * stride + capacity
        send_buf[at, :] = (nn(onehot(spot == slot), feat_buf[...]) + nn(onehot(last), ids)).astype(BF16)
        copies.append(pltpu.make_async_copy(send_buf.at[at, :], send_ref.at[at, :], sems.at[2 + k]))
        copies[k].start()
    for c in copies:
        c.wait()


def split_kernel(self_ref, neg_ref, old_ref, bank_ref, neg_col_ref, old_col_ref, held_ref, parts_ref, bank_buf, sem):
    owned, width = bank_buf.shape
    negs = neg_ref.shape[1]
    load = pltpu.make_async_copy(bank_ref, bank_buf, sem)
    load.start()
    me = self_ref[0]
    wanted = neg_ref[pl.ds(me, 1), :] - me * owned
    wanted = jnp.concatenate([wanted] * (LANES // negs), axis=1)
    neg_col = id_col(wanted)[0:negs, :]
    neg_col_ref[...] = jnp.broadcast_to(neg_col, neg_col_ref.shape)
    same = neg_col == iota((negs, owned), 1)
    old = jnp.sum(jnp.where(same, old_ref[...], 0.0), axis=1, keepdims=True)
    old_col_ref[...] = jnp.broadcast_to(old, old_col_ref.shape)
    pick = onehot(same)
    load.wait()
    bank = bank_buf[...]
    high = bank.astype(BF16)
    rest = bank - high.astype(F32)
    middle = rest.astype(BF16)
    low = (rest - middle.astype(F32)).astype(BF16)
    parts_ref[:, 0:width] = high
    parts_ref[:, width : 2 * width] = middle
    if parts_ref.shape[1] > 2 * width:
        parts_ref[:, 2 * width :] = low
    held_ref[...] = nn(pick, high) + nn(pick, middle) + nn(pick, low)


def blend(bank, sums, counts):
    safe = jnp.maximum(counts, 1.0)
    return jnp.where(counts > 0, 0.5 * bank + 0.5 * sums / safe, bank)


def mean_kernel(owners, capacity, after_ref, neg_ref, held_ref, parts_ref, got_ref, ids_ref, new_ref, pack_ref, rows_ref):
    owned = parts_ref.shape[0]
    negs, width = held_ref.shape
    sent_rows = got_ref.shape[0]
    stride = sent_rows // owners
    slots = rows_ref.shape[0]
    keep = slots // owners
    last = iota((owners, sent_rows), 1) == iota((owners, sent_rows), 0) * stride + capacity
    sent = nn(onehot(last), got_ref[:, 0 : 2 * LANES]).astype(BF16)
    place = iota((LANES, slots), 1).astype(F32)
    within = place - keep * jnp.floor((place + 0.5) * (1.0 / keep))
    spread = onehot(within == iota((LANES, slots), 0).astype(F32))
    wide = 32.0 * nn(sent[:, 0:LANES], spread) + nn(sent[:, LANES:], spread)
    first = iota((owners, slots), 0) * keep
    spot = iota((owners, slots), 1)
    ids = jnp.sum(jnp.where((spot >= first) & (spot < first + keep), wide, 0.0), axis=0, keepdims=True)
    ids = jnp.where(ids > 0.5, ids - 1.0, float(owned)).astype(I32)
    ids_ref[...] = ids
    for b in range(owners if keep < stride else 0):
        rows_ref[b * keep : (b + 1) * keep, :] = got_ref[b * stride : b * stride + keep, :]
    if keep == stride:
        rows_ref[...] = got_ref[...]
    got = rows_ref[...]
    col = id_col(ids)
    parts = 3
    block = slots // parts if slots % (16 * parts) == 0 else slots
    squares = []
    for k in range(slots // block):
        at = slice(k * block, (k + 1) * block)
        picked = nn(onehot(iota((block, owned), 1) == col[at]), parts_ref[...])
        bank = functools.reduce(jnp.add, [picked[:, j : j + width] for j in range(0, picked.shape[1], width)])
        same = jnp.where(col[at] == ids, 1.0, 0.0)
        new = blend(bank, nn(same.astype(BF16), got), jnp.sum(same, axis=1, keepdims=True))
        new_ref[at, :] = new
        differ = got[at].astype(F32) - new
        squares.append(jnp.sum(differ * differ, axis=1, keepdims=True))
    squared = to_row(jnp.concatenate(squares, axis=0))
    same = jnp.where(neg_ref[:, 0:1] == ids, 1.0, 0.0)
    pack_ref[0:negs, :] = blend(held_ref[...], nn(same.astype(BF16), got), jnp.sum(same, axis=1, keepdims=True))
    for k in range(-(-slots // width)):
        piece = squared[:, k * width : min((k + 1) * width, slots)]
        pack_ref[negs + k : negs + k + 1, 0 : piece.shape[1]] = piece


def concentration(same, dist, old):
    counts = jnp.sum(jnp.where(same, 1.0, 0.0), axis=1, keepdims=True)
    total = jnp.sum(jnp.where(same, dist, 0.0), axis=1, keepdims=True)
    safe = jnp.maximum(counts, 1.0)
    return jnp.where(counts > 0, total / (safe * jnp.log(safe + 10.0)), old)


def neg_kernel(self_ref, ids_ref, neg_ref, old_ref, pack_ref, other_ref, full_ref, own_ref, dist_ref):
    slots, width = ids_ref.shape[1], pack_ref.shape[1]
    negs = neg_ref.shape[0]
    half = negs // 2
    pieces = []
    for k in range(-(-slots // width)):
        part = pack_ref[negs + k : negs + k + 1, :] + other_ref[negs + k : negs + k + 1, :]
        pieces.append(part[:, 0 : min(width, slots - k * width)])
    dist = jnp.sqrt(jnp.concatenate(pieces, axis=1) + 0.25)
    dist_ref[...] = dist
    conc = concentration(neg_ref[:, 0:1] == ids_ref[...], dist, old_ref[:, 0:1])
    mine = (pack_ref[0:negs, :] / conc).astype(BF16)
    other = (other_ref[0:negs, :] / conc).astype(BF16)
    full_ref[:, 0:width] = mine
    full_ref[:, width:] = other
    first = self_ref[1] == 0
    own_ref[:, 0:width] = jnp.where(first, mine[0:half], mine[half:])
    own_ref[:, width:] = jnp.where(first, other[0:half], other[half:])


def scale_kernel(capacity, ids_ref, new_ref, dist_ref, out_ref, buf, sems):
    owners = buf.shape[0]
    stride = new_ref.shape[0] // owners
    ids, dist = ids_ref[...], dist_ref[...]
    col = id_col(ids)
    copies = []
    half = owners // 2
    for k in range(2):
        at = slice(k * half * stride, (k + 1) * half * stride)
        scaled = new_ref[at, :] / concentration(col[at] == ids, dist, 1.0)
        for b in range(half):
            buf[k * half + b] = scaled[b * stride : b * stride + capacity].astype(BF16)
        copies.append(
            pltpu.make_async_copy(buf.at[pl.ds(k * half, half)], out_ref.at[pl.ds(k * half, half)], sems.at[k])
        )
        copies[k].start()
    for c in copies:
        c.wait()


def join_kernel(*refs):
    pieces, joined = refs[1:-2], refs[-2]
    at = 0
    for p in pieces:
        joined[at : at + p.shape[0], :] = p[...]
        at += p.shape[0]


def owner_kernel(ids_ref, dist_ref, got_ref, bank_ref, old_ref, new_ref, conc_ref):
    block = bank_ref.shape[0]
    slots = got_ref.shape[0]
    base = pl.program_id(0) * block
    same = jnp.where(iota((block, slots), 0) + base == ids_ref[...], 1.0, 0.0)
    sums = nn(same.astype(BF16), got_ref[...])
    new_ref[...] = blend(bank_ref[...], sums, jnp.sum(same, axis=1, keepdims=True))
    turned = iota((slots, block), 1) + base == id_col(ids_ref[...])
    counts = jnp.sum(jnp.where(turned, 1.0, 0.0), axis=0, keepdims=True)
    total = jnp.sum(jnp.where(turned, to_col(dist_ref[...])[:, 0:1], 0.0), axis=0, keepdims=True)
    safe = jnp.maximum(counts, 1.0)
    conc_ref[...] = jnp.where(counts > 0, total / (safe * jnp.log(safe + 10.0)), old_ref[...])


def owner_call(ids, dist, got, bank, old):
    owned, width = bank.shape
    slots = got.shape[0]
    block = 256
    whole = lambda k: (0, 0)
    return pl.pallas_call(
        owner_kernel,
        grid=(owned // block,),
        in_specs=[
            pl.BlockSpec((1, slots), whole),
            pl.BlockSpec((1, slots), whole),
            pl.BlockSpec((slots, width), whole),
            pl.BlockSpec((block, width), lambda k: (k, 0)),
            pl.BlockSpec((1, block), lambda k: (0, k)),
        ],
        out_specs=[pl.BlockSpec((block, width), lambda k: (k, 0)), pl.BlockSpec((1, block), lambda k: (0, k))],
        out_shape=[shape((owned, width), F32), shape((1, owned), F32)],
        compiler_params=pltpu.CompilerParams(vmem_limit_bytes=VMEM),
        cost_estimate=pl.CostEstimate(flops=10**12, bytes_accessed=8 * owned * width, transcendentals=0),
    )(ids, dist, got, placed(bank, pltpu.HBM), placed(old, pltpu.HBM))


def flash_kernel(owners, owned, capacity, after_ref, label_ref, mine_ref, other_ref, *refs):
    parts, (keep_ref, stats_ref, send_ref, slot_ref, copy_ref) = refs[:-5], refs[-5:]
    width = mine_ref.shape[1]
    slot = slot_of(*ranks_of(label_ref[...], owners, owned), capacity)
    slot_ref[...] = to_col(slot.astype(F32)).astype(I32)
    copy_ref[...] = mine_ref[...]
    rows = mine_ref.shape[0]
    mine, other = mine_ref[...], other_ref[...]
    logits = [nt(mine, p[:, 0:width]) + nt(other, p[:, width:]) for p in parts]
    top = functools.reduce(jnp.maximum, [jnp.max(l, axis=1, keepdims=True) for l in logits])
    total = jnp.zeros((rows, 1), F32)
    grad = jnp.zeros((rows, 2 * width), F32)
    for l, p in zip(logits, parts):
        weight = jnp.exp(l - top)
        total = total + jnp.sum(weight, axis=1, keepdims=True)
        grad = grad + nn(weight.astype(BF16), p[...])
    keep_ref[...] = grad[:, 0:width]
    send_ref[0:rows, :] = grad[:, width:]
    stats = jnp.concatenate([to_row(top), to_row(total)], axis=0)
    stats_ref[0:2, :] = stats
    send_ref[rows : rows + 2, 0:rows] = stats


def positive_kernel(slot_ref, query_ref, back_ref, rows_ref, part_ref):
    rows, slots = query_ref.shape[0], back_ref.shape[0]
    found = nn(onehot(iota((rows, slots), 1) == slot_ref[:, 0:1]), back_ref[...])
    rows_ref[...] = found.astype(BF16)
    part = to_row(jnp.sum(query_ref[...].astype(F32) * found, axis=1, keepdims=True))
    part_ref[...] = jnp.broadcast_to(part, part_ref.shape)


def final_kernel(self_ref, part_ref, far_ref, stats_ref, keep_ref, sent_ref, rows_ref, loss_ref, grad_ref):
    rows = keep_ref.shape[0]
    first = self_ref[1] == 0
    here, there = stats_ref[0:2, :], sent_ref[rows : rows + 2, 0:rows]
    low = jnp.where(first, here, there)
    high = jnp.where(first, there, here)
    positive = part_ref[0:1, :] + far_ref[0:1, :]
    top = jnp.maximum(jnp.maximum(low[0:1], high[0:1]), positive)
    exppos = jnp.exp(positive - top)
    total = low[1:2] * jnp.exp(low[0:1] - top) + high[1:2] * jnp.exp(high[0:1] - top) + exppos
    loss_ref[...] = jnp.log(total) + top - positive
    mine = to_col(jnp.exp(here[0:1] - top) / total)[:, 0:1]
    other = to_col(jnp.exp(there[0:1] - top) / total)[:, 0:1]
    pull = to_col(exppos / total - 1.0)[:, 0:1]
    grad_ref[...] = keep_ref[...] * mine + sent_ref[0:rows, :] * other + pull * rows_ref[...].astype(F32)


def swap(value):
    return lax.ppermute(value, "mp", [(0, 1), (1, 0)])


def hop(value, count, bits):
    return lax.ppermute(value, "dp", [(k, k ^ bits) for k in range(count)])


def two_hop(value, count, bits):
    return lax.ppermute(
        value, ("dp", "mp"), [(2 * k + c, 2 * (k ^ bits[c]) + c) for k in range(count) for c in range(2)]
    )


def join(value, pieces):
    rows = sum(p.shape[0] for p in pieces)
    return pl.pallas_call(
        join_kernel,
        out_shape=[pltpu.VMEM((rows, pieces[0].shape[1]), BF16), pltpu.HBM(value.shape, value.dtype)],
        in_specs=[pl.BlockSpec(memory_space=pltpu.HBM)] + [pl.BlockSpec(memory_space=pltpu.VMEM) for _ in pieces],
        out_specs=[pl.BlockSpec(memory_space=pltpu.VMEM), pl.BlockSpec(memory_space=pltpu.HBM)],
        input_output_aliases={0: 1},
        compiler_params=pltpu.CompilerParams(vmem_limit_bytes=VMEM),
    )(placed(value, pltpu.HBM), *[placed(p, pltpu.VMEM) for p in pieces])


def body(features, labels, queries, bank, old_conc, neg_index):
    count = lax.axis_size("dp")
    me, core = lax.axis_index("dp"), lax.axis_index("mp")
    owned, width = bank.shape
    rows = features.shape[0]
    capacity = 3 * rows // count
    stride = 8 * -(-(capacity + 1) // 8)
    slots = count * stride
    negs = neg_index.shape[0] // count
    half = negs // 2
    place = jnp.stack([me, core]).astype(I32)
    loads = [pltpu.VMEM((1, rows), I32), pltpu.VMEM((rows, width), BF16)]

    label_row = labels.reshape(1, rows)
    (send,) = call(
        functools.partial(pack_kernel, count, owned, capacity),
        (shape((slots, width), BF16),),
        label_row, features, flops=2 * slots * rows * width, hbm=(0, 1), out_hbm=(0,),
        scratch=[*loads, pltpu.VMEM((slots, width), BF16), pltpu.SemaphoreType.DMA((4,))],
    )
    query_far = swap(queries)
    got = lax.all_to_all(send.reshape(count, stride, width), "dp", split_axis=0, concat_axis=0)
    got = got.reshape(slots, width)

    neg_col, old_col, held, parts = call(
        split_kernel,
        (shape((negs, LANES), I32), shape((negs, LANES), F32), shape((negs, width), F32), shape((owned, 2 * width), BF16)),
        place, neg_index.reshape(count, negs), old_conc.reshape(1, owned), bank, smem=(0,), hbm=(3,), free=(1, 2),
        scratch=[pltpu.VMEM((owned, width), F32), pltpu.SemaphoreType.DMA],
    )
    sent_rows = slots
    slots = count * capacity if capacity % 16 == 0 else slots
    extra = 8 * -(-slots // (8 * width))
    ids, new, pack, got = call(
        functools.partial(mean_kernel, count, capacity),
        (shape((1, slots), I32), shape((slots, width), F32), shape((negs + extra, width), F32), shape((slots, width), BF16)),
        query_far, neg_col, held, parts, got, flops=8 * slots * owned * width, hbm=(0,),
    )
    full, own, dist = call(
        neg_kernel,
        (shape((negs, 2 * width), BF16), shape((half, 2 * width), BF16), shape((1, slots), F32)),
        place, ids, neg_col, old_col, pack, swap(pack), smem=(0,),
    )
    (scaled,) = call(
        functools.partial(scale_kernel, capacity),
        (shape((count, capacity, width), BF16),),
        ids, new, dist, out_hbm=(0,),
        scratch=[pltpu.VMEM((count, capacity, width), BF16), pltpu.SemaphoreType.DMA((2,))],
    )
    step = count // 4
    line = [own, two_hop(full, count, (step, 2 * step)), hop(own, count, 3 * step)]
    joined, scaled = join(scaled, line)
    pieces = [joined]
    while step > 1:
        few = min(4, step)
        step //= few
        pieces = [joined] + [hop(joined, count, step * k) for k in range(1, few)]
        if step > 1:
            joined = jnp.concatenate(pieces, axis=0)
    back = lax.all_to_all(scaled, "dp", split_axis=0, concat_axis=0)
    new_bank, new_conc = owner_call(ids, dist, got, bank, old_conc.reshape(1, owned))
    keep, stats, sent, slot, query = call(
        functools.partial(flash_kernel, count, owned, capacity),
        (
            shape((rows, width), F32), shape((8, rows), F32), shape((rows + 8, width), F32),
            shape((rows, LANES), I32), shape((rows, width), BF16),
        ),
        new_conc, label_row, queries, query_far, *pieces,
        flops=8 * rows * half * count * width, hbm=(0,), free=range(1, 99),
    )
    sent = swap(sent)
    found, part = call(
        positive_kernel,
        (shape((rows, width), BF16), shape((8, rows), F32)),
        slot, query, back.reshape(count * capacity, width), flops=2 * slots * rows * width,
    )
    loss, grad = call(
        final_kernel,
        (shape((1, rows), F32), shape((rows, width), F32)),
        place, part, swap(part), stats, keep, sent, found, smem=(0,), out_free=(0, 1),
    )
    return (new_bank, new_conc.reshape(owned), loss.reshape(rows), grad)


def solution(mesh):
    placed = (P("dp", "mp"), P("dp"), P("dp", "mp"), P("dp", "mp"), P("dp"), P())
    return jax.shard_map(
        body,
        mesh=mesh,
        in_specs=placed,
        out_specs=(P("dp", "mp"), P("dp"), P("dp"), P("dp", "mp")),
        check_vma=False,
    )
```

time: 91.3 us -> 71.3 us (0.78)
  local copies, waits for them, and re-layouts: 16.3 us -> 0.11 us
  starting transfers between devices: 29.9 us -> 19.2 us
  Pallas kernels: 11.8 us -> 22 us
  waiting for transfers between devices: 30.9 us -> 28.6 us
  other arithmetic: 1.05 us -> 0.07 us
    ppermute x10 -> x4, waiting for transfers between devices: 30.3 us -> 4.98 us  [hop(): return lax.ppermute(value, 'dp', [(k, k ^ bits) for k in range(count)])]
    all_to_all x2, waiting for transfers between devices: 0.01 us -> 21.1 us  [the longest x1 14.8 us: body(): lax.all_to_all(send.reshape(count, stride, width), 'dp', split_axis=0, co...]
    unnamed x49 -> x16, local copies, waits for them, and re-layouts: 12.6 us -> 0.04 us
    ppermute x10 -> x4, starting transfers between devices: 15.1 us -> 4.5 us  [hop(): return lax.ppermute(value, 'dp', [(k, k ^ bits) for k in range(count)])]
    pallas_call x7 -> x9, Pallas kernels: 8.81 us -> 17.5 us  [the longest x8 16.8 us: call(): pl.pallas_call(kernel, out_shape=[o if k in out_free else space(o.shape,...]
    gather x2 -> x0, local copies, waits for them, and re-layouts: 3.53 us -> none  [the longest x1 2.86 us: body(): bank[jnp.concatenate([jnp.minimum(ids_row.reshape(slots), owned - 1), bot...]
    ppermute x4, waiting for transfers between devices: 0.56 us -> 2.46 us  [swap(): return lax.ppermute(value, 'mp', [(0, 1), (1, 0)])]
    ppermute x0 -> x1, starting transfers between devices: none -> 1.88 us  [two_hop(): lax.ppermute(value, ('dp', 'mp'), [(2 * k + c, 2 * (k ^ bits[c]) + c) for...]
  transfers between devices with their start and end apart: 16 -> 11, of which waited for: 9 -> 6; matrix products, arithmetic and copies ran while one was open for 6% -> 0% of each run, Pallas kernels for 7% -> 19%
where the time goes in v2:
time: 71.3 us; the launch traced here: 70.8 us
  waiting for transfers between devices  28.6 us (40%)
  Pallas kernels  22 us (31%)
  starting transfers between devices  19.2 us (27%)
  between operations  0.82 us (1%)
    pallas_call x8, Pallas kernels, call(): pl.pallas_call(kernel, out_shape=[o if k in out_free else space(o.shape,...  16.8 us
    all_to_all x1, waiting for transfers between devices, body(): lax.all_to_all(send.reshape(count, stride, width), 'dp', split_axis=0, co...  14.8 us
    all_to_all x1, starting transfers between devices, body(): lax.all_to_all(send.reshape(count, stride, width), 'dp', split_axis=0, co...  8.32 us
    all_to_all x1, waiting for transfers between devices, body(): back = lax.all_to_all(scaled, 'dp', split_axis=0, concat_axis=0)  6.29 us
    ppermute x4, waiting for transfers between devices, hop(): return lax.ppermute(value, 'dp', [(k, k ^ bits) for k in range(count)])  4.98 us
    pallas_call x1, Pallas kernels, owner_call(): pl.pallas_call(owner_kernel, grid=(owned // block,), in_specs=[pl.BlockSp...  4.55 us
    ppermute x4, starting transfers between devices, hop(): return lax.ppermute(value, 'dp', [(k, k ^ bits) for k in range(count)])  4.5 us
    all_to_all x1, starting transfers between devices, body(): back = lax.all_to_all(scaled, 'dp', split_axis=0, concat_axis=0)  4.25 us
  transfers between devices with their start and end apart: 11, of which 6 were waited for; matrix products, arithmetic and copies ran while one was open for 0% of the time, Pallas kernels for 19%

profile of v2, /device:TPU:0, one launch (start us, length us, event | category | flops | bytes accessed | tf_op | source)
XLA Modules:
  0.0 70.8 jit_solution(13334550826972935848)
XLA Ops:
  0.7 0.0 copy-start.2
  0.7 2.5 %shard_map.94 = bf16[896,384]{1,0:T(8,128)(2,1)} custom-call(s32[1,256]{1,0:T(1,128)} %bitcast.12, bf16[256,384]{1,0:T(8,128)(2,1)} %feat_ref.1), custom_call_target="tpu_custom_call" | custom-call | flops 176160768 | bytes 885760 | tf_op jit(solution)/shard_map/pallas_call | solution.py:21
  3.2 8.3 %all-to-all-start = ((bf16[16,56,384]{2,1,0:T(8,128)(2,1)}), bf16[16,56,384]{2,1,0:T(8,128)(2,1)S(1)}, u32[]{:S(2)}, u32[]{:S(2)}) async-start(bf16[16,56,384]{2,1,0:T(8,128)(2,1)} %bitcast.14), calls=%async_computation | async-start | bytes 1376256 | tf_op jit(solution)/shard_map/all_to_all | solution.py:377
  11.5 0.1 collective-permute-start
  11.6 0.1 reshape.33.neg_ref
  11.7 0.1 pad_add_fusion.self_ref
  11.8 2.9 %shard_map.93 = (s32[64,128]{1,0:T(8,128)S(1)}, f32[64,128]{1,0:T(8,128)S(1)}, f32[64,384]{1,0:T(8,128)S(1)}, bf16[1024,768]{1,0:T(8,128)(2,1)S(1)}) custom-call(s32[2]{0:T(128)S(1)} %pad_add_fusion.self_ref, s32[16,64]{1,0:T(8,128)S(1)} %reshape.33.neg_ref, f32[1,1024]{1,0:T(1,128)S(1)} %bitcast.11, f32[1024,384]{1,0:T(8,128)} %bank_ref.3), custom_call_target="tpu_custom_call" | custom-call | bytes 3317768 | tf_op jit(solution)/shard_map/pallas_call | solution.py:21
  14.7 14.8 %all-to-all-done = bf16[16,56,384]{2,1,0:T(8,128)(2,1)S(1)} async-done(((bf16[16,56,384]{2,1,0:T(8,128)(2,1)}), bf16[16,56,384]{2,1,0:T(8,128)(2,1)S(1)}, u32[]{:S(2)}, u32[]{:S(2)}) %all-to-all-start) | async-done | bytes 688160 | tf_op jit(solution)/shard_map/all_to_all | solution.py:377
  29.5 3.2 %shard_map.95 = (s32[1,768]{1,0:T(1,128)S(1)}, f32[768,384]{1,0:T(8,128)S(1)}, f32[72,384]{1,0:T(8,128)S(1)}, bf16[768,384]{1,0:T(8,128)(2,1)S(1)}) custom-call(bf16[256,384]{1,0:T(8,128)(2,1)} %copy-done.5, s32[64,128]{1,0:T(8,128)S(1)} %get-tuple-element.28.neg_ref, f32[64,384]{1,0:T(8,128)S(1)} %get-tuple-element.29.held_ref, ...), custom_call_target="tpu_custom_call" | custom-call | flops 2415919104 | bytes 4471808 | tf_op jit(solution)/shard_map/pallas_call | solution.py:21
  32.7 0.0 collective-permute-start.1
  32.8 1.3 %collective-permute-done.1.other_ref = f32[72,384]{1,0:T(8,128)S(1)} collective-permute-done((f32[72,384]{1,0:T(8,128)S(1)}, f32[72,384]{1,0:T(8,128)S(1)}, u32[]{:S(2)}, u32[]{:S(2)}) %collective-permute-start.1) | collective-permute-done | bytes 110624 | tf_op jit(solution)/shard_map/ppermute | solution.py:331
  34.1 0.8 %shard_map.96 = (bf16[64,768]{1,0:T(8,128)(2,1)S(1)}, bf16[32,768]{1,0:T(8,128)(2,1)S(1)}, f32[1,768]{1,0:T(1,128)S(1)}) custom-call(s32[2]{0:T(128)S(1)} %pad_add_fusion.self_ref, s32[1,768]{1,0:T(1,128)S(1)} %get-tuple-element.31.ids_ref, s32[64,128]{1,0:T(8,128)S(1)} %get-tuple-element.28.neg_ref, f32[64,128]{1,0:T(8,128)S(1)} %get-tuple-element.32.old_ref, ...), custom_call_target="tpu_custom_call" | custom-call | bytes 440328 | tf_op jit(solution)/shard_map/pallas_call | solution.py:21
  34.9 1.9 %collective-permute-start.2 = (bf16[64,768]{1,0:T(8,128)(2,1)S(1)}, bf16[64,768]{1,0:T(8,128)(2,1)S(1)}, u32[]{:S(2)}, u32[]{:S(2)}) collective-permute-start(bf16[64,768]{1,0:T(8,128)(2,1)S(1)} %get-tuple-element.40), channel_id=1, source_target_pairs={{0,8},{1,17},{2,10},{3,19},{4,12},{5,21},{6,14},{7,23},{8,0},{9,25... | collective-permute-start | bytes 294920 | tf_op jit(solution)/shard_map/ppermute | solution.py:339
  36.8 1.0 %collective-permute-start.3 = (bf16[32,768]{1,0:T(8,128)(2,1)S(1)}, bf16[32,768]{1,0:T(8,128)(2,1)S(1)}, u32[]{:S(2)}, u32[]{:S(2)}) collective-permute-start(bf16[32,768]{1,0:T(8,128)(2,1)S(1)} %get-tuple-element.39.refs_1_), channel_id=1, source_target_pairs={{0,24},{2,26},{4,28},{6,30},{8,16},{10,18},{12,20},{14,22},{16,8},... | collective-permute-start | bytes 147464 | tf_op jit(solution)/shard_map/ppermute | solution.py:335
  37.8 1.6 %shard_map.98.refs_0_ = bf16[16,48,384]{2,1,0:T(8,128)(2,1)} custom-call(s32[1,768]{1,0:T(1,128)S(1)} %get-tuple-element.31.ids_ref, f32[768,384]{1,0:T(8,128)S(1)} %get-tuple-element.38.new_ref, f32[1,768]{1,0:T(1,128)S(1)} %get-tuple-element.34.dist_ref), custom_call_target="tpu_custom_call" | custom-call | bytes 1775616 | tf_op jit(solution)/shard_map/pallas_call | solution.py:21
  39.4 3.4 %collective-permute-done.3.refs_3_ = bf16[32,768]{1,0:T(8,128)(2,1)S(1)} collective-permute-done((bf16[32,768]{1,0:T(8,128)(2,1)S(1)}, bf16[32,768]{1,0:T(8,128)(2,1)S(1)}, u32[]{:S(2)}, u32[]{:S(2)}) %collective-permute-start.3) | collective-permute-done | bytes 49184 | tf_op jit(solution)/shard_map/ppermute | solution.py:335
  42.7 0.7 shard_map.99
  43.4 1.0 %collective-permute-start.6 = (bf16[128,768]{1,0:T(8,128)(2,1)}, bf16[128,768]{1,0:T(8,128)(2,1)}, u32[]{:S(2)}, u32[]{:S(2)}) collective-permute-start(bf16[128,768]{1,0:T(8,128)(2,1)} %get-tuple-element.41.refs_0_), channel_id=1, source_target_pairs={{0,6},{2,4},{4,2},{6,0},{8,14},{10,12},{12,10},{14,8},{16,22},{18,... | collective-permute-start | bytes 589832 | tf_op jit(solution)/shard_map/ppermute | solution.py:335
  44.4 1.3 %collective-permute-start.5 = (bf16[128,768]{1,0:T(8,128)(2,1)}, bf16[128,768]{1,0:T(8,128)(2,1)}, u32[]{:S(2)}, u32[]{:S(2)}) collective-permute-start(bf16[128,768]{1,0:T(8,128)(2,1)} %get-tuple-element.41.refs_0_), channel_id=1, source_target_pairs={{0,4},{2,6},{4,0},{6,2},{8,12},{10,14},{12,8},{14,10},{16,20},{18,... | collective-permute-start | bytes 589832 | tf_op jit(solution)/shard_map/ppermute | solution.py:335
  45.7 1.2 %collective-permute-start.4 = (bf16[128,768]{1,0:T(8,128)(2,1)}, bf16[128,768]{1,0:T(8,128)(2,1)}, u32[]{:S(2)}, u32[]{:S(2)}) collective-permute-start(bf16[128,768]{1,0:T(8,128)(2,1)} %get-tuple-element.41.refs_0_), channel_id=1, source_target_pairs={{0,2},{2,0},{4,6},{6,4},{8,10},{10,8},{12,14},{14,12},{16,18},{18,... | collective-permute-start | bytes 589832 | tf_op jit(solution)/shard_map/ppermute | solution.py:335
  46.9 4.2 %all-to-all-start.1 = ((bf16[16,48,384]{2,1,0:T(8,128)(2,1)}), bf16[16,48,384]{2,1,0:T(8,128)(2,1)}, u32[]{:S(2)}, u32[]{:S(2)}) async-start(bf16[16,48,384]{2,1,0:T(8,128)(2,1)} %get-tuple-element.44), calls=%async_computation.1 | async-start | bytes 1179648 | tf_op jit(solution)/shard_map/all_to_all | solution.py:415
  51.2 0.0 copy-start.3
  51.2 0.0 copy-start.6
  51.2 4.5 %shard_map.97 = (f32[1024,384]{1,0:T(8,128)}, f32[1,1024]{1,0:T(1,128)}) custom-call(s32[1,768]{1,0:T(1,128)S(1)} %get-tuple-element.31.ids_ref, f32[1,768]{1,0:T(1,128)S(1)} %get-tuple-element.34.dist_ref, bf16[768,384]{1,0:T(8,128)(2,1)S(1)} %get-tuple-element.35.got_ref, f32[1024,384]{1,0:T(8,128)} %bank_ref.3, f32[1,1024]{1,0:T(1,128)} %bitcast.10), custom_call_target="tpu_custom_call" | custom-call | flops 999999995904 | bytes 3145728 | tf_op jit(solution)/shard_map/pallas_call | solution.py:265
  55.7 1.6 %collective-permute-done.5.refs_2_ = bf16[128,768]{1,0:T(8,128)(2,1)} collective-permute-done((bf16[128,768]{1,0:T(8,128)(2,1)}, bf16[128,768]{1,0:T(8,128)(2,1)}, u32[]{:S(2)}, u32[]{:S(2)}) %collective-permute-start.5) | collective-permute-done | bytes 196640 | tf_op jit(solution)/shard_map/ppermute | solution.py:335
  57.4 2.6 %shard_map.100 = (f32[256,384]{1,0:T(8,128)S(1)}, f32[8,256]{1,0:T(8,128)S(1)}, f32[264,384]{1,0:T(8,128)S(1)}, s32[256,128]{1,0:T(8,128)S(1)}, bf16[256,384]{1,0:T(8,128)(2,1)S(1)}) custom-call(f32[1,1024]{1,0:T(1,128)} %get-tuple-element.37.after_ref, s32[1,256]{1,0:T(1,128)S(1)} %bitcast.13, bf16[256,384]{1,0:T(8,128)(2,1)S(1)} %copy-done.4, ...), custom_call_target="tpu_custom_call" | custom-call | flops 402653184 | bytes 2319360 | tf_op jit(solution)/shard_map/pallas_call | solution.py:21
  60.0 0.1 collective-permute-start.8
  60.0 6.3 %all-to-all-done.1 = bf16[16,48,384]{2,1,0:T(8,128)(2,1)} async-done(((bf16[16,48,384]{2,1,0:T(8,128)(2,1)}), bf16[16,48,384]{2,1,0:T(8,128)(2,1)}, u32[]{:S(2)}, u32[]{:S(2)}) %all-to-all-start.1) | async-done | bytes 589856 | tf_op jit(solution)/shard_map/all_to_all | solution.py:415
  66.3 1.6 %shard_map.101 = (bf16[256,384]{1,0:T(8,128)(2,1)S(1)}, f32[8,256]{1,0:T(8,128)S(1)}) custom-call(s32[256,128]{1,0:T(8,128)S(1)} %get-tuple-element.42.slot_ref, bf16[256,384]{1,0:T(8,128)(2,1)S(1)} %get-tuple-element.43.query_ref, bf16[768,384]{1,0:T(8,128)(2,1)} %bitcast.7.back_ref), custom_call_target="tpu_custom_call" | custom-call | flops 150994944 | bytes 1122304 | tf_op jit(solution)/shard_map/pallas_call | solution.py:21
  67.9 0.0 collective-permute-start.7
  68.0 1.1 %collective-permute-done.7.far_ref = f32[8,256]{1,0:T(8,128)S(1)} collective-permute-done((f32[8,256]{1,0:T(8,128)S(1)}, f32[8,256]{1,0:T(8,128)S(1)}, u32[]{:S(2)}, u32[]{:S(2)}) %collective-permute-start.7) | collective-permute-done | bytes 8224 | tf_op jit(solution)/shard_map/ppermute | solution.py:331
  69.1 1.6 %shard_map.102 = (f32[1,256]{1,0:T(1,128)}, f32[256,384]{1,0:T(8,128)}) custom-call(s32[2]{0:T(128)S(1)} %copy-done.1, f32[8,256]{1,0:T(8,128)S(1)} %get-tuple-element.45.part_ref, f32[8,256]{1,0:T(8,128)S(1)} %collective-permute-done.7.far_ref, f32[8,256]{1,0:T(8,128)S(1)} %get-tuple-element.46.stats_ref, f32[256,384]{1,0:T(8,128)S(1)} %get-tuple-element.47.keep_ref, ...), custom_call_target="tpu_custom_call" | custom-call | bytes 1414152 | tf_op jit(solution)/shard_map/pallas_call | solution.py:21
  (18 shorter events, 0.0 us)
Async XLA Ops:
  0.6 10.9 %copy-start.4 = (bf16[256,384]{1,0:T(8,128)(2,1)S(1)}, bf16[256,384]{1,0:T(8,128)(2,1)}, u32[]{:S(2)}) copy-start(bf16[256,384]{1,0:T(8,128)(2,1)} %mine_ref.1) | copy-start | bytes 589828
  0.6 11.0 %copy-start.7 = (s32[1024]{0:T(1024)S(1)}, s32[1024]{0:T(1024)}, u32[]{:S(2)}) copy-start(s32[1024]{0:T(1024)} %param.11) | copy-start | bytes 12292
  0.7 11.1 %copy-start.2 = (f32[1024]{0:T(1024)S(1)}, f32[1024]{0:T(1024)}, u32[]{:S(2)}) copy-start(f32[1024]{0:T(1024)} %param.10) | copy-start | bytes 12292
  3.2 26.3 %all-to-all-start = ((bf16[16,56,384]{2,1,0:T(8,128)(2,1)}), bf16[16,56,384]{2,1,0:T(8,128)(2,1)S(1)}, u32[]{:S(2)}, u32[]{:S(2)}) async-start(bf16[16,56,384]{2,1,0:T(8,128)(2,1)} %bitcast.14), calls=%async_computation | async-start | bytes 1376256 | tf_op jit(solution)/shard_map/all_to_all | solution.py:377
  11.5 3.1 %collective-permute-start = (bf16[256,384]{1,0:T(8,128)(2,1)S(1)}, bf16[256,384]{1,0:T(8,128)(2,1)S(1)}, u32[]{:S(2)}, u32[]{:S(2)}) collective-permute-start(bf16[256,384]{1,0:T(8,128)(2,1)S(1)} %copy-done.4), channel_id=1, source_target_pairs={{0,1},{1,0},{2,3},{3,2},{4,5},{5,4},{6,7},{7,6},{8,9},{9,8},{10,11... | collective-permute-start | bytes 589832 | tf_op jit(solution)/shard_map/ppermute | solution.py:331
  11.8 22.3 %copy-start = (s32[2]{0:T(128)}, s32[2]{0:T(128)S(1)}, u32[]{:S(2)}) copy-start(s32[2]{0:T(128)S(1)} %pad_add_fusion.self_ref) | copy-start | bytes 28
  14.6 14.9 %copy-start.5 = (bf16[256,384]{1,0:T(8,128)(2,1)}, bf16[256,384]{1,0:T(8,128)(2,1)S(1)}, u32[]{:S(2)}) copy-start(bf16[256,384]{1,0:T(8,128)(2,1)S(1)} %collective-permute-done.after_ref.other_ref) | copy-start | bytes 589828
  32.7 1.4 %collective-permute-start.1 = (f32[72,384]{1,0:T(8,128)S(1)}, f32[72,384]{1,0:T(8,128)S(1)}, u32[]{:S(2)}, u32[]{:S(2)}) collective-permute-start(f32[72,384]{1,0:T(8,128)S(1)} %get-tuple-element.33.pack_ref), channel_id=1, source_target_pairs={{0,1},{1,0},{2,3},{3,2},{4,5},{5,4},{6,7},{7,6},{8,9},{9,8},{10,11... | collective-permute-start | bytes 331784 | tf_op jit(solution)/shard_map/ppermute | solution.py:331
  34.9 7.8 %collective-permute-start.2 = (bf16[64,768]{1,0:T(8,128)(2,1)S(1)}, bf16[64,768]{1,0:T(8,128)(2,1)S(1)}, u32[]{:S(2)}, u32[]{:S(2)}) collective-permute-start(bf16[64,768]{1,0:T(8,128)(2,1)S(1)} %get-tuple-element.40), channel_id=1, source_target_pairs={{0,8},{1,17},{2,10},{3,19},{4,12},{5,21},{6,14},{7,23},{8,0},{9,25... | collective-permute-start | bytes 294920 | tf_op jit(solution)/shard_map/ppermute | solution.py:339
  36.8 5.9 %collective-permute-start.3 = (bf16[32,768]{1,0:T(8,128)(2,1)S(1)}, bf16[32,768]{1,0:T(8,128)(2,1)S(1)}, u32[]{:S(2)}, u32[]{:S(2)}) collective-permute-start(bf16[32,768]{1,0:T(8,128)(2,1)S(1)} %get-tuple-element.39.refs_1_), channel_id=1, source_target_pairs={{0,24},{2,26},{4,28},{6,30},{8,16},{10,18},{12,20},{14,22},{16,8},... | collective-permute-start | bytes 147464 | tf_op jit(solution)/shard_map/ppermute | solution.py:335
  43.4 12.3 %collective-permute-start.6 = (bf16[128,768]{1,0:T(8,128)(2,1)}, bf16[128,768]{1,0:T(8,128)(2,1)}, u32[]{:S(2)}, u32[]{:S(2)}) collective-permute-start(bf16[128,768]{1,0:T(8,128)(2,1)} %get-tuple-element.41.refs_0_), channel_id=1, source_target_pairs={{0,6},{2,4},{4,2},{6,0},{8,14},{10,12},{12,10},{14,8},{16,22},{18,... | collective-permute-start | bytes 589832 | tf_op jit(solution)/shard_map/ppermute | solution.py:335
  44.4 12.9 %collective-permute-start.5 = (bf16[128,768]{1,0:T(8,128)(2,1)}, bf16[128,768]{1,0:T(8,128)(2,1)}, u32[]{:S(2)}, u32[]{:S(2)}) collective-permute-start(bf16[128,768]{1,0:T(8,128)(2,1)} %get-tuple-element.41.refs_0_), channel_id=1, source_target_pairs={{0,4},{2,6},{4,0},{6,2},{8,12},{10,14},{12,8},{14,10},{16,20},{18,... | collective-permute-start | bytes 589832 | tf_op jit(solution)/shard_map/ppermute | solution.py:335
  45.7 11.6 %collective-permute-start.4 = (bf16[128,768]{1,0:T(8,128)(2,1)}, bf16[128,768]{1,0:T(8,128)(2,1)}, u32[]{:S(2)}, u32[]{:S(2)}) collective-permute-start(bf16[128,768]{1,0:T(8,128)(2,1)} %get-tuple-element.41.refs_0_), channel_id=1, source_target_pairs={{0,2},{2,0},{4,6},{6,4},{8,10},{10,8},{12,14},{14,12},{16,18},{18,... | collective-permute-start | bytes 589832 | tf_op jit(solution)/shard_map/ppermute | solution.py:335
  46.9 19.4 %all-to-all-start.1 = ((bf16[16,48,384]{2,1,0:T(8,128)(2,1)}), bf16[16,48,384]{2,1,0:T(8,128)(2,1)}, u32[]{:S(2)}, u32[]{:S(2)}) async-start(bf16[16,48,384]{2,1,0:T(8,128)(2,1)} %get-tuple-element.44), calls=%async_computation.1 | async-start | bytes 1179648 | tf_op jit(solution)/shard_map/all_to_all | solution.py:415
  51.2 6.2 %copy-start.3 = (s32[256]{0:T(256)S(1)}, s32[256]{0:T(256)}, u32[]{:S(2)}) copy-start(s32[256]{0:T(256)} %param.7) | copy-start | bytes 3076
  51.2 6.2 %copy-start.6 = (bf16[256,384]{1,0:T(8,128)(2,1)S(1)}, bf16[256,384]{1,0:T(8,128)(2,1)}, u32[]{:S(2)}) copy-start(bf16[256,384]{1,0:T(8,128)(2,1)} %copy-done.5) | copy-start | bytes 589828
  55.7 13.4 %copy-start.1 = (s32[2]{0:T(128)S(1)}, s32[2]{0:T(128)}, u32[]{:S(2)}) copy-start(s32[2]{0:T(128)} %copy-done) | copy-start | bytes 28
  60.0 8.0 %collective-permute-start.8 = (f32[264,384]{1,0:T(8,128)S(1)}, f32[264,384]{1,0:T(8,128)S(1)}, u32[]{:S(2)}, u32[]{:S(2)}) collective-permute-start(f32[264,384]{1,0:T(8,128)S(1)} %get-tuple-element.48), channel_id=1, source_target_pairs={{0,1},{1,0},{2,3},{3,2},{4,5},{5,4},{6,7},{7,6},{8,9},{9,8},{10,11... | collective-permute-start | bytes 1216520 | tf_op jit(solution)/shard_map/ppermute | solution.py:331
  67.9 1.2 %collective-permute-start.7 = (f32[8,256]{1,0:T(8,128)S(1)}, f32[8,256]{1,0:T(8,128)S(1)}, u32[]{:S(2)}, u32[]{:S(2)}) collective-permute-start(f32[8,256]{1,0:T(8,128)S(1)} %get-tuple-element.45.part_ref), channel_id=1, source_target_pairs={{0,1},{1,0},{2,3},{3,2},{4,5},{5,4},{6,7},{7,6},{8,9},{9,8},{10,11... | collective-permute-start | bytes 24584 | tf_op jit(solution)/shard_map/ppermute | solution.py:331

commit v3 on v2

--- a/solution.py
+++ b/solution.py
@@ -24,6 +24,7 @@
         in_specs=[pl.BlockSpec(memory_space=space) for space in spaces],
         out_specs=[pl.BlockSpec(memory_space=space) for space in out_spaces],
         scratch_shapes=list(scratch),
+        name=getattr(kernel, "func", kernel).__name__,
         compiler_params=pltpu.CompilerParams(vmem_limit_bytes=VMEM),
         cost_estimate=pl.CostEstimate(flops=flops, bytes_accessed=moved, transcendentals=0),
     )(*[placed(a, space, k in free) for k, (a, space) in enumerate(zip(args, spaces))])
@@ -79,10 +80,9 @@
     return (owner * stride + rank).astype(I32)
 
 
-def pack_kernel(owners, owned, capacity, label_ref, feat_ref, send_ref, label_buf, feat_buf, send_buf, sems):
-    slots, width = send_buf.shape
-    rows = label_buf.shape[1]
-    stride = slots // owners
+def pack_kernel(owners, owned, stride, label_ref, feat_ref, send_ref, label_buf, feat_buf, send_buf, sems):
+    rows, width = feat_buf.shape
+    block = send_buf.shape[0] // owners
     labels = pltpu.make_async_copy(label_ref, label_buf, sems.at[0])
     feats = pltpu.make_async_copy(feat_ref, feat_buf, sems.at[1])
     labels.start()
@@ -93,19 +93,24 @@
     slot = slot_of(mine, rank, stride)
     value = jnp.where(mine, (label - iota((owners, rows), 0) * owned + 1).astype(F32), 0.0)
     high = jnp.floor(value * (1.0 / 32.0))
-    low = value - 32.0 * high
+    value = jnp.concatenate([high, value - 32.0 * high], axis=0).astype(BF16)
     place = onehot(to_col(rank)[:, 0:1] == iota((rows, LANES), 1).astype(F32))
-    ids = jnp.concatenate(
-        [nn(high.astype(BF16), place), nn(low.astype(BF16), place), jnp.zeros((owners, width - 2 * LANES), F32)], axis=1
-    ).astype(BF16)
+    ids = nn(value, place).astype(BF16)
+    row, part = iota((8 * owners, 2 * owners), 0), iota((8 * owners, 2 * owners), 1)
+    ids = nn(onehot(row == jnp.where(part < owners, 8 * part, 8 * (part - owners) + 1)), ids).astype(BF16)
     feats.wait()
-    half = slots // 2
+    half = owners // 2
     copies = []
     for k in range(2):
-        at = slice(k * half, (k + 1) * half)
-        spot = iota((half, rows), 0) + k * half
-        last = iota((half, owners), 0) + k * half == iota((half, owners), 1) * stride + capacity
-        send_buf[at, :] = (nn(onehot(spot == slot), feat_buf[...]) + nn(onehot(last), ids)).astype(BF16)
+        spot = iota((half * stride, rows), 0) + k * half * stride
+        picked = nn(onehot(spot == slot), feat_buf[...]).astype(BF16)
+        for b in range(half):
+            at = (k * half + b) * block
+            for j in range(width // LANES):
+                piece = picked[b * stride : (b + 1) * stride, j * LANES : (j + 1) * LANES]
+                send_buf[at + j * stride : at + (j + 1) * stride, :] = piece
+            send_buf[at + block - 8 : at + block, :] = ids[(k * half + b) * 8 : (k * half + b + 1) * 8, :]
+        at = slice(k * half * block, (k + 1) * half * block)
         copies.append(pltpu.make_async_copy(send_buf.at[at, :], send_ref.at[at, :], sems.at[2 + k]))
         copies[k].start()
     for c in copies:
@@ -144,28 +149,29 @@
     return jnp.where(counts > 0, 0.5 * bank + 0.5 * sums / safe, bank)
 
 
-def mean_kernel(owners, capacity, after_ref, neg_ref, held_ref, parts_ref, got_ref, ids_ref, new_ref, pack_ref, rows_ref):
+def mean_kernel(owners, after_ref, neg_ref, held_ref, parts_ref, got_ref, ids_ref, new_ref, pack_ref, rows_ref):
     owned = parts_ref.shape[0]
     negs, width = held_ref.shape
-    sent_rows = got_ref.shape[0]
-    stride = sent_rows // owners
     slots = rows_ref.shape[0]
     keep = slots // owners
-    last = iota((owners, sent_rows), 1) == iota((owners, sent_rows), 0) * stride + capacity
-    sent = nn(onehot(last), got_ref[:, 0 : 2 * LANES]).astype(BF16)
+    block = got_ref.shape[0] // owners
+    stride = (block - 8) // (width // LANES)
+    spot, part = iota((2 * owners, got_ref.shape[0]), 1), iota((2 * owners, got_ref.shape[0]), 0)
+    first = jnp.where(part < owners, part * block, (part - owners) * block + 1) + block - 8
+    sent = nn(onehot(spot == first), got_ref[...]).astype(BF16)
     place = iota((LANES, slots), 1).astype(F32)
     within = place - keep * jnp.floor((place + 0.5) * (1.0 / keep))
     spread = onehot(within == iota((LANES, slots), 0).astype(F32))
-    wide = 32.0 * nn(sent[:, 0:LANES], spread) + nn(sent[:, LANES:], spread)
+    wide = 32.0 * nn(sent[0:owners], spread) + nn(sent[owners:], spread)
     first = iota((owners, slots), 0) * keep
     spot = iota((owners, slots), 1)
     ids = jnp.sum(jnp.where((spot >= first) & (spot < first + keep), wide, 0.0), axis=0, keepdims=True)
     ids = jnp.where(ids > 0.5, ids - 1.0, float(owned)).astype(I32)
     ids_ref[...] = ids
-    for b in range(owners if keep < stride else 0):
-        rows_ref[b * keep : (b + 1) * keep, :] = got_ref[b * stride : b * stride + keep, :]
-    if keep == stride:
-        rows_ref[...] = got_ref[...]
+    for b in range(owners):
+        for j in range(width // LANES):
+            at = b * block + j * stride
+            rows_ref[b * keep : (b + 1) * keep, j * LANES : (j + 1) * LANES] = got_ref[at : at + keep, :]
     got = rows_ref[...]
     col = id_col(ids)
     parts = 3
@@ -236,7 +242,7 @@
 
 
 def join_kernel(*refs):
-    pieces, joined = refs[1:-2], refs[-2]
+    pieces, joined = refs[:-1], refs[-1]
     at = 0
     for p in pieces:
         joined[at : at + p.shape[0], :] = p[...]
@@ -274,8 +280,9 @@
         ],
         out_specs=[pl.BlockSpec((block, width), lambda k: (k, 0)), pl.BlockSpec((1, block), lambda k: (0, k))],
         out_shape=[shape((owned, width), F32), shape((1, owned), F32)],
+        name="owner_kernel",
         compiler_params=pltpu.CompilerParams(vmem_limit_bytes=VMEM),
-        cost_estimate=pl.CostEstimate(flops=10**12, bytes_accessed=8 * owned * width, transcendentals=0),
+        cost_estimate=pl.CostEstimate(flops=10000000000, bytes_accessed=8 * owned * width, transcendentals=0),
     )(ids, dist, got, placed(bank, pltpu.HBM), placed(old, pltpu.HBM))
 
 
@@ -349,6 +356,7 @@
         in_specs=[pl.BlockSpec(memory_space=pltpu.HBM)] + [pl.BlockSpec(memory_space=pltpu.VMEM) for _ in pieces],
         out_specs=[pl.BlockSpec(memory_space=pltpu.VMEM), pl.BlockSpec(memory_space=pltpu.HBM)],
         input_output_aliases={0: 1},
+        name="join_kernel",
         compiler_params=pltpu.CompilerParams(vmem_limit_bytes=VMEM),
     )(placed(value, pltpu.HBM), *[placed(p, pltpu.VMEM) for p in pieces])
 
@@ -359,7 +367,8 @@
     owned, width = bank.shape
     rows = features.shape[0]
     capacity = 3 * rows // count
-    stride = 8 * -(-(capacity + 1) // 8)
+    stride = 8 * -(-capacity // 8)
+    block = stride * (width // LANES) + 8
     slots = count * stride
     negs = neg_index.shape[0] // count
     half = negs // 2
@@ -368,14 +377,14 @@
 
     label_row = labels.reshape(1, rows)
     (send,) = call(
-        functools.partial(pack_kernel, count, owned, capacity),
-        (shape((slots, width), BF16),),
+        functools.partial(pack_kernel, count, owned, stride),
+        (shape((count * block, LANES), BF16),),
         label_row, features, flops=2 * slots * rows * width, hbm=(0, 1), out_hbm=(0,),
-        scratch=[*loads, pltpu.VMEM((slots, width), BF16), pltpu.SemaphoreType.DMA((4,))],
+        scratch=[*loads, pltpu.VMEM((count * block, LANES), BF16), pltpu.SemaphoreType.DMA((4,))],
     )
     query_far = swap(queries)
-    got = lax.all_to_all(send.reshape(count, stride, width), "dp", split_axis=0, concat_axis=0)
-    got = got.reshape(slots, width)
+    got = lax.all_to_all(send.reshape(count, block, LANES), "dp", split_axis=0, concat_axis=0)
+    got = got.reshape(count * block, LANES)
 
     neg_col, old_col, held, parts = call(
         split_kernel,
@@ -383,11 +392,9 @@
         place, neg_index.reshape(count, negs), old_conc.reshape(1, owned), bank, smem=(0,), hbm=(3,), free=(1, 2),
         scratch=[pltpu.VMEM((owned, width), F32), pltpu.SemaphoreType.DMA],
     )
-    sent_rows = slots
-    slots = count * capacity if capacity % 16 == 0 else slots
     extra = 8 * -(-slots // (8 * width))
     ids, new, pack, got = call(
-        functools.partial(mean_kernel, count, capacity),
+        functools.partial(mean_kernel, count),
         (shape((1, slots), I32), shape((slots, width), F32), shape((negs + extra, width), F32), shape((slots, width), BF16)),
         query_far, neg_col, held, parts, got, flops=8 * slots * owned * width, hbm=(0,),
     )
@@ -399,12 +406,12 @@
     (scaled,) = call(
         functools.partial(scale_kernel, capacity),
         (shape((count, capacity, width), BF16),),
-        ids, new, dist, out_hbm=(0,),
+        ids, new, dist, out_hbm=(0,), flops=1000000000000,
         scratch=[pltpu.VMEM((count, capacity, width), BF16), pltpu.SemaphoreType.DMA((2,))],
     )
     step = count // 4
     line = [own, two_hop(full, count, (step, 2 * step)), hop(own, count, 3 * step)]
-    joined, scaled = join(scaled, line)
+    (joined,) = call(join_kernel, (shape((sum(p.shape[0] for p in line), 2 * width), BF16),), *line)
     pieces = [joined]
     while step > 1:
         few = min(4, step)

time: 71.3 us -> 66.4 us (0.931)
  waiting for transfers between devices: 28.6 us -> 25.4 us
  Pallas kernels: 22 us -> 20.5 us
    all_to_all x1, waiting for transfers between devices: 6.29 us -> 0.01 us  [body(): back = lax.all_to_all(scaled, 'dp', split_axis=0, concat_axis=0)]
    ppermute x4, waiting for transfers between devices: 4.98 us -> 9.58 us  [hop(): return lax.ppermute(value, 'dp', [(k, k ^ bits) for k in range(count)])]
    ppermute x1, starting transfers between devices: 1.88 us -> 0.01 us  [two_hop(): lax.ppermute(value, ('dp', 'mp'), [(2 * k + c, 2 * (k ^ bits[c]) + c) for...]
    all_to_all x1, waiting for transfers between devices: 14.8 us -> 13.7 us  [body(): lax.all_to_all(send.reshape(count, block, LANES), 'dp', split_axis=0, con...]
    ppermute x4, starting transfers between devices: 4.5 us -> 5.36 us  [hop(): return lax.ppermute(value, 'dp', [(k, k ^ bits) for k in range(count)])]
    pallas_call x8 -> x9, Pallas kernels: 16.8 us -> 16 us  [call(): pl.pallas_call(kernel, out_shape=[o if k in out_free else space(o.shape,...]
  transfers between devices with their start and end apart: 11 -> 11, of which waited for: 6 -> 7; matrix products, arithmetic and copies ran while one was open for 0% -> 0% of each run, Pallas kernels for 19% -> 18%
where the time goes in v3:
time: 66.4 us; the launch traced here: 65.9 us
  waiting for transfers between devices  25.4 us (38%)
  Pallas kernels  20.5 us (31%)
  starting transfers between devices  19 us (29%)
  between operations  0.8 us (1%)
    pallas_call x9, Pallas kernels, call(): pl.pallas_call(kernel, out_shape=[o if k in out_free else space(o.shape,...  16 us
    all_to_all x1, waiting for transfers between devices, body(): lax.all_to_all(send.reshape(count, block, LANES), 'dp', split_axis=0, con...  13.7 us
    ppermute x4, waiting for transfers between devices, hop(): return lax.ppermute(value, 'dp', [(k, k ^ bits) for k in range(count)])  9.58 us
    all_to_all x1, starting transfers between devices, body(): lax.all_to_all(send.reshape(count, block, LANES), 'dp', split_axis=0, con...  8.33 us
    ppermute x4, starting transfers between devices, hop(): return lax.ppermute(value, 'dp', [(k, k ^ bits) for k in range(count)])  5.36 us
    all_to_all x1, starting transfers between devices, body(): back = lax.all_to_all(scaled, 'dp', split_axis=0, concat_axis=0)  4.59 us
    pallas_call x1, Pallas kernels, owner_call(): pl.pallas_call(owner_kernel, grid=(owned // block,), in_specs=[pl.BlockSp...  4.54 us
    ppermute x4, waiting for transfers between devices, swap(): return lax.ppermute(value, 'mp', [(0, 1), (1, 0)])  2.14 us
  transfers between devices with their start and end apart: 11, of which 7 were waited for; matrix products, arithmetic and copies ran while one was open for 0% of the time, Pallas kernels for 18%

profile of v3, /device:TPU:0, one launch (start us, length us, event | category | flops | bytes accessed | tf_op | source)
XLA Modules:
  0.0 65.9 jit_solution(2193919429754493341)
XLA Ops:
  0.7 0.0 copy-start.2
  0.7 2.4 %pack_kernel.1 = bf16[2432,128]{1,0:T(8,128)(2,1)} custom-call(s32[1,256]{1,0:T(1,128)} %bitcast.13, bf16[256,384]{1,0:T(8,128)(2,1)} %feat_ref.1), custom_call_target="tpu_custom_call" | custom-call | flops 150994944 | bytes 820224 | tf_op jit(solution)/shard_map/pack_kernel/pallas_call | solution.py:21
  3.1 8.3 %all-to-all-start = ((bf16[16,152,128]{2,1,0:T(8,128)(2,1)}), bf16[16,152,128]{2,1,0:T(8,128)(2,1)S(1)}, u32[]{:S(2)}, u32[]{:S(2)}) async-start(bf16[16,152,128]{2,1,0:T(8,128)(2,1)} %bitcast.15), calls=%async_computation | async-start | bytes 1245184 | tf_op jit(solution)/shard_map/all_to_all | solution.py:386
  11.5 0.1 collective-permute-start
  11.6 0.1 reshape.33.neg_ref
  11.6 0.1 pad_add_fusion.self_ref
  11.7 2.9 %split_kernel.1 = (s32[64,128]{1,0:T(8,128)S(1)}, f32[64,128]{1,0:T(8,128)S(1)}, f32[64,384]{1,0:T(8,128)S(1)}, bf16[1024,768]{1,0:T(8,128)(2,1)S(1)}) custom-call(s32[2]{0:T(128)S(1)} %pad_add_fusion.self_ref, s32[16,64]{1,0:T(8,128)S(1)} %reshape.33.neg_ref, f32[1,1024]{1,0:T(1,128)S(1)} %bitcast.12, f32[1024,384]{1,0:T(8,128)} %bank_ref.3), custom_call_target="tpu_custom_call" | custom-call | bytes 3317768 | tf_op jit(solution)/shard_map/split_kernel/pallas_call | solution.py:21
  14.6 0.0 copy-start.5
  14.6 13.7 %all-to-all-done = bf16[16,152,128]{2,1,0:T(8,128)(2,1)S(1)} async-done(((bf16[16,152,128]{2,1,0:T(8,128)(2,1)}), bf16[16,152,128]{2,1,0:T(8,128)(2,1)S(1)}, u32[]{:S(2)}, u32[]{:S(2)}) %all-to-all-start) | async-done | bytes 622624 | tf_op jit(solution)/shard_map/all_to_all | solution.py:386
  28.3 3.2 %mean_kernel.1 = (s32[1,768]{1,0:T(1,128)S(1)}, f32[768,384]{1,0:T(8,128)S(1)}, f32[72,384]{1,0:T(8,128)S(1)}, bf16[768,384]{1,0:T(8,128)(2,1)S(1)}) custom-call(bf16[256,384]{1,0:T(8,128)(2,1)} %copy-done.5, s32[64,128]{1,0:T(8,128)S(1)} %get-tuple-element.26.neg_ref, f32[64,384]{1,0:T(8,128)S(1)} %get-tuple-element.27.held_ref, ...), custom_call_target="tpu_custom_call" | custom-call | flops 2415919104 | bytes 4406272 | tf_op jit(solution)/shard_map/mean_kernel/pallas_call | solution.py:21
  31.5 0.0 collective-permute-start.1
  31.5 1.3 %collective-permute-done.1.other_ref = f32[72,384]{1,0:T(8,128)S(1)} collective-permute-done((f32[72,384]{1,0:T(8,128)S(1)}, f32[72,384]{1,0:T(8,128)S(1)}, u32[]{:S(2)}, u32[]{:S(2)}) %collective-permute-start.1) | collective-permute-done | bytes 110624 | tf_op jit(solution)/shard_map/ppermute | solution.py:338
  32.8 1.5 %neg_kernel.1 = (bf16[64,768]{1,0:T(8,128)(2,1)}, bf16[32,768]{1,0:T(8,128)(2,1)}, f32[1,768]{1,0:T(1,128)S(1)}) custom-call(s32[2]{0:T(128)S(1)} %pad_add_fusion.self_ref, s32[1,768]{1,0:T(1,128)S(1)} %get-tuple-element.29.ids_ref, s32[64,128]{1,0:T(8,128)S(1)} %get-tuple-element.26.neg_ref, f32[64,128]{1,0:T(8,128)S(1)} %get-tuple-element.30.old_ref, ...), custom_call_target="tpu_custom_call" | custom-call | bytes 440328 | tf_op jit(solution)/shard_map/neg_kernel/pallas_call | solution.py:21
  34.3 1.8 %collective-permute-start.3 = (bf16[32,768]{1,0:T(8,128)(2,1)}, bf16[32,768]{1,0:T(8,128)(2,1)}, u32[]{:S(2)}, u32[]{:S(2)}) collective-permute-start(bf16[32,768]{1,0:T(8,128)(2,1)} %get-tuple-element.36.refs_0_), channel_id=1, source_target_pairs={{0,24},{2,26},{4,28},{6,30},{8,16},{10,18},{12,20},{14,22},{16,8},... | collective-permute-start | bytes 147464 | tf_op jit(solution)/shard_map/ppermute | solution.py:342
  36.1 0.0 collective-permute-start.2
  36.1 1.6 %scale_kernel.1 = bf16[16,48,384]{2,1,0:T(8,128)(2,1)} custom-call(s32[1,768]{1,0:T(1,128)S(1)} %get-tuple-element.29.ids_ref, f32[768,384]{1,0:T(8,128)S(1)} %get-tuple-element.40.new_ref, f32[1,768]{1,0:T(1,128)S(1)} %get-tuple-element.32.dist_ref), custom_call_target="tpu_custom_call" | custom-call | flops 999999995904 | bytes 1775616 | tf_op jit(solution)/shard_map/scale_kernel/pallas_call | solution.py:21
  37.7 4.6 %all-to-all-start.1 = ((bf16[16,48,384]{2,1,0:T(8,128)(2,1)}), bf16[16,48,384]{2,1,0:T(8,128)(2,1)S(1)}, u32[]{:S(2)}, u32[]{:S(2)}) async-start(bf16[16,48,384]{2,1,0:T(8,128)(2,1)} %scale_kernel.1), calls=%async_computation.1 | async-start | bytes 1179648 | tf_op jit(solution)/shard_map/all_to_all | solution.py:422
  42.3 0.9 %join_kernel.1.refs_0_ = bf16[128,768]{1,0:T(8,128)(2,1)S(1)} custom-call(bf16[32,768]{1,0:T(8,128)(2,1)} %get-tuple-element.36.refs_0_, bf16[64,768]{1,0:T(8,128)(2,1)} %collective-permute-done.2.refs_1_, bf16[32,768]{1,0:T(8,128)(2,1)} %collective-permute-done.3.refs_2_), custom_call_target="tpu_custom_call" | custom-call | bytes 393216 | tf_op jit(solution)/shard_map/join_kernel/pallas_call | solution.py:21
  43.2 2.9 %collective-permute-start.6 = (bf16[128,768]{1,0:T(8,128)(2,1)S(1)}, bf16[128,768]{1,0:T(8,128)(2,1)S(1)}, u32[]{:S(2)}, u32[]{:S(2)}) collective-permute-start(bf16[128,768]{1,0:T(8,128)(2,1)S(1)} %join_kernel.1.refs_0_), channel_id=1, source_target_pairs={{0,6},{2,4},{4,2},{6,0},{8,14},{10,12},{12,10},{14,8},{16,22},{18,... | collective-permute-start | bytes 589832 | tf_op jit(solution)/shard_map/ppermute | solution.py:342
  46.1 0.6 collective-permute-start.5
  46.7 0.1 collective-permute-start.4
  46.8 4.5 %owner_kernel.1 = (f32[1024,384]{1,0:T(8,128)}, f32[1,1024]{1,0:T(1,128)}) custom-call(s32[1,768]{1,0:T(1,128)S(1)} %get-tuple-element.29.ids_ref, f32[1,768]{1,0:T(1,128)S(1)} %get-tuple-element.32.dist_ref, bf16[768,384]{1,0:T(8,128)(2,1)S(1)} %get-tuple-element.33.got_ref, f32[1024,384]{1,0:T(8,128)} %bank_ref.3, f32[1,1024]{1,0:T(1,128)} %bitcast.11), custom_call_target="tpu_custom_call" | custom-call | flops 10000000000 | bytes 3145728 | tf_op jit(solution)/shard_map/owner_kernel/pallas_call | solution.py:271
  51.3 5.1 %collective-permute-done.6.refs_3_ = bf16[128,768]{1,0:T(8,128)(2,1)S(1)} collective-permute-done((bf16[128,768]{1,0:T(8,128)(2,1)S(1)}, bf16[128,768]{1,0:T(8,128)(2,1)S(1)}, u32[]{:S(2)}, u32[]{:S(2)}) %collective-permute-start.6) | collective-permute-done | bytes 196640 | tf_op jit(solution)/shard_map/ppermute | solution.py:342
  56.4 3.9 %collective-permute-done.5.refs_2_ = bf16[128,768]{1,0:T(8,128)(2,1)S(1)} collective-permute-done((bf16[128,768]{1,0:T(8,128)(2,1)S(1)}, bf16[128,768]{1,0:T(8,128)(2,1)S(1)}, u32[]{:S(2)}, u32[]{:S(2)}) %collective-permute-start.5) | collective-permute-done | bytes 196640 | tf_op jit(solution)/shard_map/ppermute | solution.py:342
  60.3 0.6 collective-permute-done.4.refs_1_
  60.9 1.4 %flash_kernel.1 = (f32[256,384]{1,0:T(8,128)S(1)}, f32[8,256]{1,0:T(8,128)S(1)}, f32[264,384]{1,0:T(8,128)S(1)}, s32[256,128]{1,0:T(8,128)S(1)}, bf16[256,384]{1,0:T(8,128)(2,1)S(1)}) custom-call(f32[1,1024]{1,0:T(1,128)} %get-tuple-element.35.after_ref, s32[1,256]{1,0:T(1,128)S(1)} %bitcast.14, bf16[256,384]{1,0:T(8,128)(2,1)S(1)} %copy-done.4, ...), custom_call_target="tpu_custom_call" | custom-call | flops 402653184 | bytes 2319360 | tf_op jit(solution)/shard_map/flash_kernel/pallas_call | solution.py:21
  62.3 0.1 collective-permute-start.8
  62.4 0.5 positive_kernel.1
  62.9 0.5 collective-permute-start.7
  63.4 0.6 collective-permute-done.8.sent_ref
  64.1 0.2 collective-permute-done.7.far_ref
  64.3 1.6 %final_kernel.1 = (f32[1,256]{1,0:T(1,128)}, f32[256,384]{1,0:T(8,128)}) custom-call(s32[2]{0:T(128)S(1)} %copy-done.1, f32[8,256]{1,0:T(8,128)S(1)} %get-tuple-element.41.part_ref, f32[8,256]{1,0:T(8,128)S(1)} %collective-permute-done.7.far_ref, f32[8,256]{1,0:T(8,128)S(1)} %get-tuple-element.42.stats_ref, f32[256,384]{1,0:T(8,128)S(1)} %get-tuple-element.43.keep_ref, ...), custom_call_target="tpu_custom_call" | custom-call | bytes 1414152 | tf_op jit(solution)/shard_map/final_kernel/pallas_call | solution.py:21
  (18 shorter events, 0.0 us)
Async XLA Ops:
  0.6 10.8 %copy-start.4 = (bf16[256,384]{1,0:T(8,128)(2,1)S(1)}, bf16[256,384]{1,0:T(8,128)(2,1)}, u32[]{:S(2)}) copy-start(bf16[256,384]{1,0:T(8,128)(2,1)} %mine_ref.1) | copy-start | bytes 589828
  0.6 10.9 %copy-start.7 = (s32[1024]{0:T(1024)S(1)}, s32[1024]{0:T(1024)}, u32[]{:S(2)}) copy-start(s32[1024]{0:T(1024)} %param.11) | copy-start | bytes 12292
  0.7 11.1 %copy-start.2 = (f32[1024]{0:T(1024)S(1)}, f32[1024]{0:T(1024)}, u32[]{:S(2)}) copy-start(f32[1024]{0:T(1024)} %param.10) | copy-start | bytes 12292
  3.1 25.2 %all-to-all-start = ((bf16[16,152,128]{2,1,0:T(8,128)(2,1)}), bf16[16,152,128]{2,1,0:T(8,128)(2,1)S(1)}, u32[]{:S(2)}, u32[]{:S(2)}) async-start(bf16[16,152,128]{2,1,0:T(8,128)(2,1)} %bitcast.15), calls=%async_computation | async-start | bytes 1245184 | tf_op jit(solution)/shard_map/all_to_all | solution.py:386
  11.5 3.1 %collective-permute-start = (bf16[256,384]{1,0:T(8,128)(2,1)S(1)}, bf16[256,384]{1,0:T(8,128)(2,1)S(1)}, u32[]{:S(2)}, u32[]{:S(2)}) collective-permute-start(bf16[256,384]{1,0:T(8,128)(2,1)S(1)} %copy-done.4), channel_id=1, source_target_pairs={{0,1},{1,0},{2,3},{3,2},{4,5},{5,4},{6,7},{7,6},{8,9},{9,8},{10,11... | collective-permute-start | bytes 589832 | tf_op jit(solution)/shard_map/ppermute | solution.py:338
  11.7 21.1 %copy-start = (s32[2]{0:T(128)}, s32[2]{0:T(128)S(1)}, u32[]{:S(2)}) copy-start(s32[2]{0:T(128)S(1)} %pad_add_fusion.self_ref) | copy-start | bytes 28
  14.6 13.7 %copy-start.5 = (bf16[256,384]{1,0:T(8,128)(2,1)}, bf16[256,384]{1,0:T(8,128)(2,1)S(1)}, u32[]{:S(2)}) copy-start(bf16[256,384]{1,0:T(8,128)(2,1)S(1)} %collective-permute-done.after_ref.other_ref) | copy-start | bytes 589828
  31.5 1.4 %collective-permute-start.1 = (f32[72,384]{1,0:T(8,128)S(1)}, f32[72,384]{1,0:T(8,128)S(1)}, u32[]{:S(2)}, u32[]{:S(2)}) collective-permute-start(f32[72,384]{1,0:T(8,128)S(1)} %get-tuple-element.31.pack_ref), channel_id=1, source_target_pairs={{0,1},{1,0},{2,3},{3,2},{4,5},{5,4},{6,7},{7,6},{8,9},{9,8},{10,11... | collective-permute-start | bytes 331784 | tf_op jit(solution)/shard_map/ppermute | solution.py:338
  34.3 8.0 %collective-permute-start.3 = (bf16[32,768]{1,0:T(8,128)(2,1)}, bf16[32,768]{1,0:T(8,128)(2,1)}, u32[]{:S(2)}, u32[]{:S(2)}) collective-permute-start(bf16[32,768]{1,0:T(8,128)(2,1)} %get-tuple-element.36.refs_0_), channel_id=1, source_target_pairs={{0,24},{2,26},{4,28},{6,30},{8,16},{10,18},{12,20},{14,22},{16,8},... | collective-permute-start | bytes 147464 | tf_op jit(solution)/shard_map/ppermute | solution.py:342
  36.1 6.2 %collective-permute-start.2 = (bf16[64,768]{1,0:T(8,128)(2,1)}, bf16[64,768]{1,0:T(8,128)(2,1)}, u32[]{:S(2)}, u32[]{:S(2)}) collective-permute-start(bf16[64,768]{1,0:T(8,128)(2,1)} %get-tuple-element.37), channel_id=1, source_target_pairs={{0,8},{1,17},{2,10},{3,19},{4,12},{5,21},{6,14},{7,23},{8,0},{9,25... | collective-permute-start | bytes 294920 | tf_op jit(solution)/shard_map/ppermute | solution.py:346
  37.7 24.7 %all-to-all-start.1 = ((bf16[16,48,384]{2,1,0:T(8,128)(2,1)}), bf16[16,48,384]{2,1,0:T(8,128)(2,1)S(1)}, u32[]{:S(2)}, u32[]{:S(2)}) async-start(bf16[16,48,384]{2,1,0:T(8,128)(2,1)} %scale_kernel.1), calls=%async_computation.1 | async-start | bytes 1179648 | tf_op jit(solution)/shard_map/all_to_all | solution.py:422
  43.2 13.2 %collective-permute-start.6 = (bf16[128,768]{1,0:T(8,128)(2,1)S(1)}, bf16[128,768]{1,0:T(8,128)(2,1)S(1)}, u32[]{:S(2)}, u32[]{:S(2)}) collective-permute-start(bf16[128,768]{1,0:T(8,128)(2,1)S(1)} %join_kernel.1.refs_0_), channel_id=1, source_target_pairs={{0,6},{2,4},{4,2},{6,0},{8,14},{10,12},{12,10},{14,8},{16,22},{18,... | collective-permute-start | bytes 589832 | tf_op jit(solution)/shard_map/ppermute | solution.py:342
  46.1 14.2 %collective-permute-start.5 = (bf16[128,768]{1,0:T(8,128)(2,1)S(1)}, bf16[128,768]{1,0:T(8,128)(2,1)S(1)}, u32[]{:S(2)}, u32[]{:S(2)}) collective-permute-start(bf16[128,768]{1,0:T(8,128)(2,1)S(1)} %join_kernel.1.refs_0_), channel_id=1, source_target_pairs={{0,4},{2,6},{4,0},{6,2},{8,12},{10,14},{12,8},{14,10},{16,20},{18,... | collective-permute-start | bytes 589832 | tf_op jit(solution)/shard_map/ppermute | solution.py:342
  46.7 14.2 %collective-permute-start.4 = (bf16[128,768]{1,0:T(8,128)(2,1)S(1)}, bf16[128,768]{1,0:T(8,128)(2,1)S(1)}, u32[]{:S(2)}, u32[]{:S(2)}) collective-permute-start(bf16[128,768]{1,0:T(8,128)(2,1)S(1)} %join_kernel.1.refs_0_), channel_id=1, source_target_pairs={{0,2},{2,0},{4,6},{6,4},{8,10},{10,8},{12,14},{14,12},{16,18},{18,... | collective-permute-start | bytes 589832 | tf_op jit(solution)/shard_map/ppermute | solution.py:342
  46.8 14.1 %copy-start.3 = (s32[256]{0:T(256)S(1)}, s32[256]{0:T(256)}, u32[]{:S(2)}) copy-start(s32[256]{0:T(256)} %param.7) | copy-start | bytes 3076
  46.8 14.1 %copy-start.6 = (bf16[256,384]{1,0:T(8,128)(2,1)S(1)}, bf16[256,384]{1,0:T(8,128)(2,1)}, u32[]{:S(2)}) copy-start(bf16[256,384]{1,0:T(8,128)(2,1)} %copy-done.5) | copy-start | bytes 589828
  51.3 12.9 %copy-start.1 = (s32[2]{0:T(128)S(1)}, s32[2]{0:T(128)}, u32[]{:S(2)}) copy-start(s32[2]{0:T(128)} %copy-done) | copy-start | bytes 28
  62.3 1.8 %collective-permute-start.8 = (f32[264,384]{1,0:T(8,128)S(1)}, f32[264,384]{1,0:T(8,128)S(1)}, u32[]{:S(2)}, u32[]{:S(2)}) collective-permute-start(f32[264,384]{1,0:T(8,128)S(1)} %get-tuple-element.44), channel_id=1, source_target_pairs={{0,1},{1,0},{2,3},{3,2},{4,5},{5,4},{6,7},{7,6},{8,9},{9,8},{10,11... | collective-permute-start | bytes 1216520 | tf_op jit(solution)/shard_map/ppermute | solution.py:338
  62.9 1.4 %collective-permute-start.7 = (f32[8,256]{1,0:T(8,128)S(1)}, f32[8,256]{1,0:T(8,128)S(1)}, u32[]{:S(2)}, u32[]{:S(2)}) collective-permute-start(f32[8,256]{1,0:T(8,128)S(1)} %get-tuple-element.41.part_ref), channel_id=1, source_target_pairs={{0,1},{1,0},{2,3},{3,2},{4,5},{5,4},{6,7},{7,6},{8,9},{9,8},{10,11... | collective-permute-start | bytes 24584 | tf_op jit(solution)/shard_map/ppermute | solution.py:338

commit v4 on v3

v4 whole, which is shorter than its diff:
```python
import functools

import jax
import jax.numpy as jnp
from jax import lax
from jax.experimental import pallas as pl
from jax.experimental.pallas import tpu as pltpu
from jax.sharding import PartitionSpec as P

F32 = jnp.float32
BF16 = jnp.bfloat16
I32 = jnp.int32
LANES = 128
VMEM = 24 * 2**20


def call(kernel, outs, *args, flops=0, smem=(), hbm=(), out_hbm=(), free=(), out_free=(), scratch=()):
    moved = sum(a.size * a.dtype.itemsize for a in args) + sum(o.size * o.dtype.itemsize for o in outs)
    spaces = [pltpu.SMEM if k in smem else pltpu.HBM if k in hbm else pltpu.VMEM for k in range(len(args))]
    out_spaces = [pltpu.HBM if k in out_hbm else pltpu.VMEM for k in range(len(outs))]
    return pl.pallas_call(
        kernel,
        out_shape=[o if k in out_free else space(o.shape, o.dtype) for k, (o, space) in enumerate(zip(outs, out_spaces))],
        in_specs=[pl.BlockSpec(memory_space=space) for space in spaces],
        out_specs=[pl.BlockSpec(memory_space=space) for space in out_spaces],
        scratch_shapes=list(scratch),
        name=getattr(kernel, "func", kernel).__name__,
        compiler_params=pltpu.CompilerParams(vmem_limit_bytes=VMEM),
        cost_estimate=pl.CostEstimate(flops=flops, bytes_accessed=moved, transcendentals=0),
    )(*[placed(a, space, k in free) for k, (a, space) in enumerate(zip(args, spaces))])


def placed(value, space, free=False):
    return value if free or space is pltpu.SMEM else pltpu.with_memory_space_constraint(value, space)


def shape(dims, dtype):
    return jax.ShapeDtypeStruct(dims, dtype)


def nt(a, b):
    return lax.dot_general(a, b, (((1,), (1,)), ((), ())), preferred_element_type=F32)


def nn(a, b):
    return jnp.dot(a, b, preferred_element_type=F32)


def iota(dims, axis):
    return lax.broadcasted_iota(I32, dims, axis)


def onehot(mask):
    return jnp.where(mask, 1.0, 0.0).astype(BF16)


def to_col(row):
    return jnp.transpose(jnp.broadcast_to(row, (LANES, row.shape[1])))


def to_row(col):
    return jnp.transpose(jnp.broadcast_to(col, (col.shape[0], LANES)))[0:1, :]


def id_col(ids):
    return to_col(ids.astype(F32))[:, 0:1].astype(I32)


def ahead(rows):
    return onehot(iota((rows, rows), 0) <= iota((rows, rows), 1))


def ranks_of(label, owners, owned, before):
    start = iota((owners, label.shape[1]), 0) * owned
    mine = (label >= start) & (label < start + owned)
    running = nn(onehot(mine), before)
    return mine, jnp.sum(jnp.where(mine, running, 0.0), axis=0, keepdims=True) - 1.0


def slot_of(mine, rank, stride):
    owner = jnp.sum(jnp.where(mine, iota(mine.shape, 0).astype(F32), 0.0), axis=0, keepdims=True)
    return (owner * stride + rank).astype(I32)


def pack_kernel(owners, owned, stride, label_ref, feat_ref, send_ref, label_buf, feat_buf, send_buf, sems):
    rows, width = feat_buf.shape
    block = send_buf.shape[0] // owners
    labels = pltpu.make_async_copy(label_ref, label_buf, sems.at[0])
    feats = pltpu.make_async_copy(feat_ref, feat_buf, sems.at[1])
    labels.start()
    feats.start()
    before = ahead(rows)
    labels.wait()
    label = label_buf[...]
    mine, rank = ranks_of(label, owners, owned, before)
    slot = slot_of(mine, rank, stride)
    value = jnp.where(mine, (label - iota((owners, rows), 0) * owned + 1).astype(F32), 0.0)
    high = jnp.floor(value * (1.0 / 32.0))
    value = jnp.concatenate([high, value - 32.0 * high], axis=0).astype(BF16)
    ids = nt(value, onehot(iota((LANES, rows), 0).astype(F32) == rank))
    feats.wait()
    chunks = 4
    part = owners // chunks
    copies = []
    row = iota((8, LANES), 0)
    for k in range(chunks):
        spot = iota((part * stride, rows), 0) + k * part * stride
        picked = nn(onehot(spot == slot), feat_buf[...]).astype(BF16)
        for c in range(part):
            b = k * part + c
            for j in range(width // LANES):
                piece = picked[c * stride : (c + 1) * stride, j * LANES : (j + 1) * LANES]
                send_buf[b * block + j * stride : b * block + (j + 1) * stride, :] = piece
            tail = jnp.where(row == 0, ids[b : b + 1], jnp.where(row == 1, ids[owners + b : owners + b + 1], 0.0))
            send_buf[(b + 1) * block - 8 : (b + 1) * block, :] = tail.astype(BF16)
        at = slice(k * part * block, (k + 1) * part * block)
        copies.append(pltpu.make_async_copy(send_buf.at[at, :], send_ref.at[at, :], sems.at[2 + k]))
        copies[k].start()
    for c in copies:
        c.wait()


def split_kernel(keep, self_ref, neg_ref, old_ref, bank_ref, neg_col_ref, old_col_ref, held_ref, parts_ref, spread_ref, bank_buf, sem):
    owned, width = bank_buf.shape
    negs = neg_ref.shape[1]
    load = pltpu.make_async_copy(bank_ref, bank_buf, sem)
    load.start()
    me = self_ref[0]
    wanted = neg_ref[pl.ds(me, 1), :] - me * owned
    wanted = jnp.concatenate([wanted] * (LANES // negs), axis=1)
    neg_col = id_col(wanted)[0:negs, :]
    neg_col_ref[...] = jnp.broadcast_to(neg_col, neg_col_ref.shape)
    same = neg_col == iota((negs, owned), 1)
    old = jnp.sum(jnp.where(same, old_ref[...], 0.0), axis=1, keepdims=True)
    old_col_ref[...] = jnp.broadcast_to(old, old_col_ref.shape)
    pick = onehot(same)
    place = iota(spread_ref.shape, 1).astype(F32)
    within = place - keep * jnp.floor((place + 0.5) * (1.0 / keep))
    spread_ref[...] = onehot(within == iota(spread_ref.shape, 0).astype(F32))
    load.wait()
    bank = bank_buf[...]
    high = bank.astype(BF16)
    rest = bank - high.astype(F32)
    middle = rest.astype(BF16)
    low = (rest - middle.astype(F32)).astype(BF16)
    parts_ref[:, 0:width] = high
    parts_ref[:, width : 2 * width] = middle
    held_ref[...] = nn(pick, high) + nn(pick, middle) + nn(pick, low)


def blend(bank, sums, counts):
    safe = jnp.maximum(counts, 1.0)
    return jnp.where(counts > 0, 0.5 * bank + 0.5 * sums / safe, bank)


def mean_kernel(
    owners, after_ref, neg_ref, held_ref, parts_ref, spread_ref, got_ref,
    ids_ref, new_ref, pack_ref, rows_ref, count_ref, neg_count_ref, table,
):
    owned = parts_ref.shape[0]
    negs, width = held_ref.shape
    slots = new_ref.shape[0]
    keep = slots // owners
    block = got_ref.shape[0] // owners
    for b in range(owners):
        sent = got_ref[(b + 1) * block - 8 : (b + 1) * block, :].astype(F32)
        table[b : b + 1, :] = sent[0:1]
        table[owners + b : owners + b + 1, :] = sent[1:2]
        for j in range(width // LANES):
            at = b * block + j * keep
            rows_ref[b * keep : (b + 1) * keep, j * LANES : (j + 1) * LANES] = got_ref[at : at + keep, :]
    rows_ref[:, width:] = jnp.ones((slots, LANES), BF16)
    wide = nn(table[...].astype(BF16), spread_ref[...])
    wide = 32.0 * wide[0:owners] + wide[owners:]
    first = iota((owners, slots), 0) * keep
    spot = iota((owners, slots), 1)
    ids = jnp.sum(jnp.where((spot >= first) & (spot < first + keep), wide, 0.0), axis=0, keepdims=True)
    ids = jnp.where(ids > 0.5, ids - 1.0, float(owned)).astype(I32)
    ids_ref[...] = ids
    got = rows_ref[...]
    col = id_col(ids)
    block = 256 if slots % 256 == 0 else slots
    squares = []
    for k in range(slots // block):
        at = slice(k * block, (k + 1) * block)
        picked = nn(onehot(iota((block, owned), 1) == col[at]), parts_ref[...])
        sums = nn(onehot(col[at] == ids), got)
        count_ref[at, :] = sums[:, width:]
        new = blend(picked[:, 0:width] + picked[:, width:], sums[:, 0:width], sums[:, width : width + 1])
        new_ref[at, :] = new
        differ = got[at, 0:width].astype(F32) - new
        squares.append(jnp.sum(differ * differ, axis=1, keepdims=True))
    squared = to_row(jnp.concatenate(squares, axis=0))
    sums = nn(onehot(neg_ref[:, 0:1] == ids), got)
    neg_count_ref[...] = sums[:, width:]
    pack_ref[0:negs, :] = blend(held_ref[...], sums[:, 0:width], sums[:, width : width + 1])
    for k in range(-(-slots // width)):
        piece = squared[:, k * width : min((k + 1) * width, slots)]
        pack_ref[negs + k : negs + k + 1, 0 : piece.shape[1]] = piece


def weight_of(counts):
    safe = jnp.maximum(counts, 1.0)
    return safe * jnp.log(safe + 10.0)


def prepare_kernel(owners, owned, capacity, count_ref, label_ref, query_ref, weight_ref, slot_ref, copy_ref):
    weight_ref[...] = weight_of(count_ref[...])
    slot = slot_of(*ranks_of(label_ref[...], owners, owned, ahead(label_ref.shape[1])), capacity)
    slot_ref[...] = to_col(slot.astype(F32)).astype(I32)
    copy_ref[...] = query_ref[...]


def scale_kernel(
    capacity, self_ref, ids_ref, neg_ref, count_ref, old_ref, pack_ref, new_ref, weight_ref, other_ref,
    full_ref, own_ref, dist_ref, out_ref, full_buf, own_buf, buf, sems,
):
    slots, width = new_ref.shape
    negs = neg_ref.shape[0]
    half = negs // 2
    ids = ids_ref[...]
    pieces = []
    for k in range(-(-slots // width)):
        part = pack_ref[negs + k : negs + k + 1, :] + other_ref[negs + k : negs + k + 1, :]
        pieces.append(part[:, 0 : min(width, slots - k * width)])
    dist = jnp.sqrt(jnp.concatenate(pieces, axis=1) + 0.25)
    dist_ref[...] = dist
    total = jnp.sum(jnp.where(neg_ref[:, 0:1] == ids, dist, 0.0), axis=1, keepdims=True)
    counts = count_ref[:, 0:1]
    conc = jnp.where(counts > 0, total / weight_of(counts), old_ref[:, 0:1])
    mine = (pack_ref[0:negs, :] / conc).astype(BF16)
    other = (other_ref[0:negs, :] / conc).astype(BF16)
    full_buf[:, 0:width] = mine
    full_buf[:, width:] = other
    first = self_ref[1] == 0
    own_buf[:, 0:width] = jnp.where(first, mine[0:half], mine[half:])
    own_buf[:, width:] = jnp.where(first, other[0:half], other[half:])
    copies = [pltpu.make_async_copy(full_buf, full_ref, sems.at[0]), pltpu.make_async_copy(own_buf, own_ref, sems.at[1])]
    for c in copies:
        c.start()
    owners = out_ref.shape[0] // capacity
    stride = slots // owners
    col = id_col(ids)
    parts = 2
    for k in range(parts):
        at = slice(k * slots // parts, (k + 1) * slots // parts)
        total = jnp.sum(jnp.where(col[at] == ids, dist, 0.0), axis=1, keepdims=True)
        scaled = new_ref[at, :] / (total / weight_ref[at, 0:1])
        few = owners // parts
        to = slice(k * few * capacity, (k + 1) * few * capacity)
        if stride == capacity:
            buf[to, :] = scaled.astype(BF16)
        for b in range(few if stride != capacity else 0):
            at = (k * few + b) * capacity
            buf[at : at + capacity, :] = scaled[b * stride : b * stride + capacity].astype(BF16)
        copies.append(pltpu.make_async_copy(buf.at[to, :], out_ref.at[to, :], sems.at[2 + k]))
        copies[-1].start()
    for c in copies:
        c.wait()


def join_kernel(*refs):
    pieces, joined = refs[:-1], refs[-1]
    at = 0
    for p in pieces:
        joined[at : at + p.shape[0], :] = p[...]
        at += p.shape[0]


def again_kernel(after_ref, value_ref, out_ref):
    out_ref[...] = value_ref[...]


def owner_kernel(ids_ref, dist_ref, got_ref, bank_ref, old_ref, new_ref, conc_ref):
    block = bank_ref.shape[0]
    slots = got_ref.shape[0]
    base = pl.program_id(0) * block
    same = jnp.where(iota((block, slots), 0) + base == ids_ref[...], 1.0, 0.0)
    width = bank_ref.shape[1]
    sums = nn(same.astype(BF16), got_ref[...])
    new_ref[...] = blend(bank_ref[...], sums[:, 0:width], sums[:, width : width + 1])
    turned = iota((slots, block), 1) + base == id_col(ids_ref[...])
    counts = jnp.sum(jnp.where(turned, 1.0, 0.0), axis=0, keepdims=True)
    total = jnp.sum(jnp.where(turned, to_col(dist_ref[...])[:, 0:1], 0.0), axis=0, keepdims=True)
    conc_ref[...] = jnp.where(counts > 0, total / weight_of(counts), old_ref[...])


def owner_call(ids, dist, got, bank, old):
    owned, width = bank.shape
    slots = got.shape[0]
    block = 256
    whole = lambda k: (0, 0)
    return pl.pallas_call(
        owner_kernel,
        grid=(owned // block,),
        in_specs=[
            pl.BlockSpec((1, slots), whole),
            pl.BlockSpec((1, slots), whole),
            pl.BlockSpec(got.shape, whole),
            pl.BlockSpec((block, width), lambda k: (k, 0)),
            pl.BlockSpec((1, block), lambda k: (0, k)),
        ],
        out_specs=[pl.BlockSpec((block, width), lambda k: (k, 0)), pl.BlockSpec((1, block), lambda k: (0, k))],
        out_shape=[shape((owned, width), F32), shape((1, owned), F32)],
        name="owner_kernel",
        compiler_params=pltpu.CompilerParams(vmem_limit_bytes=VMEM),
        cost_estimate=pl.CostEstimate(flops=20000000000, bytes_accessed=8 * owned * width, transcendentals=0),
    )(ids, dist, got, placed(bank, pltpu.HBM), placed(old, pltpu.HBM))


def logits_kernel(after_ref, mine_ref, other_ref, *refs):
    parts, (weight_ref, negs_ref, stats_ref) = refs[:-3], refs[-3:]
    rows, width = mine_ref.shape
    at = 0
    for p in parts:
        negs_ref[at : at + p.shape[0], :] = p[...]
        at += p.shape[0]
    logits = nt(mine_ref[...], negs_ref[:, 0:width]) + nt(other_ref[...], negs_ref[:, width:])
    top = jnp.max(logits, axis=1, keepdims=True)
    weight = jnp.exp(logits - top)
    weight_ref[...] = weight.astype(BF16)
    total = jnp.sum(weight, axis=1, keepdims=True)
    lane = iota((rows, LANES), 1)
    stats = jnp.transpose(jnp.where(lane == 0, top, jnp.where(lane == 1, total, 0.0)))
    stats_ref[...] = stats[0:8, :]


def pull_kernel(weight_ref, negs_ref, keep_ref, send_ref):
    width = keep_ref.shape[1]
    grad = nn(weight_ref[...], negs_ref[...])
    send_ref[...] = grad[:, width:]
    keep_ref[...] = grad[:, 0:width]


def positive_kernel(slot_ref, query_ref, back_ref, rows_ref, part_ref):
    rows, slots = query_ref.shape[0], back_ref.shape[0]
    found = nn(onehot(iota((rows, slots), 1) == slot_ref[:, 0:1]), back_ref[...])
    rows_ref[...] = found.astype(BF16)
    part = to_row(jnp.sum(query_ref[...].astype(F32) * found, axis=1, keepdims=True))
    part_ref[...] = jnp.broadcast_to(part, part_ref.shape)


def factor_kernel(self_ref, part_ref, far_ref, here_ref, there_ref, loss_ref, factor_ref):
    rows = part_ref.shape[1]
    first = self_ref[1] == 0
    here, there = here_ref[0:2, :], there_ref[0:2, :]
    low = jnp.where(first, here, there)
    high = jnp.where(first, there, here)
    positive = part_ref[0:1, :] + far_ref[0:1, :]
    top = jnp.maximum(jnp.maximum(low[0:1], high[0:1]), positive)
    exppos = jnp.exp(positive - top)
    total = low[1:2] * jnp.exp(low[0:1] - top) + high[1:2] * jnp.exp(high[0:1] - top) + exppos
    loss_ref[...] = jnp.log(total) + top - positive
    factors = jnp.concatenate(
        [jnp.exp(here[0:1] - top) / total, jnp.exp(there[0:1] - top) / total, exppos / total - 1.0], axis=0
    )
    factor_ref[...] = jnp.transpose(jnp.concatenate([factors, jnp.zeros((LANES - 3, rows), F32)], axis=0))


def final_kernel(factor_ref, rows_ref, keep_ref, sent_ref, lost_ref, grad_ref, loss_ref, grad_buf, sems):
    rows = keep_ref.shape[0]
    half = rows // 2
    copies = [pltpu.make_async_copy(lost_ref, loss_ref, sems.at[2])]
    copies[0].start()
    for k in range(2):
        at = slice(k * half, (k + 1) * half)
        mine, other, pull = (factor_ref[at, j : j + 1] for j in range(3))
        grad_buf[at, :] = keep_ref[at, :] * mine + sent_ref[at, :] * other + pull * rows_ref[at, :].astype(F32)
        copies.append(pltpu.make_async_copy(grad_buf.at[at, :], grad_ref.at[at, :], sems.at[k]))
        copies[-1].start()
    for c in copies:
        c.wait()


def swap(value):
    return lax.ppermute(value, "mp", [(0, 1), (1, 0)])


def hop(value, count, bits):
    return lax.ppermute(value, "dp", [(k, k ^ bits) for k in range(count)])


def two_hop(value, count, bits):
    return lax.ppermute(
        value, ("dp", "mp"), [(2 * k + c, 2 * (k ^ bits[c]) + c) for k in range(count) for c in range(2)]
    )


def body(features, labels, queries, bank, old_conc, neg_index):
    count = lax.axis_size("dp")
    me, core = lax.axis_index("dp"), lax.axis_index("mp")
    owned, width = bank.shape
    rows = features.shape[0]
    capacity = 3 * rows // count
    stride = 8 * -(-capacity // 8)
    block = stride * (width // LANES) + 8
    slots = count * stride
    negs = neg_index.shape[0] // count
    half = negs // 2
    place = jnp.stack([me, core]).astype(I32)
    loads = [pltpu.VMEM((1, rows), I32), pltpu.VMEM((rows, width), BF16)]

    label_row = labels.reshape(1, rows)
    (send,) = call(
        functools.partial(pack_kernel, count, owned, stride),
        (shape((count * block, LANES), BF16),),
        label_row, features, flops=2 * slots * rows * width, hbm=(0, 1), out_hbm=(0,),
        scratch=[*loads, pltpu.VMEM((count * block, LANES), BF16), pltpu.SemaphoreType.DMA((6,))],
    )
    query_far = swap(queries)
    got = lax.all_to_all(send.reshape(count, block, LANES), "dp", split_axis=0, concat_axis=0)
    got = got.reshape(count * block, LANES)

    neg_col, old_col, held, parts, spread = call(
        functools.partial(split_kernel, stride),
        (
            shape((negs, LANES), I32), shape((negs, LANES), F32), shape((negs, width), F32),
            shape((owned, 2 * width), BF16), shape((LANES, slots), BF16),
        ),
        place, neg_index.reshape(count, negs), old_conc.reshape(1, owned), bank, smem=(0,), hbm=(3,), free=(1, 2),
        scratch=[pltpu.VMEM((owned, width), F32), pltpu.SemaphoreType.DMA],
    )
    extra = 8 * -(-slots // (8 * width))
    ids, new, pack, got, counts, neg_counts = call(
        functools.partial(mean_kernel, count),
        (
            shape((1, slots), I32), shape((slots, width), F32), shape((negs + extra, width), F32),
            shape((slots, width + LANES), BF16), shape((slots, LANES), F32), shape((negs, LANES), F32),
        ),
        query_far, neg_col, held, parts, spread, got, flops=8 * slots * owned * width, hbm=(0,),
        scratch=[pltpu.VMEM((2 * count, LANES), F32)],
    )
    weights, slot, query = call(
        functools.partial(prepare_kernel, count, owned, capacity),
        (shape((slots, LANES), F32), shape((rows, LANES), I32), shape((rows, width), BF16)),
        counts, label_row, queries, free=(1, 2),
    )
    full, own, dist, scaled = call(
        functools.partial(scale_kernel, capacity),
        (
            shape((negs, 2 * width), BF16), shape((half, 2 * width), BF16), shape((1, slots), F32),
            shape((count * capacity, width), BF16),
        ),
        place, ids, neg_col, neg_counts, old_col, pack, new, weights, swap(pack), smem=(0,), out_hbm=(0, 1, 3),
        scratch=[
            pltpu.VMEM((negs, 2 * width), BF16), pltpu.VMEM((half, 2 * width), BF16),
            pltpu.VMEM((count * capacity, width), BF16), pltpu.SemaphoreType.DMA((4,)),
        ],
    )
    step = count // 4
    line = [own, two_hop(full, count, (step, 2 * step)), hop(own, count, 3 * step)]
    (joined,) = call(join_kernel, (shape((sum(p.shape[0] for p in line), 2 * width), BF16),), *line)
    back = lax.all_to_all(scaled.reshape(count, capacity, width), "dp", split_axis=0, concat_axis=0)
    new_bank, new_conc = owner_call(ids, dist, got, bank, old_conc.reshape(1, owned))
    if step == 4:
        first = two_hop(joined, count, (1, 2))
        second = two_hop(joined, count, (2, 1))
        (again,) = call(again_kernel, (shape(joined.shape, BF16),), new_conc, first, hbm=(0,))
        pieces = [joined, again, second, two_hop(again, count, (2, 1))]
    while step > 1 and step != 4:
        few = min(4, step)
        step //= few
        pieces = [joined] + [hop(joined, count, step * k) for k in range(1, few)]
        if step > 1:
            joined = jnp.concatenate(pieces, axis=0)
    found, part = call(
        positive_kernel,
        (shape((rows, width), BF16), shape((8, rows), F32)),
        slot, query, back.reshape(count * capacity, width), flops=2 * slots * rows * width,
    )
    weight, all_negs, stats = call(
        logits_kernel,
        (shape((rows, half * count), BF16), shape((half * count, 2 * width), BF16), shape((8, rows), F32)),
        part, query, query_far, *pieces, flops=4 * rows * half * count * width, free=range(2, 99),
    )
    far_stats = swap(stats)
    keep, sent = call(
        pull_kernel,
        (shape((rows, width), F32), shape((rows, width), F32)),
        weight, all_negs, flops=4 * rows * half * count * width,
    )
    sent = swap(sent)
    loss, factors = call(
        factor_kernel,
        (shape((1, rows), F32), shape((rows, LANES), F32)),
        place, part, swap(part), stats, far_stats, smem=(0,),
    )
    grad, loss = call(
        final_kernel,
        (shape((rows, width), F32), shape((1, rows), F32)),
        factors, found, keep, sent, loss, out_hbm=(0, 1),
        scratch=[pltpu.VMEM((rows, width), F32), pltpu.SemaphoreType.DMA((3,))],
    )
    return (new_bank, new_conc.reshape(owned), loss.reshape(rows), grad)


def solution(mesh):
    placed = (P("dp", "mp"), P("dp"), P("dp", "mp"), P("dp", "mp"), P("dp"), P())
    return jax.shard_map(
        body,
        mesh=mesh,
        in_specs=placed,
        out_specs=(P("dp", "mp"), P("dp"), P("dp"), P("dp", "mp")),
        check_vma=False,
    )
```

time: 66.4 us -> 64.1 us (0.965)
  waiting for transfers between devices: 25.4 us -> 23 us
  Pallas kernels: 20.5 us -> 18.6 us
  starting transfers between devices: 19 us -> 20.2 us
  local copies, waits for them, and re-layouts: 0.11 us -> 0.91 us
    ppermute x4 -> x1, waiting for transfers between devices: 9.58 us -> 0.52 us  [hop(): return lax.ppermute(value, 'dp', [(k, k ^ bits) for k in range(count)])]
    all_to_all x1, waiting for transfers between devices: 0.01 us -> 6.65 us  [body(): lax.all_to_all(scaled.reshape(count, capacity, width), 'dp', split_axis=0...]
    ppermute x1 -> x4, starting transfers between devices: 0.01 us -> 5.47 us  [two_hop(): lax.ppermute(value, ('dp', 'mp'), [(2 * k + c, 2 * (k ^ bits[c]) + c) for...]
    ppermute x4 -> x1, starting transfers between devices: 5.36 us -> 0.98 us  [hop(): return lax.ppermute(value, 'dp', [(k, k ^ bits) for k in range(count)])]
    pallas_call x9 -> x12, Pallas kernels: 16 us -> 13.9 us  [call(): pl.pallas_call(kernel, out_shape=[o if k in out_free else space(o.shape,...]
    unnamed x16 -> x18, local copies, waits for them, and re-layouts: 0.04 us -> 0.84 us
    ppermute x4 -> x5, waiting for transfers between devices: 2.14 us -> 2.13 us  [swap(): return lax.ppermute(value, 'mp', [(0, 1), (1, 0)])]
  transfers between devices with their start and end apart: 11 -> 12, of which waited for: 7 -> 5; matrix products, arithmetic and copies ran while one was open for 0% -> 0% of each run, Pallas kernels for 18% -> 14%
where the time goes in v4:
time: 64.1 us; the launch traced here: 63.7 us
  waiting for transfers between devices  23 us (36%)
  starting transfers between devices  20.2 us (32%)
  Pallas kernels  18.6 us (29%)
  local copies, waits for them, and re-layouts  0.91 us (1%)
  between operations  0.83 us (1%)
    pallas_call x12, Pallas kernels, call(): pl.pallas_call(kernel, out_shape=[o if k in out_free else space(o.shape,...  13.9 us
    all_to_all x1, waiting for transfers between devices, body(): lax.all_to_all(send.reshape(count, block, LANES), 'dp', split_axis=0, con...  13.7 us
    all_to_all x1, starting transfers between devices, body(): lax.all_to_all(send.reshape(count, block, LANES), 'dp', split_axis=0, con...  8.33 us
    all_to_all x1, waiting for transfers between devices, body(): lax.all_to_all(scaled.reshape(count, capacity, width), 'dp', split_axis=0...  6.65 us
    ppermute x4, starting transfers between devices, two_hop(): lax.ppermute(value, ('dp', 'mp'), [(2 * k + c, 2 * (k ^ bits[c]) + c) for...  5.47 us
    pallas_call x1, Pallas kernels, owner_call(): pl.pallas_call(owner_kernel, grid=(owned // block,), in_specs=[pl.BlockSp...  4.72 us
    all_to_all x1, starting transfers between devices, body(): lax.all_to_all(scaled.reshape(count, capacity, width), 'dp', split_axis=0...  4.64 us
    ppermute x5, waiting for transfers between devices, swap(): return lax.ppermute(value, 'mp', [(0, 1), (1, 0)])  2.13 us
  transfers between devices with their start and end apart: 12, of which 5 were waited for; matrix products, arithmetic and copies ran while one was open for 0% of the time, Pallas kernels for 14%

profile of v4, /device:TPU:0, one launch (start us, length us, event | category | flops | bytes accessed | tf_op | source)
XLA Modules:
  0.0 63.7 jit_solution(3656922583684750629)
XLA Ops:
  0.7 2.1 %pack_kernel.1 = bf16[2432,128]{1,0:T(8,128)(2,1)} custom-call(s32[1,256]{1,0:T(1,128)} %bitcast.14, bf16[256,384]{1,0:T(8,128)(2,1)} %feat_ref.1), custom_call_target="tpu_custom_call" | custom-call | flops 150994944 | bytes 820224 | tf_op jit(solution)/shard_map/pack_kernel/pallas_call | solution.py:21
  2.8 8.3 %all-to-all-start = ((bf16[16,152,128]{2,1,0:T(8,128)(2,1)}), bf16[16,152,128]{2,1,0:T(8,128)(2,1)S(1)}, u32[]{:S(2)}, u32[]{:S(2)}) async-start(bf16[16,152,128]{2,1,0:T(8,128)(2,1)} %bitcast.16), calls=%async_computation | async-start | bytes 1245184 | tf_op jit(solution)/shard_map/all_to_all | solution.py:411
  11.1 0.1 collective-permute-start
  11.2 0.1 reshape.36.neg_ref
  11.3 0.1 pad_add_fusion.self_ref
  11.4 2.9 %split_kernel.1 = (s32[64,128]{1,0:T(8,128)S(1)}, f32[64,128]{1,0:T(8,128)S(1)}, f32[64,384]{1,0:T(8,128)S(1)}, bf16[1024,768]{1,0:T(8,128)(2,1)S(1)}, bf16[128,768]{1,0:T(8,128)(2,1)S(1)}) custom-call(s32[2]{0:T(128)S(1)} %pad_add_fusion.self_ref, s32[16,64]{1,0:T(8,128)S(1)} %reshape.36.neg_ref, f32[1,1024]{1,0:T(1,128)S(1)} %bitcast.13, f32[1024,384]{1,0:T(8,128)} %bank_ref.3), custom_call_target="tpu_custom_call" | custom-call | bytes 3514376 | tf_op jit(solution)/shard_map/split_kernel/pallas_call | solution.py:21
  14.3 13.7 %all-to-all-done = bf16[16,152,128]{2,1,0:T(8,128)(2,1)S(1)} async-done(((bf16[16,152,128]{2,1,0:T(8,128)(2,1)}), bf16[16,152,128]{2,1,0:T(8,128)(2,1)S(1)}, u32[]{:S(2)}, u32[]{:S(2)}) %all-to-all-start) | async-done | bytes 622624 | tf_op jit(solution)/shard_map/all_to_all | solution.py:411
  28.0 3.2 %mean_kernel.1 = (s32[1,768]{1,0:T(1,128)S(1)}, f32[768,384]{1,0:T(8,128)S(1)}, f32[72,384]{1,0:T(8,128)S(1)}, bf16[768,512]{1,0:T(8,128)(2,1)S(1)}, f32[768,128]{1,0:T(8,128)S(1)}, /*index=5*/f32[64,128]{1,0:T(8,128)S(1)}) custom-call(bf16[256,384]{1,0:T(8,128)(2,1)} %copy-done, s32[64,128]{1,0:T(8,128)S(1)} %get-tuple-element.35.neg_ref, ...), custom_call_target="tpu_custom_call" | custom-call | flops 2415919104 | bytes 5225472 | tf_op jit(solution)/shard_map/mean_kernel/pallas_call | solution.py:21
  31.1 0.1 collective-permute-start.1
  31.2 0.3 prepare_kernel.1
  31.5 1.0 %collective-permute-done.1.other_ref = f32[72,384]{1,0:T(8,128)S(1)} collective-permute-done((f32[72,384]{1,0:T(8,128)S(1)}, f32[72,384]{1,0:T(8,128)S(1)}, u32[]{:S(2)}, u32[]{:S(2)}) %collective-permute-start.1) | collective-permute-done | bytes 110624 | tf_op jit(solution)/shard_map/ppermute | solution.py:376
  32.5 2.1 %scale_kernel.1 = (bf16[64,768]{1,0:T(8,128)(2,1)}, bf16[32,768]{1,0:T(8,128)(2,1)}, f32[1,768]{1,0:T(1,128)S(1)}, bf16[768,384]{1,0:T(8,128)(2,1)}) custom-call(s32[2]{0:T(128)S(1)} %pad_add_fusion.self_ref, s32[1,768]{1,0:T(1,128)S(1)} %get-tuple-element.39.ids_ref, s32[64,128]{1,0:T(8,128)S(1)} %get-tuple-element.35.neg_ref, ...), custom_call_target="tpu_custom_call" | custom-call | bytes 2635784 | tf_op jit(solution)/shard_map/scale_kernel/pallas_call | solution.py:21
  34.7 1.7 %collective-permute-start.3 = (bf16[64,768]{1,0:T(8,128)(2,1)}, bf16[64,768]{1,0:T(8,128)(2,1)S(1)}, u32[]{:S(2)}, u32[]{:S(2)}) collective-permute-start(bf16[64,768]{1,0:T(8,128)(2,1)} %get-tuple-element.55), channel_id=1, source_target_pairs={{0,8},{1,17},{2,10},{3,19},{4,12},{5,21},{6,14},{7,23},{8,0},{9,25... | collective-permute-start | bytes 294920 | tf_op jit(solution)/shard_map/ppermute | solution.py:384
  36.3 1.0 %collective-permute-start.4 = (bf16[32,768]{1,0:T(8,128)(2,1)}, bf16[32,768]{1,0:T(8,128)(2,1)S(1)}, u32[]{:S(2)}, u32[]{:S(2)}) collective-permute-start(bf16[32,768]{1,0:T(8,128)(2,1)} %get-tuple-element.54.refs_0_), channel_id=1, source_target_pairs={{0,24},{2,26},{4,28},{6,30},{8,16},{10,18},{12,20},{14,22},{16,8},... | collective-permute-start | bytes 147464 | tf_op jit(solution)/shard_map/ppermute | solution.py:380
  37.3 4.6 %all-to-all-start.1 = ((bf16[16,48,384]{2,1,0:T(8,128)(2,1)}), bf16[16,48,384]{2,1,0:T(8,128)(2,1)S(1)}, u32[]{:S(2)}, u32[]{:S(2)}) async-start(bf16[16,48,384]{2,1,0:T(8,128)(2,1)} %bitcast.17), calls=%async_computation.1 | async-start | bytes 1179648 | tf_op jit(solution)/shard_map/all_to_all | solution.py:453
  42.0 0.5 collective-permute-done.4.refs_2_
  42.5 0.8 %copy-done.3 = bf16[32,768]{1,0:T(8,128)(2,1)S(1)} copy-done((bf16[32,768]{1,0:T(8,128)(2,1)S(1)}, bf16[32,768]{1,0:T(8,128)(2,1)}, u32[]{:S(2)}) %copy-start.3) | copy-done | bytes 49176
  43.3 1.5 %collective-permute-start.5 = (bf16[128,768]{1,0:T(8,128)(2,1)S(1)}, bf16[128,768]{1,0:T(8,128)(2,1)S(1)}, u32[]{:S(2)}, u32[]{:S(2)}) collective-permute-start(bf16[128,768]{1,0:T(8,128)(2,1)S(1)} %join_kernel.1.refs_0_), channel_id=1, source_target_pairs={{0,2},{1,5},{2,0},{3,7},{4,6},{5,1},{6,4},{7,3},{8,10},{9,13},{10,... | collective-permute-start | bytes 589832 | tf_op jit(solution)/shard_map/ppermute | solution.py:384
  44.8 4.7 %owner_kernel.1 = (f32[1024,384]{1,0:T(8,128)}, f32[1,1024]{1,0:T(1,128)}) custom-call(s32[1,768]{1,0:T(1,128)S(1)} %get-tuple-element.39.ids_ref, f32[1,768]{1,0:T(1,128)S(1)} %get-tuple-element.46.dist_ref, bf16[768,512]{1,0:T(8,128)(2,1)S(1)} %copy-done.7, f32[1024,384]{1,0:T(8,128)} %bank_ref.3, f32[1,1024]{1,0:T(1,128)} %bitcast.12), custom_call_target="tpu_custom_call" | custom-call | flops 20000000000 | bytes 3145728 | tf_op jit(solution)/shard_map/owner_kernel/pallas_call | solution.py:293
  49.5 1.5 %collective-permute-start.6 = (bf16[128,768]{1,0:T(8,128)(2,1)S(1)}, bf16[128,768]{1,0:T(8,128)(2,1)S(1)}, u32[]{:S(2)}, u32[]{:S(2)}) collective-permute-start(bf16[128,768]{1,0:T(8,128)(2,1)S(1)} %join_kernel.1.refs_0_), channel_id=1, source_target_pairs={{0,4},{1,3},{2,6},{3,1},{4,0},{5,7},{6,2},{7,5},{8,12},{9,11},{10,... | collective-permute-start | bytes 589832 | tf_op jit(solution)/shard_map/ppermute | solution.py:384
  51.0 0.9 %collective-permute-start.7 = (bf16[128,768]{1,0:T(8,128)(2,1)S(1)}, bf16[128,768]{1,0:T(8,128)(2,1)S(1)}, u32[]{:S(2)}, u32[]{:S(2)}) collective-permute-start(bf16[128,768]{1,0:T(8,128)(2,1)S(1)} %again_kernel.1.refs_1_), channel_id=1, source_target_pairs={{0,4},{1,3},{2,6},{3,1},{4,0},{5,7},{6,2},{7,5},{8,12},{9,11},{10,... | collective-permute-start | bytes 589832 | tf_op jit(solution)/shard_map/ppermute | solution.py:384
  51.9 6.7 %all-to-all-done.1 = bf16[16,48,384]{2,1,0:T(8,128)(2,1)S(1)} async-done(((bf16[16,48,384]{2,1,0:T(8,128)(2,1)}), bf16[16,48,384]{2,1,0:T(8,128)(2,1)S(1)}, u32[]{:S(2)}, u32[]{:S(2)}) %all-to-all-start.1) | async-done | bytes 589856 | tf_op jit(solution)/shard_map/all_to_all | solution.py:453
  58.5 0.5 positive_kernel.1
  59.1 0.7 %logits_kernel.1 = (bf16[256,512]{1,0:T(8,128)(2,1)S(1)}, bf16[512,768]{1,0:T(8,128)(2,1)S(1)}, f32[8,256]{1,0:T(8,128)S(1)}) custom-call(f32[8,256]{1,0:T(8,128)S(1)} %get-tuple-element.53.after_ref.part_ref, bf16[256,384]{1,0:T(8,128)(2,1)S(1)} %get-tuple-element.51.query_ref.mine_ref, bf16[256,384]{1,0:T(8,128)(2,1)S(1)} %copy-done.1, ...), custom_call_target="tpu_custom_call" | custom-call | flops 201326592 | bytes 2244608 | tf_op jit(solution)/shard_map/logits_kernel/pallas_call | solution.py:21
  59.8 0.4 pull_kernel.1
  60.2 0.1 collective-permute-start.9
  60.3 0.5 collective-permute-start.2
  60.8 0.1 collective-permute-start.8
  60.8 1.1 %collective-permute-done.2.far_ref = f32[8,256]{1,0:T(8,128)S(1)} collective-permute-done((f32[8,256]{1,0:T(8,128)S(1)}, f32[8,256]{1,0:T(8,128)S(1)}, u32[]{:S(2)}, u32[]{:S(2)}) %collective-permute-start.2) | collective-permute-done | bytes 8224 | tf_op jit(solution)/shard_map/ppermute | solution.py:376
  62.0 0.0 collective-permute-done.8.there_ref
  62.0 0.7 %factor_kernel.1 = (f32[1,256]{1,0:T(1,128)S(1)}, f32[256,128]{1,0:T(8,128)S(1)}) custom-call(s32[2]{0:T(128)S(1)} %pad_add_fusion.self_ref, f32[8,256]{1,0:T(8,128)S(1)} %get-tuple-element.53.after_ref.part_ref, f32[8,256]{1,0:T(8,128)S(1)} %collective-permute-done.2.far_ref, f32[8,256]{1,0:T(8,128)S(1)} %get-tuple-element.56.here_ref, ...), custom_call_target="tpu_custom_call" | custom-call | bytes 164872 | tf_op jit(solution)/shard_map/factor_kernel/pallas_call | solution.py:21
  62.7 0.9 %final_kernel.1 = (f32[256,384]{1,0:T(8,128)}, f32[1,256]{1,0:T(1,128)}) custom-call(f32[256,128]{1,0:T(8,128)S(1)} %get-tuple-element.57.factor_ref, bf16[256,384]{1,0:T(8,128)(2,1)S(1)} %get-tuple-element.58.rows_ref, f32[256,384]{1,0:T(8,128)S(1)} %get-tuple-element.61.keep_ref, f32[256,384]{1,0:T(8,128)S(1)} %collective-permute-done.9.sent_ref, ...), custom_call_target="tpu_custom_call" | custom-call | bytes 1509376 | tf_op jit(solution)/shard_map/final_kernel/pallas_call | solution.py:21
  (25 shorter events, 0.1 us)
Async XLA Ops:
  0.6 10.5 %copy-start.2 = (bf16[256,384]{1,0:T(8,128)(2,1)S(1)}, bf16[256,384]{1,0:T(8,128)(2,1)}, u32[]{:S(2)}) copy-start(bf16[256,384]{1,0:T(8,128)(2,1)} %query_ref.1) | copy-start | bytes 589828
  0.6 10.6 %copy-start.8 = (s32[1024]{0:T(1024)S(1)}, s32[1024]{0:T(1024)}, u32[]{:S(2)}) copy-start(s32[1024]{0:T(1024)} %param.11) | copy-start | bytes 12292
  0.7 10.7 %copy-start.4 = (f32[1024]{0:T(1024)S(1)}, f32[1024]{0:T(1024)}, u32[]{:S(2)}) copy-start(f32[1024]{0:T(1024)} %param.10) | copy-start | bytes 12292
  2.8 25.2 %all-to-all-start = ((bf16[16,152,128]{2,1,0:T(8,128)(2,1)}), bf16[16,152,128]{2,1,0:T(8,128)(2,1)S(1)}, u32[]{:S(2)}, u32[]{:S(2)}) async-start(bf16[16,152,128]{2,1,0:T(8,128)(2,1)} %bitcast.16), calls=%async_computation | async-start | bytes 1245184 | tf_op jit(solution)/shard_map/all_to_all | solution.py:411
  11.1 3.1 %collective-permute-start = (bf16[256,384]{1,0:T(8,128)(2,1)S(1)}, bf16[256,384]{1,0:T(8,128)(2,1)S(1)}, u32[]{:S(2)}, u32[]{:S(2)}) collective-permute-start(bf16[256,384]{1,0:T(8,128)(2,1)S(1)} %copy-done.2), channel_id=1, source_target_pairs={{0,1},{1,0},{2,3},{3,2},{4,5},{5,4},{6,7},{7,6},{8,9},{9,8},{10,11... | collective-permute-start | bytes 589832 | tf_op jit(solution)/shard_map/ppermute | solution.py:376
  14.3 13.7 %copy-start = (bf16[256,384]{1,0:T(8,128)(2,1)}, bf16[256,384]{1,0:T(8,128)(2,1)S(1)}, u32[]{:S(2)}) copy-start(bf16[256,384]{1,0:T(8,128)(2,1)S(1)} %collective-permute-done.after_ref.other_ref) | copy-start | bytes 589828
  28.0 3.2 %copy-start.5 = (s32[256]{0:T(256)S(1)}, s32[256]{0:T(256)}, u32[]{:S(2)}) copy-start(s32[256]{0:T(256)} %param.7) | copy-start | bytes 3076
  31.1 5.2 %copy-start.6 = (bf16[768,512]{1,0:T(8,128)(2,1)}, bf16[768,512]{1,0:T(8,128)(2,1)S(1)}, u32[]{:S(2)}) copy-start(bf16[768,512]{1,0:T(8,128)(2,1)S(1)} %get-tuple-element.47.got_ref) | copy-start | bytes 2359300
  31.1 1.4 %collective-permute-start.1 = (f32[72,384]{1,0:T(8,128)S(1)}, f32[72,384]{1,0:T(8,128)S(1)}, u32[]{:S(2)}, u32[]{:S(2)}) collective-permute-start(f32[72,384]{1,0:T(8,128)S(1)} %get-tuple-element.42.pack_ref), channel_id=1, source_target_pairs={{0,1},{1,0},{2,3},{3,2},{4,5},{5,4},{6,7},{7,6},{8,9},{9,8},{10,11... | collective-permute-start | bytes 331784 | tf_op jit(solution)/shard_map/ppermute | solution.py:376
  34.7 7.8 %collective-permute-start.3 = (bf16[64,768]{1,0:T(8,128)(2,1)}, bf16[64,768]{1,0:T(8,128)(2,1)S(1)}, u32[]{:S(2)}, u32[]{:S(2)}) collective-permute-start(bf16[64,768]{1,0:T(8,128)(2,1)} %get-tuple-element.55), channel_id=1, source_target_pairs={{0,8},{1,17},{2,10},{3,19},{4,12},{5,21},{6,14},{7,23},{8,0},{9,25... | collective-permute-start | bytes 294920 | tf_op jit(solution)/shard_map/ppermute | solution.py:384
  36.3 8.5 %copy-start.7 = (bf16[768,512]{1,0:T(8,128)(2,1)S(1)}, bf16[768,512]{1,0:T(8,128)(2,1)}, u32[]{:S(2)}) copy-start(bf16[768,512]{1,0:T(8,128)(2,1)} %copy-done.6) | copy-start | bytes 2359300
  36.3 6.2 %collective-permute-start.4 = (bf16[32,768]{1,0:T(8,128)(2,1)}, bf16[32,768]{1,0:T(8,128)(2,1)S(1)}, u32[]{:S(2)}, u32[]{:S(2)}) collective-permute-start(bf16[32,768]{1,0:T(8,128)(2,1)} %get-tuple-element.54.refs_0_), channel_id=1, source_target_pairs={{0,24},{2,26},{4,28},{6,30},{8,16},{10,18},{12,20},{14,22},{16,8},... | collective-permute-start | bytes 147464 | tf_op jit(solution)/shard_map/ppermute | solution.py:380
  37.3 21.2 %all-to-all-start.1 = ((bf16[16,48,384]{2,1,0:T(8,128)(2,1)}), bf16[16,48,384]{2,1,0:T(8,128)(2,1)S(1)}, u32[]{:S(2)}, u32[]{:S(2)}) async-start(bf16[16,48,384]{2,1,0:T(8,128)(2,1)} %bitcast.17), calls=%async_computation.1 | async-start | bytes 1179648 | tf_op jit(solution)/shard_map/all_to_all | solution.py:453
  42.5 0.8 %copy-start.3 = (bf16[32,768]{1,0:T(8,128)(2,1)S(1)}, bf16[32,768]{1,0:T(8,128)(2,1)}, u32[]{:S(2)}) copy-start(bf16[32,768]{1,0:T(8,128)(2,1)} %get-tuple-element.54.refs_0_) | copy-start | bytes 147460
  43.3 7.7 %collective-permute-start.5 = (bf16[128,768]{1,0:T(8,128)(2,1)S(1)}, bf16[128,768]{1,0:T(8,128)(2,1)S(1)}, u32[]{:S(2)}, u32[]{:S(2)}) collective-permute-start(bf16[128,768]{1,0:T(8,128)(2,1)S(1)} %join_kernel.1.refs_0_), channel_id=1, source_target_pairs={{0,2},{1,5},{2,0},{3,7},{4,6},{5,1},{6,4},{7,3},{8,10},{9,13},{10,... | collective-permute-start | bytes 589832 | tf_op jit(solution)/shard_map/ppermute | solution.py:384
  44.8 14.3 %copy-start.1 = (bf16[256,384]{1,0:T(8,128)(2,1)S(1)}, bf16[256,384]{1,0:T(8,128)(2,1)}, u32[]{:S(2)}) copy-start(bf16[256,384]{1,0:T(8,128)(2,1)} %copy-done) | copy-start | bytes 589828
  49.5 9.6 %collective-permute-start.6 = (bf16[128,768]{1,0:T(8,128)(2,1)S(1)}, bf16[128,768]{1,0:T(8,128)(2,1)S(1)}, u32[]{:S(2)}, u32[]{:S(2)}) collective-permute-start(bf16[128,768]{1,0:T(8,128)(2,1)S(1)} %join_kernel.1.refs_0_), channel_id=1, source_target_pairs={{0,4},{1,3},{2,6},{3,1},{4,0},{5,7},{6,2},{7,5},{8,12},{9,11},{10,... | collective-permute-start | bytes 589832 | tf_op jit(solution)/shard_map/ppermute | solution.py:384
  51.0 8.1 %collective-permute-start.7 = (bf16[128,768]{1,0:T(8,128)(2,1)S(1)}, bf16[128,768]{1,0:T(8,128)(2,1)S(1)}, u32[]{:S(2)}, u32[]{:S(2)}) collective-permute-start(bf16[128,768]{1,0:T(8,128)(2,1)S(1)} %again_kernel.1.refs_1_), channel_id=1, source_target_pairs={{0,4},{1,3},{2,6},{3,1},{4,0},{5,7},{6,2},{7,5},{8,12},{9,11},{10,... | collective-permute-start | bytes 589832 | tf_op jit(solution)/shard_map/ppermute | solution.py:384
  60.2 2.5 %collective-permute-start.9 = (f32[256,384]{1,0:T(8,128)S(1)}, f32[256,384]{1,0:T(8,128)S(1)}, u32[]{:S(2)}, u32[]{:S(2)}) collective-permute-start(f32[256,384]{1,0:T(8,128)S(1)} %get-tuple-element.62), channel_id=1, source_target_pairs={{0,1},{1,0},{2,3},{3,2},{4,5},{5,4},{6,7},{7,6},{8,9},{9,8},{10,11... | collective-permute-start | bytes 1179656 | tf_op jit(solution)/shard_map/ppermute | solution.py:376
  60.3 1.7 %collective-permute-start.2 = (f32[8,256]{1,0:T(8,128)S(1)}, f32[8,256]{1,0:T(8,128)S(1)}, u32[]{:S(2)}, u32[]{:S(2)}) collective-permute-start(f32[8,256]{1,0:T(8,128)S(1)} %get-tuple-element.53.after_ref.part_ref), channel_id=1, source_target_pairs={{0,1},{1,0},{2,3},{3,2},{4,5},{5,4},{6,7},{7,6},{8,9},{9,8},{10,11... | collective-permute-start | bytes 24584 | tf_op jit(solution)/shard_map/ppermute | solution.py:376
  60.8 1.2 %collective-permute-start.8 = (f32[8,256]{1,0:T(8,128)S(1)}, f32[8,256]{1,0:T(8,128)S(1)}, u32[]{:S(2)}, u32[]{:S(2)}) collective-permute-start(f32[8,256]{1,0:T(8,128)S(1)} %get-tuple-element.56.here_ref), channel_id=1, source_target_pairs={{0,1},{1,0},{2,3},{3,2},{4,5},{5,4},{6,7},{7,6},{8,9},{9,8},{10,11... | collective-permute-start | bytes 24584 | tf_op jit(solution)/shard_map/ppermute | solution.py:376

commit v5 on v4

--- a/solution.py
+++ b/solution.py
@@ -12,6 +12,8 @@
 I32 = jnp.int32
 LANES = 128
 VMEM = 24 * 2**20
+OUT = (7, 14, 5, 13, 8, 10, 15, 11, 0, 3, 9, 1, 2, 12, 6, 4)
+BACK = (4, 0, 5, 6, 8, 12, 2, 3, 1, 11, 9, 14, 15, 10, 13, 7)
 
 
 def call(kernel, outs, *args, flops=0, smem=(), hbm=(), out_hbm=(), free=(), out_free=(), scratch=()):
@@ -77,9 +79,22 @@
     return mine, jnp.sum(jnp.where(mine, running, 0.0), axis=0, keepdims=True) - 1.0
 
 
-def slot_of(mine, rank, stride):
-    owner = jnp.sum(jnp.where(mine, iota(mine.shape, 0).astype(F32), 0.0), axis=0, keepdims=True)
-    return (owner * stride + rank).astype(I32)
+def order_of(owners, order):
+    return order if owners == len(order) else tuple(range(owners))
+
+
+def slot_of(mine, rank, stride, order):
+    owners = mine.shape[0]
+    owner = place = iota(mine.shape, 0)
+    for k, device in enumerate(order_of(owners, order)):
+        place = jnp.where(owner == device, k, place) if k != device else place
+    place = jnp.sum(jnp.where(mine, place.astype(F32), 0.0), axis=0, keepdims=True)
+    return (place * stride + rank).astype(I32)
+
+
+def exchange(value, order):
+    groups = [list(order_of(lax.axis_size("dp"), order))]
+    return lax.all_to_all(value, "dp", split_axis=0, concat_axis=0, axis_index_groups=groups)
 
 
 def pack_kernel(owners, owned, stride, label_ref, feat_ref, send_ref, label_buf, feat_buf, send_buf, sems):
@@ -93,7 +108,7 @@
     labels.wait()
     label = label_buf[...]
     mine, rank = ranks_of(label, owners, owned, before)
-    slot = slot_of(mine, rank, stride)
+    slot = slot_of(mine, rank, stride, OUT)
     value = jnp.where(mine, (label - iota((owners, rows), 0) * owned + 1).astype(F32), 0.0)
     high = jnp.floor(value * (1.0 / 32.0))
     value = jnp.concatenate([high, value - 32.0 * high], axis=0).astype(BF16)
@@ -111,7 +126,8 @@
             for j in range(width // LANES):
                 piece = picked[c * stride : (c + 1) * stride, j * LANES : (j + 1) * LANES]
                 send_buf[b * block + j * stride : b * block + (j + 1) * stride, :] = piece
-            tail = jnp.where(row == 0, ids[b : b + 1], jnp.where(row == 1, ids[owners + b : owners + b + 1], 0.0))
+            o = order_of(owners, OUT)[b]
+            tail = jnp.where(row == 0, ids[o : o + 1], jnp.where(row == 1, ids[owners + o : owners + o + 1], 0.0))
             send_buf[(b + 1) * block - 8 : (b + 1) * block, :] = tail.astype(BF16)
         at = slice(k * part * block, (k + 1) * part * block)
         copies.append(pltpu.make_async_copy(send_buf.at[at, :], send_ref.at[at, :], sems.at[2 + k]))
@@ -163,11 +179,12 @@
     keep = slots // owners
     block = got_ref.shape[0] // owners
     for b in range(owners):
-        sent = got_ref[(b + 1) * block - 8 : (b + 1) * block, :].astype(F32)
+        c = order_of(owners, OUT).index(order_of(owners, BACK)[b])
+        sent = got_ref[(c + 1) * block - 8 : (c + 1) * block, :].astype(F32)
         table[b : b + 1, :] = sent[0:1]
         table[owners + b : owners + b + 1, :] = sent[1:2]
         for j in range(width // LANES):
-            at = b * block + j * keep
+            at = c * block + j * keep
             rows_ref[b * keep : (b + 1) * keep, j * LANES : (j + 1) * LANES] = got_ref[at : at + keep, :]
     rows_ref[:, width:] = jnp.ones((slots, LANES), BF16)
     wide = nn(table[...].astype(BF16), spread_ref[...])
@@ -206,14 +223,14 @@
 
 def prepare_kernel(owners, owned, capacity, count_ref, label_ref, query_ref, weight_ref, slot_ref, copy_ref):
     weight_ref[...] = weight_of(count_ref[...])
-    slot = slot_of(*ranks_of(label_ref[...], owners, owned, ahead(label_ref.shape[1])), capacity)
+    slot = slot_of(*ranks_of(label_ref[...], owners, owned, ahead(label_ref.shape[1])), capacity, BACK)
     slot_ref[...] = to_col(slot.astype(F32)).astype(I32)
     copy_ref[...] = query_ref[...]
 
 
 def scale_kernel(
     capacity, self_ref, ids_ref, neg_ref, count_ref, old_ref, pack_ref, new_ref, weight_ref, other_ref,
-    full_ref, own_ref, dist_ref, out_ref, full_buf, own_buf, buf, sems,
+    full_ref, own_ref, dist_ref, out_ref, own_buf, full_buf, buf, sems,
 ):
     slots, width = new_ref.shape
     negs = neg_ref.shape[0]
@@ -325,11 +342,12 @@
     stats_ref[...] = stats[0:8, :]
 
 
-def pull_kernel(weight_ref, negs_ref, keep_ref, send_ref):
-    width = keep_ref.shape[1]
-    grad = nn(weight_ref[...], negs_ref[...])
-    send_ref[...] = grad[:, width:]
-    keep_ref[...] = grad[:, 0:width]
+def pull_kernel(weight_ref, negs_ref, far_ref):
+    far_ref[...] = nn(weight_ref[...], negs_ref[:, far_ref.shape[1] :])
+
+
+def near_kernel(after_ref, weight_ref, negs_ref, near_ref):
+    near_ref[...] = nn(weight_ref[...], negs_ref[:, 0 : near_ref.shape[1]])
 
 
 def positive_kernel(slot_ref, query_ref, back_ref, rows_ref, part_ref):
@@ -408,7 +426,7 @@
         scratch=[*loads, pltpu.VMEM((count * block, LANES), BF16), pltpu.SemaphoreType.DMA((6,))],
     )
     query_far = swap(queries)
-    got = lax.all_to_all(send.reshape(count, block, LANES), "dp", split_axis=0, concat_axis=0)
+    got = exchange(send.reshape(count, block, LANES), OUT)
     got = got.reshape(count * block, LANES)
 
     neg_col, old_col, held, parts, spread = call(
@@ -435,22 +453,22 @@
         (shape((slots, LANES), F32), shape((rows, LANES), I32), shape((rows, width), BF16)),
         counts, label_row, queries, free=(1, 2),
     )
-    full, own, dist, scaled = call(
+    full, own, dist, scaled, own_near = call(
         functools.partial(scale_kernel, capacity),
         (
             shape((negs, 2 * width), BF16), shape((half, 2 * width), BF16), shape((1, slots), F32),
-            shape((count * capacity, width), BF16),
+            shape((count * capacity, width), BF16), shape((half, 2 * width), BF16),
         ),
         place, ids, neg_col, neg_counts, old_col, pack, new, weights, swap(pack), smem=(0,), out_hbm=(0, 1, 3),
         scratch=[
-            pltpu.VMEM((negs, 2 * width), BF16), pltpu.VMEM((half, 2 * width), BF16),
-            pltpu.VMEM((count * capacity, width), BF16), pltpu.SemaphoreType.DMA((4,)),
+            pltpu.VMEM((negs, 2 * width), BF16), pltpu.VMEM((count * capacity, width), BF16),
+            pltpu.SemaphoreType.DMA((4,)),
         ],
     )
     step = count // 4
-    line = [own, two_hop(full, count, (step, 2 * step)), hop(own, count, 3 * step)]
+    line = [own_near, two_hop(full, count, (step, 2 * step)), hop(own, count, 3 * step)]
     (joined,) = call(join_kernel, (shape((sum(p.shape[0] for p in line), 2 * width), BF16),), *line)
-    back = lax.all_to_all(scaled.reshape(count, capacity, width), "dp", split_axis=0, concat_axis=0)
+    back = exchange(scaled.reshape(count, capacity, width), BACK)
     new_bank, new_conc = owner_call(ids, dist, got, bank, old_conc.reshape(1, owned))
     if step == 4:
         first = two_hop(joined, count, (1, 2))
@@ -474,11 +492,9 @@
         part, query, query_far, *pieces, flops=4 * rows * half * count * width, free=range(2, 99),
     )
     far_stats = swap(stats)
-    keep, sent = call(
-        pull_kernel,
-        (shape((rows, width), F32), shape((rows, width), F32)),
-        weight, all_negs, flops=4 * rows * half * count * width,
-    )
+    flops = 2 * rows * half * count * width
+    (sent,) = call(pull_kernel, (shape((rows, width), F32),), weight, all_negs, flops=flops)
+    (keep,) = call(near_kernel, (shape((rows, width), F32),), sent, weight, all_negs, flops=flops)
     sent = swap(sent)
     loss, factors = call(
         factor_kernel,

time: 64.1 us -> 60.5 us (0.944)
  waiting for transfers between devices: 23 us -> 16.8 us
  starting transfers between devices: 20.2 us -> 23.4 us
  local copies, waits for them, and re-layouts: 0.91 us -> 0.11 us
    all_to_all x2, waiting for transfers between devices: 20.4 us -> 13.6 us  [exchange(): lax.all_to_all(value, 'dp', split_axis=0, concat_axis=0, axis_index_group...]
    ppermute x4, starting transfers between devices: 5.47 us -> 7.29 us  [two_hop(): lax.ppermute(value, ('dp', 'mp'), [(2 * k + c, 2 * (k ^ bits[c]) + c) for...]
    ppermute x4, waiting for transfers between devices: 0.01 us -> 1.32 us  [two_hop(): lax.ppermute(value, ('dp', 'mp'), [(2 * k + c, 2 * (k ^ bits[c]) + c) for...]
    all_to_all x2, starting transfers between devices: 13 us -> 13.9 us  [exchange(): lax.all_to_all(value, 'dp', split_axis=0, concat_axis=0, axis_index_group...]
    unnamed x18 -> x16, local copies, waits for them, and re-layouts: 0.84 us -> 0.04 us
    pallas_call x12 -> x13, Pallas kernels: 13.9 us -> 14.1 us  [call(): pl.pallas_call(kernel, out_shape=[o if k in out_free else space(o.shape,...]
  transfers between devices with their start and end apart: 12 -> 12, of which waited for: 5 -> 5; matrix products, arithmetic and copies ran while one was open for 0% -> 0% of each run, Pallas kernels for 14% -> 16%
where the time goes in v5:
time: 60.5 us; the launch traced here: 60.1 us
  starting transfers between devices  23.4 us (39%)
  Pallas kernels  18.8 us (31%)
  waiting for transfers between devices  16.8 us (28%)
  between operations  0.82 us (1%)
    pallas_call x13, Pallas kernels, call(): pl.pallas_call(kernel, out_shape=[o if k in out_free else space(o.shape,...  14.1 us
    all_to_all x2, starting transfers between devices, exchange(): lax.all_to_all(value, 'dp', split_axis=0, concat_axis=0, axis_index_group...  13.9 us
    all_to_all x2, waiting for transfers between devices, exchange(): lax.all_to_all(value, 'dp', split_axis=0, concat_axis=0, axis_index_group...  13.6 us
    ppermute x4, starting transfers between devices, two_hop(): lax.ppermute(value, ('dp', 'mp'), [(2 * k + c, 2 * (k ^ bits[c]) + c) for...  7.29 us
    pallas_call x1, Pallas kernels, owner_call(): pl.pallas_call(owner_kernel, grid=(owned // block,), in_specs=[pl.BlockSp...  4.72 us
    ppermute x5, waiting for transfers between devices, swap(): return lax.ppermute(value, 'mp', [(0, 1), (1, 0)])  1.82 us
    ppermute x1, starting transfers between devices, hop(): return lax.ppermute(value, 'dp', [(k, k ^ bits) for k in range(count)])  1.46 us
    ppermute x4, waiting for transfers between devices, two_hop(): lax.ppermute(value, ('dp', 'mp'), [(2 * k + c, 2 * (k ^ bits[c]) + c) for...  1.32 us
  transfers between devices with their start and end apart: 12, of which 5 were waited for; matrix products, arithmetic and copies ran while one was open for 0% of the time, Pallas kernels for 16%

profile of v5, /device:TPU:0, one launch (start us, length us, event | category | flops | bytes accessed | tf_op | source)
XLA Modules:
  0.0 60.1 jit_solution(10309153828739093637)
XLA Ops:
  0.7 2.1 %pack_kernel.1 = bf16[2432,128]{1,0:T(8,128)(2,1)} custom-call(s32[1,256]{1,0:T(1,128)} %bitcast.14, bf16[256,384]{1,0:T(8,128)(2,1)} %feat_ref.1), custom_call_target="tpu_custom_call" | custom-call | flops 150994944 | bytes 820224 | tf_op jit(solution)/shard_map/pack_kernel/pallas_call | solution.py:23
  2.8 8.8 %all-to-all-start = ((bf16[16,152,128]{2,1,0:T(8,128)(2,1)}), bf16[16,152,128]{2,1,0:T(8,128)(2,1)S(1)}, u32[]{:S(2)}, u32[]{:S(2)}) async-start(bf16[16,152,128]{2,1,0:T(8,128)(2,1)} %bitcast.16), calls=%async_computation | async-start | bytes 1245184 | tf_op jit(solution)/shard_map/all_to_all | solution.py:97
  11.6 0.1 collective-permute-start
  11.7 0.1 reshape.36.neg_ref
  11.8 0.1 pad_add_fusion.self_ref
  11.8 2.9 %split_kernel.1 = (s32[64,128]{1,0:T(8,128)S(1)}, f32[64,128]{1,0:T(8,128)S(1)}, f32[64,384]{1,0:T(8,128)S(1)}, bf16[1024,768]{1,0:T(8,128)(2,1)S(1)}, bf16[128,768]{1,0:T(8,128)(2,1)S(1)}) custom-call(s32[2]{0:T(128)S(1)} %pad_add_fusion.self_ref, s32[16,64]{1,0:T(8,128)S(1)} %reshape.36.neg_ref, f32[1,1024]{1,0:T(1,128)S(1)} %bitcast.13, f32[1024,384]{1,0:T(8,128)} %bank_ref.3), custom_call_target="tpu_custom_call" | custom-call | bytes 3514376 | tf_op jit(solution)/shard_map/split_kernel/pallas_call | solution.py:23
  14.7 10.2 %all-to-all-done = bf16[16,152,128]{2,1,0:T(8,128)(2,1)S(1)} async-done(((bf16[16,152,128]{2,1,0:T(8,128)(2,1)}), bf16[16,152,128]{2,1,0:T(8,128)(2,1)S(1)}, u32[]{:S(2)}, u32[]{:S(2)}) %all-to-all-start) | async-done | bytes 622624 | tf_op jit(solution)/shard_map/all_to_all | solution.py:97
  24.9 3.2 %mean_kernel.1 = (s32[1,768]{1,0:T(1,128)S(1)}, f32[768,384]{1,0:T(8,128)S(1)}, f32[72,384]{1,0:T(8,128)S(1)}, bf16[768,512]{1,0:T(8,128)(2,1)S(1)}, f32[768,128]{1,0:T(8,128)S(1)}, /*index=5*/f32[64,128]{1,0:T(8,128)S(1)}) custom-call(bf16[256,384]{1,0:T(8,128)(2,1)} %copy-done, s32[64,128]{1,0:T(8,128)S(1)} %get-tuple-element.34.neg_ref, ...), custom_call_target="tpu_custom_call" | custom-call | flops 2415919104 | bytes 5225472 | tf_op jit(solution)/shard_map/mean_kernel/pallas_call | solution.py:23
  28.1 0.1 collective-permute-start.1
  28.1 0.3 prepare_kernel.1
  28.5 1.0 %collective-permute-done.1.other_ref = f32[72,384]{1,0:T(8,128)S(1)} collective-permute-done((f32[72,384]{1,0:T(8,128)S(1)}, f32[72,384]{1,0:T(8,128)S(1)}, u32[]{:S(2)}, u32[]{:S(2)}) %collective-permute-start.1) | collective-permute-done | bytes 110624 | tf_op jit(solution)/shard_map/ppermute | solution.py:394
  29.4 2.1 %scale_kernel.1 = (bf16[64,768]{1,0:T(8,128)(2,1)}, bf16[32,768]{1,0:T(8,128)(2,1)}, f32[1,768]{1,0:T(1,128)S(1)}, bf16[768,384]{1,0:T(8,128)(2,1)}, bf16[32,768]{1,0:T(8,128)(2,1)S(1)}) custom-call(s32[2]{0:T(128)S(1)} %pad_add_fusion.self_ref, s32[1,768]{1,0:T(1,128)S(1)} %get-tuple-element.38.ids_ref, s32[64,128]{1,0:T(8,128)S(1)} %get-tuple-element.34.neg_ref, ...), custom_call_target="tpu_custom_call" | custom-call | bytes 2684936 | tf_op jit(solution)/shard_map/scale_kernel/pallas_call | solution.py:23
  31.6 2.5 %collective-permute-start.3 = (bf16[64,768]{1,0:T(8,128)(2,1)}, bf16[64,768]{1,0:T(8,128)(2,1)S(1)}, u32[]{:S(2)}, u32[]{:S(2)}) collective-permute-start(bf16[64,768]{1,0:T(8,128)(2,1)} %get-tuple-element.54), channel_id=1, source_target_pairs={{0,8},{1,17},{2,10},{3,19},{4,12},{5,21},{6,14},{7,23},{8,0},{9,25... | collective-permute-start | bytes 294920 | tf_op jit(solution)/shard_map/ppermute | solution.py:402
  34.0 1.5 %collective-permute-start.4 = (bf16[32,768]{1,0:T(8,128)(2,1)}, bf16[32,768]{1,0:T(8,128)(2,1)S(1)}, u32[]{:S(2)}, u32[]{:S(2)}) collective-permute-start(bf16[32,768]{1,0:T(8,128)(2,1)} %get-tuple-element.55), channel_id=1, source_target_pairs={{0,24},{2,26},{4,28},{6,30},{8,16},{10,18},{12,20},{14,22},{16,8},... | collective-permute-start | bytes 147464 | tf_op jit(solution)/shard_map/ppermute | solution.py:398
  35.5 5.1 %all-to-all-start.1 = ((bf16[16,48,384]{2,1,0:T(8,128)(2,1)}), bf16[16,48,384]{2,1,0:T(8,128)(2,1)S(1)}, u32[]{:S(2)}, u32[]{:S(2)}) async-start(bf16[16,48,384]{2,1,0:T(8,128)(2,1)} %bitcast.17), calls=%async_computation.1 | async-start | bytes 1179648 | tf_op jit(solution)/shard_map/all_to_all | solution.py:97
  40.6 1.5 %collective-permute-start.5 = (bf16[128,768]{1,0:T(8,128)(2,1)S(1)}, bf16[128,768]{1,0:T(8,128)(2,1)S(1)}, u32[]{:S(2)}, u32[]{:S(2)}) collective-permute-start(bf16[128,768]{1,0:T(8,128)(2,1)S(1)} %join_kernel.1.refs_0_), channel_id=1, source_target_pairs={{0,2},{1,5},{2,0},{3,7},{4,6},{5,1},{6,4},{7,3},{8,10},{9,13},{10,... | collective-permute-start | bytes 589832 | tf_op jit(solution)/shard_map/ppermute | solution.py:402
  42.2 4.7 %owner_kernel.1 = (f32[1024,384]{1,0:T(8,128)}, f32[1,1024]{1,0:T(1,128)}) custom-call(s32[1,768]{1,0:T(1,128)S(1)} %get-tuple-element.38.ids_ref, f32[1,768]{1,0:T(1,128)S(1)} %get-tuple-element.45.dist_ref, bf16[768,512]{1,0:T(8,128)(2,1)S(1)} %copy-done.6, f32[1024,384]{1,0:T(8,128)} %bank_ref.3, f32[1,1024]{1,0:T(1,128)} %bitcast.12), custom_call_target="tpu_custom_call" | custom-call | flops 20000000000 | bytes 3145728 | tf_op jit(solution)/shard_map/owner_kernel/pallas_call | solution.py:310
  46.9 1.5 %collective-permute-start.6 = (bf16[128,768]{1,0:T(8,128)(2,1)S(1)}, bf16[128,768]{1,0:T(8,128)(2,1)S(1)}, u32[]{:S(2)}, u32[]{:S(2)}) collective-permute-start(bf16[128,768]{1,0:T(8,128)(2,1)S(1)} %join_kernel.1.refs_0_), channel_id=1, source_target_pairs={{0,4},{1,3},{2,6},{3,1},{4,0},{5,7},{6,2},{7,5},{8,12},{9,11},{10,... | collective-permute-start | bytes 589832 | tf_op jit(solution)/shard_map/ppermute | solution.py:402
  48.4 1.3 %collective-permute-done.5.value_ref = bf16[128,768]{1,0:T(8,128)(2,1)S(1)} collective-permute-done((bf16[128,768]{1,0:T(8,128)(2,1)S(1)}, bf16[128,768]{1,0:T(8,128)(2,1)S(1)}, u32[]{:S(2)}, u32[]{:S(2)}) %collective-permute-start.5) | collective-permute-done | bytes 196640 | tf_op jit(solution)/shard_map/ppermute | solution.py:402
  49.7 1.8 %collective-permute-start.7 = (bf16[128,768]{1,0:T(8,128)(2,1)S(1)}, bf16[128,768]{1,0:T(8,128)(2,1)S(1)}, u32[]{:S(2)}, u32[]{:S(2)}) collective-permute-start(bf16[128,768]{1,0:T(8,128)(2,1)S(1)} %again_kernel.1.refs_1_), channel_id=1, source_target_pairs={{0,4},{1,3},{2,6},{3,1},{4,0},{5,7},{6,2},{7,5},{8,12},{9,11},{10,... | collective-permute-start | bytes 589832 | tf_op jit(solution)/shard_map/ppermute | solution.py:402
  51.5 3.5 %all-to-all-done.1 = bf16[16,48,384]{2,1,0:T(8,128)(2,1)S(1)} async-done(((bf16[16,48,384]{2,1,0:T(8,128)(2,1)}), bf16[16,48,384]{2,1,0:T(8,128)(2,1)S(1)}, u32[]{:S(2)}, u32[]{:S(2)}) %all-to-all-start.1) | async-done | bytes 589856 | tf_op jit(solution)/shard_map/all_to_all | solution.py:97
  55.0 0.5 positive_kernel.1
  55.6 0.7 %logits_kernel.1 = (bf16[256,512]{1,0:T(8,128)(2,1)S(1)}, bf16[512,768]{1,0:T(8,128)(2,1)S(1)}, f32[8,256]{1,0:T(8,128)S(1)}) custom-call(f32[8,256]{1,0:T(8,128)S(1)} %get-tuple-element.52.after_ref.part_ref, bf16[256,384]{1,0:T(8,128)(2,1)S(1)} %get-tuple-element.50.query_ref.mine_ref, bf16[256,384]{1,0:T(8,128)(2,1)S(1)} %copy-done.1, ...), custom_call_target="tpu_custom_call" | custom-call | flops 201326592 | bytes 2244608 | tf_op jit(solution)/shard_map/logits_kernel/pallas_call | solution.py:23
  56.3 0.3 pull_kernel.1.after_ref
  56.6 0.1 collective-permute-start.9
  56.7 0.5 collective-permute-start.2
  57.2 0.1 collective-permute-start.8
  57.2 0.3 near_kernel.1.keep_ref
  57.5 0.8 %collective-permute-done.2.far_ref = f32[8,256]{1,0:T(8,128)S(1)} collective-permute-done((f32[8,256]{1,0:T(8,128)S(1)}, f32[8,256]{1,0:T(8,128)S(1)}, u32[]{:S(2)}, u32[]{:S(2)}) %collective-permute-start.2) | collective-permute-done | bytes 8224 | tf_op jit(solution)/shard_map/ppermute | solution.py:394
  58.4 0.0 collective-permute-done.8.there_ref
  58.4 0.7 %factor_kernel.1 = (f32[1,256]{1,0:T(1,128)S(1)}, f32[256,128]{1,0:T(8,128)S(1)}) custom-call(s32[2]{0:T(128)S(1)} %pad_add_fusion.self_ref, f32[8,256]{1,0:T(8,128)S(1)} %get-tuple-element.52.after_ref.part_ref, f32[8,256]{1,0:T(8,128)S(1)} %collective-permute-done.2.far_ref, f32[8,256]{1,0:T(8,128)S(1)} %get-tuple-element.56.here_ref, ...), custom_call_target="tpu_custom_call" | custom-call | bytes 164872 | tf_op jit(solution)/shard_map/factor_kernel/pallas_call | solution.py:23
  59.1 0.9 %final_kernel.1 = (f32[256,384]{1,0:T(8,128)}, f32[1,256]{1,0:T(1,128)}) custom-call(f32[256,128]{1,0:T(8,128)S(1)} %get-tuple-element.57.factor_ref, bf16[256,384]{1,0:T(8,128)(2,1)S(1)} %get-tuple-element.58.rows_ref, f32[256,384]{1,0:T(8,128)S(1)} %near_kernel.1.keep_ref, f32[256,384]{1,0:T(8,128)S(1)} %collective-permute-done.9.sent_ref, ...), custom_call_target="tpu_custom_call" | custom-call | bytes 1509376 | tf_op jit(solution)/shard_map/final_kernel/pallas_call | solution.py:23
  (24 shorter events, 0.1 us)
Async XLA Ops:
  0.6 11.0 %copy-start.2 = (bf16[256,384]{1,0:T(8,128)(2,1)S(1)}, bf16[256,384]{1,0:T(8,128)(2,1)}, u32[]{:S(2)}) copy-start(bf16[256,384]{1,0:T(8,128)(2,1)} %query_ref.1) | copy-start | bytes 589828
  0.6 11.0 %copy-start.7 = (s32[1024]{0:T(1024)S(1)}, s32[1024]{0:T(1024)}, u32[]{:S(2)}) copy-start(s32[1024]{0:T(1024)} %param.11) | copy-start | bytes 12292
  0.7 11.2 %copy-start.3 = (f32[1024]{0:T(1024)S(1)}, f32[1024]{0:T(1024)}, u32[]{:S(2)}) copy-start(f32[1024]{0:T(1024)} %param.10) | copy-start | bytes 12292
  2.8 22.1 %all-to-all-start = ((bf16[16,152,128]{2,1,0:T(8,128)(2,1)}), bf16[16,152,128]{2,1,0:T(8,128)(2,1)S(1)}, u32[]{:S(2)}, u32[]{:S(2)}) async-start(bf16[16,152,128]{2,1,0:T(8,128)(2,1)} %bitcast.16), calls=%async_computation | async-start | bytes 1245184 | tf_op jit(solution)/shard_map/all_to_all | solution.py:97
  11.6 3.1 %collective-permute-start = (bf16[256,384]{1,0:T(8,128)(2,1)S(1)}, bf16[256,384]{1,0:T(8,128)(2,1)S(1)}, u32[]{:S(2)}, u32[]{:S(2)}) collective-permute-start(bf16[256,384]{1,0:T(8,128)(2,1)S(1)} %copy-done.2), channel_id=1, source_target_pairs={{0,1},{1,0},{2,3},{3,2},{4,5},{5,4},{6,7},{7,6},{8,9},{9,8},{10,11... | collective-permute-start | bytes 589832 | tf_op jit(solution)/shard_map/ppermute | solution.py:394
  14.7 10.2 %copy-start = (bf16[256,384]{1,0:T(8,128)(2,1)}, bf16[256,384]{1,0:T(8,128)(2,1)S(1)}, u32[]{:S(2)}) copy-start(bf16[256,384]{1,0:T(8,128)(2,1)S(1)} %collective-permute-done.after_ref.other_ref) | copy-start | bytes 589828
  24.9 3.2 %copy-start.4 = (s32[256]{0:T(256)S(1)}, s32[256]{0:T(256)}, u32[]{:S(2)}) copy-start(s32[256]{0:T(256)} %param.7) | copy-start | bytes 3076
  28.1 6.0 %copy-start.5 = (bf16[768,512]{1,0:T(8,128)(2,1)}, bf16[768,512]{1,0:T(8,128)(2,1)S(1)}, u32[]{:S(2)}) copy-start(bf16[768,512]{1,0:T(8,128)(2,1)S(1)} %get-tuple-element.46.got_ref) | copy-start | bytes 2359300
  28.1 1.4 %collective-permute-start.1 = (f32[72,384]{1,0:T(8,128)S(1)}, f32[72,384]{1,0:T(8,128)S(1)}, u32[]{:S(2)}, u32[]{:S(2)}) collective-permute-start(f32[72,384]{1,0:T(8,128)S(1)} %get-tuple-element.41.pack_ref), channel_id=1, source_target_pairs={{0,1},{1,0},{2,3},{3,2},{4,5},{5,4},{6,7},{7,6},{8,9},{9,8},{10,11... | collective-permute-start | bytes 331784 | tf_op jit(solution)/shard_map/ppermute | solution.py:394
  31.6 9.0 %collective-permute-start.3 = (bf16[64,768]{1,0:T(8,128)(2,1)}, bf16[64,768]{1,0:T(8,128)(2,1)S(1)}, u32[]{:S(2)}, u32[]{:S(2)}) collective-permute-start(bf16[64,768]{1,0:T(8,128)(2,1)} %get-tuple-element.54), channel_id=1, source_target_pairs={{0,8},{1,17},{2,10},{3,19},{4,12},{5,21},{6,14},{7,23},{8,0},{9,25... | collective-permute-start | bytes 294920 | tf_op jit(solution)/shard_map/ppermute | solution.py:402
  34.0 8.1 %copy-start.6 = (bf16[768,512]{1,0:T(8,128)(2,1)S(1)}, bf16[768,512]{1,0:T(8,128)(2,1)}, u32[]{:S(2)}) copy-start(bf16[768,512]{1,0:T(8,128)(2,1)} %copy-done.5) | copy-start | bytes 2359300
  34.0 6.6 %collective-permute-start.4 = (bf16[32,768]{1,0:T(8,128)(2,1)}, bf16[32,768]{1,0:T(8,128)(2,1)S(1)}, u32[]{:S(2)}, u32[]{:S(2)}) collective-permute-start(bf16[32,768]{1,0:T(8,128)(2,1)} %get-tuple-element.55), channel_id=1, source_target_pairs={{0,24},{2,26},{4,28},{6,30},{8,16},{10,18},{12,20},{14,22},{16,8},... | collective-permute-start | bytes 147464 | tf_op jit(solution)/shard_map/ppermute | solution.py:398
  35.5 19.5 %all-to-all-start.1 = ((bf16[16,48,384]{2,1,0:T(8,128)(2,1)}), bf16[16,48,384]{2,1,0:T(8,128)(2,1)S(1)}, u32[]{:S(2)}, u32[]{:S(2)}) async-start(bf16[16,48,384]{2,1,0:T(8,128)(2,1)} %bitcast.17), calls=%async_computation.1 | async-start | bytes 1179648 | tf_op jit(solution)/shard_map/all_to_all | solution.py:97
  40.6 9.0 %collective-permute-start.5 = (bf16[128,768]{1,0:T(8,128)(2,1)S(1)}, bf16[128,768]{1,0:T(8,128)(2,1)S(1)}, u32[]{:S(2)}, u32[]{:S(2)}) collective-permute-start(bf16[128,768]{1,0:T(8,128)(2,1)S(1)} %join_kernel.1.refs_0_), channel_id=1, source_target_pairs={{0,2},{1,5},{2,0},{3,7},{4,6},{5,1},{6,4},{7,3},{8,10},{9,13},{10,... | collective-permute-start | bytes 589832 | tf_op jit(solution)/shard_map/ppermute | solution.py:402
  42.2 13.4 %copy-start.1 = (bf16[256,384]{1,0:T(8,128)(2,1)S(1)}, bf16[256,384]{1,0:T(8,128)(2,1)}, u32[]{:S(2)}) copy-start(bf16[256,384]{1,0:T(8,128)(2,1)} %copy-done) | copy-start | bytes 589828
  46.9 8.7 %collective-permute-start.6 = (bf16[128,768]{1,0:T(8,128)(2,1)S(1)}, bf16[128,768]{1,0:T(8,128)(2,1)S(1)}, u32[]{:S(2)}, u32[]{:S(2)}) collective-permute-start(bf16[128,768]{1,0:T(8,128)(2,1)S(1)} %join_kernel.1.refs_0_), channel_id=1, source_target_pairs={{0,4},{1,3},{2,6},{3,1},{4,0},{5,7},{6,2},{7,5},{8,12},{9,11},{10,... | collective-permute-start | bytes 589832 | tf_op jit(solution)/shard_map/ppermute | solution.py:402
  49.7 5.9 %collective-permute-start.7 = (bf16[128,768]{1,0:T(8,128)(2,1)S(1)}, bf16[128,768]{1,0:T(8,128)(2,1)S(1)}, u32[]{:S(2)}, u32[]{:S(2)}) collective-permute-start(bf16[128,768]{1,0:T(8,128)(2,1)S(1)} %again_kernel.1.refs_1_), channel_id=1, source_target_pairs={{0,4},{1,3},{2,6},{3,1},{4,0},{5,7},{6,2},{7,5},{8,12},{9,11},{10,... | collective-permute-start | bytes 589832 | tf_op jit(solution)/shard_map/ppermute | solution.py:402
  56.6 2.5 %collective-permute-start.9 = (f32[256,384]{1,0:T(8,128)S(1)}, f32[256,384]{1,0:T(8,128)S(1)}, u32[]{:S(2)}, u32[]{:S(2)}) collective-permute-start(f32[256,384]{1,0:T(8,128)S(1)} %pull_kernel.1.after_ref), channel_id=1, source_target_pairs={{0,1},{1,0},{2,3},{3,2},{4,5},{5,4},{6,7},{7,6},{8,9},{9,8},{10,11... | collective-permute-start | bytes 1179656 | tf_op jit(solution)/shard_map/ppermute | solution.py:394
  56.7 1.7 %collective-permute-start.2 = (f32[8,256]{1,0:T(8,128)S(1)}, f32[8,256]{1,0:T(8,128)S(1)}, u32[]{:S(2)}, u32[]{:S(2)}) collective-permute-start(f32[8,256]{1,0:T(8,128)S(1)} %get-tuple-element.52.after_ref.part_ref), channel_id=1, source_target_pairs={{0,1},{1,0},{2,3},{3,2},{4,5},{5,4},{6,7},{7,6},{8,9},{9,8},{10,11... | collective-permute-start | bytes 24584 | tf_op jit(solution)/shard_map/ppermute | solution.py:394
  57.2 1.2 %collective-permute-start.8 = (f32[8,256]{1,0:T(8,128)S(1)}, f32[8,256]{1,0:T(8,128)S(1)}, u32[]{:S(2)}, u32[]{:S(2)}) collective-permute-start(f32[8,256]{1,0:T(8,128)S(1)} %get-tuple-element.56.here_ref), channel_id=1, source_target_pairs={{0,1},{1,0},{2,3},{3,2},{4,5},{5,4},{6,7},{7,6},{8,9},{9,8},{10,11... | collective-permute-start | bytes 24584 | tf_op jit(solution)/shard_map/ppermute | solution.py:394

commit v6 on v5

--- a/solution.py
+++ b/solution.py
@@ -12,13 +12,13 @@
 I32 = jnp.int32
 LANES = 128
 VMEM = 24 * 2**20
-OUT = (7, 14, 5, 13, 8, 10, 15, 11, 0, 3, 9, 1, 2, 12, 6, 4)
+OUT = (7, 14, 5, 13, 8, 10, 15, 11, 0, 2, 3, 1, 9, 12, 6, 4)
 BACK = (4, 0, 5, 6, 8, 12, 2, 3, 1, 11, 9, 14, 15, 10, 13, 7)
 
 
-def call(kernel, outs, *args, flops=0, smem=(), hbm=(), out_hbm=(), free=(), out_free=(), scratch=()):
+def call(kernel, outs, *args, flops=0, hbm=(), out_hbm=(), free=(), out_free=(), scratch=()):
     moved = sum(a.size * a.dtype.itemsize for a in args) + sum(o.size * o.dtype.itemsize for o in outs)
-    spaces = [pltpu.SMEM if k in smem else pltpu.HBM if k in hbm else pltpu.VMEM for k in range(len(args))]
+    spaces = [pltpu.HBM if k in hbm else pltpu.VMEM for k in range(len(args))]
     out_spaces = [pltpu.HBM if k in out_hbm else pltpu.VMEM for k in range(len(outs))]
     return pl.pallas_call(
         kernel,
@@ -33,7 +33,7 @@
 
 
 def placed(value, space, free=False):
-    return value if free or space is pltpu.SMEM else pltpu.with_memory_space_constraint(value, space)
+    return value if free else pltpu.with_memory_space_constraint(value, space)
 
 
 def shape(dims, dtype):
@@ -136,12 +136,12 @@
         c.wait()
 
 
-def split_kernel(keep, self_ref, neg_ref, old_ref, bank_ref, neg_col_ref, old_col_ref, held_ref, parts_ref, spread_ref, bank_buf, sem):
+def split_kernel(keep, neg_ref, old_ref, bank_ref, neg_col_ref, old_col_ref, held_ref, parts_ref, spread_ref, bank_buf, sem):
     owned, width = bank_buf.shape
     negs = neg_ref.shape[1]
     load = pltpu.make_async_copy(bank_ref, bank_buf, sem)
     load.start()
-    me = self_ref[0]
+    me = lax.axis_index("dp").astype(I32)
     wanted = neg_ref[pl.ds(me, 1), :] - me * owned
     wanted = jnp.concatenate([wanted] * (LANES // negs), axis=1)
     neg_col = id_col(wanted)[0:negs, :]
@@ -229,7 +229,7 @@
 
 
 def scale_kernel(
-    capacity, self_ref, ids_ref, neg_ref, count_ref, old_ref, pack_ref, new_ref, weight_ref, other_ref,
+    capacity, ids_ref, neg_ref, count_ref, old_ref, pack_ref, new_ref, weight_ref, other_ref,
     full_ref, own_ref, dist_ref, out_ref, own_buf, full_buf, buf, sems,
 ):
     slots, width = new_ref.shape
@@ -249,7 +249,7 @@
     other = (other_ref[0:negs, :] / conc).astype(BF16)
     full_buf[:, 0:width] = mine
     full_buf[:, width:] = other
-    first = self_ref[1] == 0
+    first = lax.axis_index("mp") == 0
     own_buf[:, 0:width] = jnp.where(first, mine[0:half], mine[half:])
     own_buf[:, width:] = jnp.where(first, other[0:half], other[half:])
     copies = [pltpu.make_async_copy(full_buf, full_ref, sems.at[0]), pltpu.make_async_copy(own_buf, own_ref, sems.at[1])]
@@ -358,34 +358,36 @@
     part_ref[...] = jnp.broadcast_to(part, part_ref.shape)
 
 
-def factor_kernel(self_ref, part_ref, far_ref, here_ref, there_ref, loss_ref, factor_ref):
+def factor_kernel(part_ref, far_ref, here_ref, there_ref, line_ref, factor_ref):
     rows = part_ref.shape[1]
-    first = self_ref[1] == 0
+    first = lax.axis_index("mp") == 0
     here, there = here_ref[0:2, :], there_ref[0:2, :]
     low = jnp.where(first, here, there)
     high = jnp.where(first, there, here)
     positive = part_ref[0:1, :] + far_ref[0:1, :]
     top = jnp.maximum(jnp.maximum(low[0:1], high[0:1]), positive)
-    exppos = jnp.exp(positive - top)
-    total = low[1:2] * jnp.exp(low[0:1] - top) + high[1:2] * jnp.exp(high[0:1] - top) + exppos
-    loss_ref[...] = jnp.log(total) + top - positive
-    factors = jnp.concatenate(
-        [jnp.exp(here[0:1] - top) / total, jnp.exp(there[0:1] - top) / total, exppos / total - 1.0], axis=0
-    )
-    factor_ref[...] = jnp.transpose(jnp.concatenate([factors, jnp.zeros((LANES - 3, rows), F32)], axis=0))
-
-
-def final_kernel(factor_ref, rows_ref, keep_ref, sent_ref, lost_ref, grad_ref, loss_ref, grad_buf, sems):
+    first_exp, last_exp, exppos = jnp.exp(low[0:1] - top), jnp.exp(high[0:1] - top), jnp.exp(positive - top)
+    total = low[1:2] * first_exp + high[1:2] * last_exp + exppos
+    once = 1.0 / total
+    line_ref[...] = jnp.concatenate([total, top - positive], axis=0)
+    mine, other = jnp.where(first, first_exp, last_exp) * once, jnp.where(first, last_exp, first_exp) * once
+    factors = jnp.concatenate([mine, other, exppos * once - 1.0, jnp.zeros((LANES - 3, rows), F32)], axis=0)
+    factor_ref[...] = jnp.transpose(factors)
+
+
+def final_kernel(factor_ref, rows_ref, keep_ref, sent_ref, line_ref, grad_ref, loss_ref, grad_buf, loss_buf, sems):
     rows = keep_ref.shape[0]
     half = rows // 2
-    copies = [pltpu.make_async_copy(lost_ref, loss_ref, sems.at[2])]
-    copies[0].start()
+    copies = []
     for k in range(2):
         at = slice(k * half, (k + 1) * half)
         mine, other, pull = (factor_ref[at, j : j + 1] for j in range(3))
         grad_buf[at, :] = keep_ref[at, :] * mine + sent_ref[at, :] * other + pull * rows_ref[at, :].astype(F32)
         copies.append(pltpu.make_async_copy(grad_buf.at[at, :], grad_ref.at[at, :], sems.at[k]))
         copies[-1].start()
+    loss_buf[...] = jnp.log(line_ref[0:1, :]) + line_ref[1:2, :]
+    copies.append(pltpu.make_async_copy(loss_buf, loss_ref, sems.at[2]))
+    copies[-1].start()
     for c in copies:
         c.wait()
 
@@ -406,7 +408,6 @@
 
 def body(features, labels, queries, bank, old_conc, neg_index):
     count = lax.axis_size("dp")
-    me, core = lax.axis_index("dp"), lax.axis_index("mp")
     owned, width = bank.shape
     rows = features.shape[0]
     capacity = 3 * rows // count
@@ -415,7 +416,6 @@
     slots = count * stride
     negs = neg_index.shape[0] // count
     half = negs // 2
-    place = jnp.stack([me, core]).astype(I32)
     loads = [pltpu.VMEM((1, rows), I32), pltpu.VMEM((rows, width), BF16)]
 
     label_row = labels.reshape(1, rows)
@@ -435,7 +435,7 @@
             shape((negs, LANES), I32), shape((negs, LANES), F32), shape((negs, width), F32),
             shape((owned, 2 * width), BF16), shape((LANES, slots), BF16),
         ),
-        place, neg_index.reshape(count, negs), old_conc.reshape(1, owned), bank, smem=(0,), hbm=(3,), free=(1, 2),
+        neg_index.reshape(count, negs), old_conc.reshape(1, owned), bank, hbm=(2,), free=(0, 1),
         scratch=[pltpu.VMEM((owned, width), F32), pltpu.SemaphoreType.DMA],
     )
     extra = 8 * -(-slots // (8 * width))
@@ -459,7 +459,7 @@
             shape((negs, 2 * width), BF16), shape((half, 2 * width), BF16), shape((1, slots), F32),
             shape((count * capacity, width), BF16), shape((half, 2 * width), BF16),
         ),
-        place, ids, neg_col, neg_counts, old_col, pack, new, weights, swap(pack), smem=(0,), out_hbm=(0, 1, 3),
+        ids, neg_col, neg_counts, old_col, pack, new, weights, swap(pack), out_hbm=(0, 1, 3),
         scratch=[
             pltpu.VMEM((negs, 2 * width), BF16), pltpu.VMEM((count * capacity, width), BF16),
             pltpu.SemaphoreType.DMA((4,)),
@@ -496,16 +496,16 @@
     (sent,) = call(pull_kernel, (shape((rows, width), F32),), weight, all_negs, flops=flops)
     (keep,) = call(near_kernel, (shape((rows, width), F32),), sent, weight, all_negs, flops=flops)
     sent = swap(sent)
-    loss, factors = call(
+    line, factors = call(
         factor_kernel,
-        (shape((1, rows), F32), shape((rows, LANES), F32)),
-        place, part, swap(part), stats, far_stats, smem=(0,),
+        (shape((2, rows), F32), shape((rows, LANES), F32)),
+        part, swap(part), stats, far_stats,
     )
     grad, loss = call(
         final_kernel,
         (shape((rows, width), F32), shape((1, rows), F32)),
-        factors, found, keep, sent, loss, out_hbm=(0, 1),
-        scratch=[pltpu.VMEM((rows, width), F32), pltpu.SemaphoreType.DMA((3,))],
+        factors, found, keep, sent, line, out_hbm=(0, 1),
+        scratch=[pltpu.VMEM((rows, width), F32), pltpu.VMEM((1, rows), F32), pltpu.SemaphoreType.DMA((3,))],
     )
     return (new_bank, new_conc.reshape(owned), loss.reshape(rows), grad)
 

time: 60.5 us -> 59.4 us (0.982)
  Pallas kernels: 18.8 us -> 17.2 us
    pallas_call x13, Pallas kernels: 14.1 us -> 12.4 us  [call(): pl.pallas_call(kernel, out_shape=[o if k in out_free else space(o.shape,...]
  transfers between devices with their start and end apart: 12 -> 12, of which waited for: 5 -> 5; matrix products, arithmetic and copies ran while one was open for 0% -> 0% of each run, Pallas kernels for 16% -> 14%
where the time goes in v6:
time: 59.4 us; the launch traced here: 59 us
  starting transfers between devices  24 us (40%)
  Pallas kernels  17.2 us (29%)
  waiting for transfers between devices  16.9 us (28%)
  between operations  0.82 us (1%)
    all_to_all x2, waiting for transfers between devices, exchange(): lax.all_to_all(value, 'dp', split_axis=0, concat_axis=0, axis_index_group...  14.2 us
    all_to_all x2, starting transfers between devices, exchange(): lax.all_to_all(value, 'dp', split_axis=0, concat_axis=0, axis_index_group...  14 us
    pallas_call x13, Pallas kernels, call(): pl.pallas_call(kernel, out_shape=[o if k in out_free else space(o.shape,...  12.4 us
    ppermute x4, starting transfers between devices, two_hop(): lax.ppermute(value, ('dp', 'mp'), [(2 * k + c, 2 * (k ^ bits[c]) + c) for...  7.77 us
    pallas_call x1, Pallas kernels, owner_call(): pl.pallas_call(owner_kernel, grid=(owned // block,), in_specs=[pl.BlockSp...  4.72 us
    ppermute x5, waiting for transfers between devices, swap(): return lax.ppermute(value, 'mp', [(0, 1), (1, 0)])  1.82 us
    ppermute x1, starting transfers between devices, hop(): return lax.ppermute(value, 'dp', [(k, k ^ bits) for k in range(count)])  1.47 us
  transfers between devices with their start and end apart: 12, of which 5 were waited for; matrix products, arithmetic and copies ran while one was open for 0% of the time, Pallas kernels for 14%

profile of v6, /device:TPU:0, one launch (start us, length us, event | category | flops | bytes accessed | tf_op | source)
XLA Modules:
  0.0 59.0 jit_solution(8354751534283813135)
XLA Ops:
  0.7 2.1 %pack_kernel.1 = bf16[2432,128]{1,0:T(8,128)(2,1)} custom-call(s32[1,256]{1,0:T(1,128)} %bitcast.12, bf16[256,384]{1,0:T(8,128)(2,1)} %feat_ref.1), custom_call_target="tpu_custom_call" | custom-call | flops 150994944 | bytes 820224 | tf_op jit(solution)/shard_map/pack_kernel/pallas_call | solution.py:23
  2.8 8.8 %all-to-all-start = ((bf16[16,152,128]{2,1,0:T(8,128)(2,1)}), bf16[16,152,128]{2,1,0:T(8,128)(2,1)S(1)}, u32[]{:S(2)}, u32[]{:S(2)}) async-start(bf16[16,152,128]{2,1,0:T(8,128)(2,1)} %bitcast.14), calls=%async_computation | async-start | bytes 1245184 | tf_op jit(solution)/shard_map/all_to_all | solution.py:97
  11.6 0.1 collective-permute-start
  11.7 0.1 reshape.36.neg_ref
  11.8 2.3 %split_kernel.1 = (s32[64,128]{1,0:T(8,128)S(1)}, f32[64,128]{1,0:T(8,128)S(1)}, f32[64,384]{1,0:T(8,128)S(1)}, bf16[1024,768]{1,0:T(8,128)(2,1)S(1)}, bf16[128,768]{1,0:T(8,128)(2,1)S(1)}) custom-call(s32[16,64]{1,0:T(8,128)S(1)} %reshape.36.neg_ref, f32[1,1024]{1,0:T(1,128)S(1)} %bitcast.11, f32[1024,384]{1,0:T(8,128)} %bank_ref.3), custom_call_target="tpu_custom_call" | custom-call | bytes 3514368 | tf_op jit(solution)/shard_map/split_kernel/pallas_call | solution.py:23
  14.1 10.7 %all-to-all-done = bf16[16,152,128]{2,1,0:T(8,128)(2,1)S(1)} async-done(((bf16[16,152,128]{2,1,0:T(8,128)(2,1)}), bf16[16,152,128]{2,1,0:T(8,128)(2,1)S(1)}, u32[]{:S(2)}, u32[]{:S(2)}) %all-to-all-start) | async-done | bytes 622624 | tf_op jit(solution)/shard_map/all_to_all | solution.py:97
  24.9 3.1 %mean_kernel.1 = (s32[1,768]{1,0:T(1,128)S(1)}, f32[768,384]{1,0:T(8,128)S(1)}, f32[72,384]{1,0:T(8,128)S(1)}, bf16[768,512]{1,0:T(8,128)(2,1)S(1)}, f32[768,128]{1,0:T(8,128)S(1)}, /*index=5*/f32[64,128]{1,0:T(8,128)S(1)}) custom-call(bf16[256,384]{1,0:T(8,128)(2,1)} %copy-done, s32[64,128]{1,0:T(8,128)S(1)} %get-tuple-element.34.neg_ref, ...), custom_call_target="tpu_custom_call" | custom-call | flops 2415919104 | bytes 5225472 | tf_op jit(solution)/shard_map/mean_kernel/pallas_call | solution.py:23
  28.0 0.1 collective-permute-start.1
  28.0 0.3 prepare_kernel.1
  28.4 1.0 %collective-permute-done.1.other_ref = f32[72,384]{1,0:T(8,128)S(1)} collective-permute-done((f32[72,384]{1,0:T(8,128)S(1)}, f32[72,384]{1,0:T(8,128)S(1)}, u32[]{:S(2)}, u32[]{:S(2)}) %collective-permute-start.1) | collective-permute-done | bytes 110624 | tf_op jit(solution)/shard_map/ppermute | solution.py:396
  29.3 1.6 %scale_kernel.1 = (bf16[64,768]{1,0:T(8,128)(2,1)}, bf16[32,768]{1,0:T(8,128)(2,1)}, f32[1,768]{1,0:T(1,128)S(1)}, bf16[768,384]{1,0:T(8,128)(2,1)}, bf16[32,768]{1,0:T(8,128)(2,1)S(1)}) custom-call(s32[1,768]{1,0:T(1,128)S(1)} %get-tuple-element.38.ids_ref, s32[64,128]{1,0:T(8,128)S(1)} %get-tuple-element.34.neg_ref, ...), custom_call_target="tpu_custom_call" | custom-call | bytes 2684928 | tf_op jit(solution)/shard_map/scale_kernel/pallas_call | solution.py:23
  30.9 2.5 %collective-permute-start.3 = (bf16[64,768]{1,0:T(8,128)(2,1)}, bf16[64,768]{1,0:T(8,128)(2,1)S(1)}, u32[]{:S(2)}, u32[]{:S(2)}) collective-permute-start(bf16[64,768]{1,0:T(8,128)(2,1)} %get-tuple-element.54), channel_id=1, source_target_pairs={{0,8},{1,17},{2,10},{3,19},{4,12},{5,21},{6,14},{7,23},{8,0},{9,25... | collective-permute-start | bytes 294920 | tf_op jit(solution)/shard_map/ppermute | solution.py:404
  33.4 1.5 %collective-permute-start.4 = (bf16[32,768]{1,0:T(8,128)(2,1)}, bf16[32,768]{1,0:T(8,128)(2,1)S(1)}, u32[]{:S(2)}, u32[]{:S(2)}) collective-permute-start(bf16[32,768]{1,0:T(8,128)(2,1)} %get-tuple-element.55), channel_id=1, source_target_pairs={{0,24},{2,26},{4,28},{6,30},{8,16},{10,18},{12,20},{14,22},{16,8},... | collective-permute-start | bytes 147464 | tf_op jit(solution)/shard_map/ppermute | solution.py:400
  34.9 5.2 %all-to-all-start.1 = ((bf16[16,48,384]{2,1,0:T(8,128)(2,1)}), bf16[16,48,384]{2,1,0:T(8,128)(2,1)S(1)}, u32[]{:S(2)}, u32[]{:S(2)}) async-start(bf16[16,48,384]{2,1,0:T(8,128)(2,1)} %bitcast.15), calls=%async_computation.1 | async-start | bytes 1179648 | tf_op jit(solution)/shard_map/all_to_all | solution.py:97
  40.1 1.5 %collective-permute-start.5 = (bf16[128,768]{1,0:T(8,128)(2,1)S(1)}, bf16[128,768]{1,0:T(8,128)(2,1)S(1)}, u32[]{:S(2)}, u32[]{:S(2)}) collective-permute-start(bf16[128,768]{1,0:T(8,128)(2,1)S(1)} %join_kernel.1.refs_0_), channel_id=1, source_target_pairs={{0,2},{1,5},{2,0},{3,7},{4,6},{5,1},{6,4},{7,3},{8,10},{9,13},{10,... | collective-permute-start | bytes 589832 | tf_op jit(solution)/shard_map/ppermute | solution.py:404
  41.6 4.7 %owner_kernel.1 = (f32[1024,384]{1,0:T(8,128)}, f32[1,1024]{1,0:T(1,128)}) custom-call(s32[1,768]{1,0:T(1,128)S(1)} %get-tuple-element.38.ids_ref, f32[1,768]{1,0:T(1,128)S(1)} %get-tuple-element.45.dist_ref, bf16[768,512]{1,0:T(8,128)(2,1)S(1)} %copy-done.6, f32[1024,384]{1,0:T(8,128)} %bank_ref.3, f32[1,1024]{1,0:T(1,128)} %bitcast.10), custom_call_target="tpu_custom_call" | custom-call | flops 20000000000 | bytes 3145728 | tf_op jit(solution)/shard_map/owner_kernel/pallas_call | solution.py:310
  46.4 1.5 %collective-permute-start.6 = (bf16[128,768]{1,0:T(8,128)(2,1)S(1)}, bf16[128,768]{1,0:T(8,128)(2,1)S(1)}, u32[]{:S(2)}, u32[]{:S(2)}) collective-permute-start(bf16[128,768]{1,0:T(8,128)(2,1)S(1)} %join_kernel.1.refs_0_), channel_id=1, source_target_pairs={{0,4},{1,3},{2,6},{3,1},{4,0},{5,7},{6,2},{7,5},{8,12},{9,11},{10,... | collective-permute-start | bytes 589832 | tf_op jit(solution)/shard_map/ppermute | solution.py:404
  47.8 0.9 %collective-permute-done.5.value_ref = bf16[128,768]{1,0:T(8,128)(2,1)S(1)} collective-permute-done((bf16[128,768]{1,0:T(8,128)(2,1)S(1)}, bf16[128,768]{1,0:T(8,128)(2,1)S(1)}, u32[]{:S(2)}, u32[]{:S(2)}) %collective-permute-start.5) | collective-permute-done | bytes 196640 | tf_op jit(solution)/shard_map/ppermute | solution.py:404
  48.7 2.3 %collective-permute-start.7 = (bf16[128,768]{1,0:T(8,128)(2,1)S(1)}, bf16[128,768]{1,0:T(8,128)(2,1)S(1)}, u32[]{:S(2)}, u32[]{:S(2)}) collective-permute-start(bf16[128,768]{1,0:T(8,128)(2,1)S(1)} %again_kernel.1.refs_1_), channel_id=1, source_target_pairs={{0,4},{1,3},{2,6},{3,1},{4,0},{5,7},{6,2},{7,5},{8,12},{9,11},{10,... | collective-permute-start | bytes 589832 | tf_op jit(solution)/shard_map/ppermute | solution.py:404
  51.0 3.5 %all-to-all-done.1 = bf16[16,48,384]{2,1,0:T(8,128)(2,1)S(1)} async-done(((bf16[16,48,384]{2,1,0:T(8,128)(2,1)}), bf16[16,48,384]{2,1,0:T(8,128)(2,1)S(1)}, u32[]{:S(2)}, u32[]{:S(2)}) %all-to-all-start.1) | async-done | bytes 589856 | tf_op jit(solution)/shard_map/all_to_all | solution.py:97
  54.5 0.5 positive_kernel.1
  55.0 0.0 copy-done.1
  55.0 0.7 %logits_kernel.1 = (bf16[256,512]{1,0:T(8,128)(2,1)S(1)}, bf16[512,768]{1,0:T(8,128)(2,1)S(1)}, f32[8,256]{1,0:T(8,128)S(1)}) custom-call(f32[8,256]{1,0:T(8,128)S(1)} %get-tuple-element.52.after_ref.part_ref, bf16[256,384]{1,0:T(8,128)(2,1)S(1)} %get-tuple-element.50.query_ref.mine_ref, bf16[256,384]{1,0:T(8,128)(2,1)S(1)} %copy-done.1, ...), custom_call_target="tpu_custom_call" | custom-call | flops 201326592 | bytes 2244608 | tf_op jit(solution)/shard_map/logits_kernel/pallas_call | solution.py:23
  55.7 0.3 pull_kernel.1.after_ref
  56.0 0.1 collective-permute-start.9
  56.1 0.5 collective-permute-start.2
  56.6 0.1 collective-permute-start.8
  56.7 0.3 near_kernel.1.keep_ref
  57.0 0.9 %collective-permute-done.2.far_ref = f32[8,256]{1,0:T(8,128)S(1)} collective-permute-done((f32[8,256]{1,0:T(8,128)S(1)}, f32[8,256]{1,0:T(8,128)S(1)}, u32[]{:S(2)}, u32[]{:S(2)}) %collective-permute-start.2) | collective-permute-done | bytes 8224 | tf_op jit(solution)/shard_map/ppermute | solution.py:396
  57.9 0.0 collective-permute-done.8.there_ref
  57.9 0.2 factor_kernel.1
  58.0 0.9 %final_kernel.1 = (f32[256,384]{1,0:T(8,128)}, f32[1,256]{1,0:T(1,128)}) custom-call(f32[256,128]{1,0:T(8,128)S(1)} %get-tuple-element.57.factor_ref, bf16[256,384]{1,0:T(8,128)(2,1)S(1)} %get-tuple-element.58.rows_ref, f32[256,384]{1,0:T(8,128)S(1)} %near_kernel.1.keep_ref, f32[256,384]{1,0:T(8,128)S(1)} %collective-permute-done.9.sent_ref, ...), custom_call_target="tpu_custom_call" | custom-call | bytes 1510400 | tf_op jit(solution)/shard_map/final_kernel/pallas_call | solution.py:23
  (23 shorter events, 0.1 us)
Async XLA Ops:
  0.6 11.0 %copy-start.2 = (bf16[256,384]{1,0:T(8,128)(2,1)S(1)}, bf16[256,384]{1,0:T(8,128)(2,1)}, u32[]{:S(2)}) copy-start(bf16[256,384]{1,0:T(8,128)(2,1)} %query_ref.1) | copy-start | bytes 589828
  0.6 11.0 %copy-start.7 = (s32[1024]{0:T(1024)S(1)}, s32[1024]{0:T(1024)}, u32[]{:S(2)}) copy-start(s32[1024]{0:T(1024)} %param.11) | copy-start | bytes 12292
  0.7 11.1 %copy-start.3 = (f32[1024]{0:T(1024)S(1)}, f32[1024]{0:T(1024)}, u32[]{:S(2)}) copy-start(f32[1024]{0:T(1024)} %param.10) | copy-start | bytes 12292
  2.8 22.1 %all-to-all-start = ((bf16[16,152,128]{2,1,0:T(8,128)(2,1)}), bf16[16,152,128]{2,1,0:T(8,128)(2,1)S(1)}, u32[]{:S(2)}, u32[]{:S(2)}) async-start(bf16[16,152,128]{2,1,0:T(8,128)(2,1)} %bitcast.14), calls=%async_computation | async-start | bytes 1245184 | tf_op jit(solution)/shard_map/all_to_all | solution.py:97
  11.6 2.5 %collective-permute-start = (bf16[256,384]{1,0:T(8,128)(2,1)S(1)}, bf16[256,384]{1,0:T(8,128)(2,1)S(1)}, u32[]{:S(2)}, u32[]{:S(2)}) collective-permute-start(bf16[256,384]{1,0:T(8,128)(2,1)S(1)} %copy-done.2), channel_id=1, source_target_pairs={{0,1},{1,0},{2,3},{3,2},{4,5},{5,4},{6,7},{7,6},{8,9},{9,8},{10,11... | collective-permute-start | bytes 589832 | tf_op jit(solution)/shard_map/ppermute | solution.py:396
  14.1 10.7 %copy-start = (bf16[256,384]{1,0:T(8,128)(2,1)}, bf16[256,384]{1,0:T(8,128)(2,1)S(1)}, u32[]{:S(2)}) copy-start(bf16[256,384]{1,0:T(8,128)(2,1)S(1)} %collective-permute-done.after_ref.other_ref) | copy-start | bytes 589828
  24.9 3.2 %copy-start.4 = (s32[256]{0:T(256)S(1)}, s32[256]{0:T(256)}, u32[]{:S(2)}) copy-start(s32[256]{0:T(256)} %param.7) | copy-start | bytes 3076
  28.0 5.5 %copy-start.5 = (bf16[768,512]{1,0:T(8,128)(2,1)}, bf16[768,512]{1,0:T(8,128)(2,1)S(1)}, u32[]{:S(2)}) copy-start(bf16[768,512]{1,0:T(8,128)(2,1)S(1)} %get-tuple-element.46.got_ref) | copy-start | bytes 2359300
  28.0 1.4 %collective-permute-start.1 = (f32[72,384]{1,0:T(8,128)S(1)}, f32[72,384]{1,0:T(8,128)S(1)}, u32[]{:S(2)}, u32[]{:S(2)}) collective-permute-start(f32[72,384]{1,0:T(8,128)S(1)} %get-tuple-element.41.pack_ref), channel_id=1, source_target_pairs={{0,1},{1,0},{2,3},{3,2},{4,5},{5,4},{6,7},{7,6},{8,9},{9,8},{10,11... | collective-permute-start | bytes 331784 | tf_op jit(solution)/shard_map/ppermute | solution.py:396
  30.9 9.1 %collective-permute-start.3 = (bf16[64,768]{1,0:T(8,128)(2,1)}, bf16[64,768]{1,0:T(8,128)(2,1)S(1)}, u32[]{:S(2)}, u32[]{:S(2)}) collective-permute-start(bf16[64,768]{1,0:T(8,128)(2,1)} %get-tuple-element.54), channel_id=1, source_target_pairs={{0,8},{1,17},{2,10},{3,19},{4,12},{5,21},{6,14},{7,23},{8,0},{9,25... | collective-permute-start | bytes 294920 | tf_op jit(solution)/shard_map/ppermute | solution.py:404
  33.4 8.2 %copy-start.6 = (bf16[768,512]{1,0:T(8,128)(2,1)S(1)}, bf16[768,512]{1,0:T(8,128)(2,1)}, u32[]{:S(2)}) copy-start(bf16[768,512]{1,0:T(8,128)(2,1)} %copy-done.5) | copy-start | bytes 2359300
  33.4 6.6 %collective-permute-start.4 = (bf16[32,768]{1,0:T(8,128)(2,1)}, bf16[32,768]{1,0:T(8,128)(2,1)S(1)}, u32[]{:S(2)}, u32[]{:S(2)}) collective-permute-start(bf16[32,768]{1,0:T(8,128)(2,1)} %get-tuple-element.55), channel_id=1, source_target_pairs={{0,24},{2,26},{4,28},{6,30},{8,16},{10,18},{12,20},{14,22},{16,8},... | collective-permute-start | bytes 147464 | tf_op jit(solution)/shard_map/ppermute | solution.py:400
  34.9 19.6 %all-to-all-start.1 = ((bf16[16,48,384]{2,1,0:T(8,128)(2,1)}), bf16[16,48,384]{2,1,0:T(8,128)(2,1)S(1)}, u32[]{:S(2)}, u32[]{:S(2)}) async-start(bf16[16,48,384]{2,1,0:T(8,128)(2,1)} %bitcast.15), calls=%async_computation.1 | async-start | bytes 1179648 | tf_op jit(solution)/shard_map/all_to_all | solution.py:97
  40.1 8.6 %collective-permute-start.5 = (bf16[128,768]{1,0:T(8,128)(2,1)S(1)}, bf16[128,768]{1,0:T(8,128)(2,1)S(1)}, u32[]{:S(2)}, u32[]{:S(2)}) collective-permute-start(bf16[128,768]{1,0:T(8,128)(2,1)S(1)} %join_kernel.1.refs_0_), channel_id=1, source_target_pairs={{0,2},{1,5},{2,0},{3,7},{4,6},{5,1},{6,4},{7,3},{8,10},{9,13},{10,... | collective-permute-start | bytes 589832 | tf_op jit(solution)/shard_map/ppermute | solution.py:404
  41.6 13.4 %copy-start.1 = (bf16[256,384]{1,0:T(8,128)(2,1)S(1)}, bf16[256,384]{1,0:T(8,128)(2,1)}, u32[]{:S(2)}) copy-start(bf16[256,384]{1,0:T(8,128)(2,1)} %copy-done) | copy-start | bytes 589828
  46.4 8.7 %collective-permute-start.6 = (bf16[128,768]{1,0:T(8,128)(2,1)S(1)}, bf16[128,768]{1,0:T(8,128)(2,1)S(1)}, u32[]{:S(2)}, u32[]{:S(2)}) collective-permute-start(bf16[128,768]{1,0:T(8,128)(2,1)S(1)} %join_kernel.1.refs_0_), channel_id=1, source_target_pairs={{0,4},{1,3},{2,6},{3,1},{4,0},{5,7},{6,2},{7,5},{8,12},{9,11},{10,... | collective-permute-start | bytes 589832 | tf_op jit(solution)/shard_map/ppermute | solution.py:404
  48.7 6.3 %collective-permute-start.7 = (bf16[128,768]{1,0:T(8,128)(2,1)S(1)}, bf16[128,768]{1,0:T(8,128)(2,1)S(1)}, u32[]{:S(2)}, u32[]{:S(2)}) collective-permute-start(bf16[128,768]{1,0:T(8,128)(2,1)S(1)} %again_kernel.1.refs_1_), channel_id=1, source_target_pairs={{0,4},{1,3},{2,6},{3,1},{4,0},{5,7},{6,2},{7,5},{8,12},{9,11},{10,... | collective-permute-start | bytes 589832 | tf_op jit(solution)/shard_map/ppermute | solution.py:404
  56.0 2.0 %collective-permute-start.9 = (f32[256,384]{1,0:T(8,128)S(1)}, f32[256,384]{1,0:T(8,128)S(1)}, u32[]{:S(2)}, u32[]{:S(2)}) collective-permute-start(f32[256,384]{1,0:T(8,128)S(1)} %pull_kernel.1.after_ref), channel_id=1, source_target_pairs={{0,1},{1,0},{2,3},{3,2},{4,5},{5,4},{6,7},{7,6},{8,9},{9,8},{10,11... | collective-permute-start | bytes 1179656 | tf_op jit(solution)/shard_map/ppermute | solution.py:396
  56.1 1.7 %collective-permute-start.2 = (f32[8,256]{1,0:T(8,128)S(1)}, f32[8,256]{1,0:T(8,128)S(1)}, u32[]{:S(2)}, u32[]{:S(2)}) collective-permute-start(f32[8,256]{1,0:T(8,128)S(1)} %get-tuple-element.52.after_ref.part_ref), channel_id=1, source_target_pairs={{0,1},{1,0},{2,3},{3,2},{4,5},{5,4},{6,7},{7,6},{8,9},{9,8},{10,11... | collective-permute-start | bytes 24584 | tf_op jit(solution)/shard_map/ppermute | solution.py:396
  56.6 1.2 %collective-permute-start.8 = (f32[8,256]{1,0:T(8,128)S(1)}, f32[8,256]{1,0:T(8,128)S(1)}, u32[]{:S(2)}, u32[]{:S(2)}) collective-permute-start(f32[8,256]{1,0:T(8,128)S(1)} %get-tuple-element.56.here_ref), channel_id=1, source_target_pairs={{0,1},{1,0},{2,3},{3,2},{4,5},{5,4},{6,7},{7,6},{8,9},{9,8},{10,11... | collective-permute-start | bytes 24584 | tf_op jit(solution)/shard_map/ppermute | solution.py:396

commit v7 on v6

--- a/solution.py
+++ b/solution.py
@@ -12,8 +12,8 @@
 I32 = jnp.int32
 LANES = 128
 VMEM = 24 * 2**20
-OUT = (7, 14, 5, 13, 8, 10, 15, 11, 0, 2, 3, 1, 9, 12, 6, 4)
-BACK = (4, 0, 5, 6, 8, 12, 2, 3, 1, 11, 9, 14, 15, 10, 13, 7)
+OUT = (7, 14, 5, 13, 1, 10, 15, 11, 0, 2, 3, 9, 8, 12, 6, 4)
+BACK = (4, 0, 5, 6, 8, 12, 2, 3, 1, 11, 9, 13, 15, 10, 14, 7)
 
 
 def call(kernel, outs, *args, flops=0, hbm=(), out_hbm=(), free=(), out_free=(), scratch=()):
@@ -197,6 +197,9 @@
     got = rows_ref[...]
     col = id_col(ids)
     block = 256 if slots % 256 == 0 else slots
+    sums = nn(onehot(neg_ref[:, 0:1] == ids), got)
+    neg_count_ref[...] = sums[:, width:]
+    pack_ref[0:negs, :] = blend(held_ref[...], sums[:, 0:width], sums[:, width : width + 1])
     squares = []
     for k in range(slots // block):
         at = slice(k * block, (k + 1) * block)
@@ -206,11 +209,8 @@
         new = blend(picked[:, 0:width] + picked[:, width:], sums[:, 0:width], sums[:, width : width + 1])
         new_ref[at, :] = new
         differ = got[at, 0:width].astype(F32) - new
-        squares.append(jnp.sum(differ * differ, axis=1, keepdims=True))
-    squared = to_row(jnp.concatenate(squares, axis=0))
-    sums = nn(onehot(neg_ref[:, 0:1] == ids), got)
-    neg_count_ref[...] = sums[:, width:]
-    pack_ref[0:negs, :] = blend(held_ref[...], sums[:, 0:width], sums[:, width : width + 1])
+        squares.append(to_row(jnp.sum(differ * differ, axis=1, keepdims=True)))
+    squared = jnp.concatenate(squares, axis=1)
     for k in range(-(-slots // width)):
         piece = squared[:, k * width : min((k + 1) * width, slots)]
         pack_ref[negs + k : negs + k + 1, 0 : piece.shape[1]] = piece

time: 59.4 us -> 59.1 us (level)
  starting transfers between devices: 24 us -> 22.7 us
  waiting for transfers between devices: 16.9 us -> 18.1 us
    ppermute x4, starting transfers between devices: 7.77 us -> 5.74 us  [two_hop(): lax.ppermute(value, ('dp', 'mp'), [(2 * k + c, 2 * (k ^ bits[c]) + c) for...]
    all_to_all x2, waiting for transfers between devices: 14.2 us -> 15.7 us  [exchange(): lax.all_to_all(value, 'dp', split_axis=0, concat_axis=0, axis_index_group...]
where the time goes in v7:
time: 59.1 us; the launch traced here: 58.7 us
  starting transfers between devices  22.7 us (38%)
  waiting for transfers between devices  18.1 us (31%)
  Pallas kernels  16.9 us (29%)
  between operations  0.82 us (1%)
    all_to_all x2, waiting for transfers between devices, exchange(): lax.all_to_all(value, 'dp', split_axis=0, concat_axis=0, axis_index_group...  15.7 us
    all_to_all x2, starting transfers between devices, exchange(): lax.all_to_all(value, 'dp', split_axis=0, concat_axis=0, axis_index_group...  14.2 us
    pallas_call x13, Pallas kernels, call(): pl.pallas_call(kernel, out_shape=[o if k in out_free else space(o.shape,...  12.2 us
    ppermute x4, starting transfers between devices, two_hop(): lax.ppermute(value, ('dp', 'mp'), [(2 * k + c, 2 * (k ^ bits[c]) + c) for...  5.74 us
    pallas_call x1, Pallas kernels, owner_call(): pl.pallas_call(owner_kernel, grid=(owned // block,), in_specs=[pl.BlockSp...  4.72 us
    ppermute x1, starting transfers between devices, hop(): return lax.ppermute(value, 'dp', [(k, k ^ bits) for k in range(count)])  1.96 us
    ppermute x5, waiting for transfers between devices, swap(): return lax.ppermute(value, 'mp', [(0, 1), (1, 0)])  1.82 us
  transfers between devices with their start and end apart: 12, of which 5 were waited for; matrix products, arithmetic and copies ran while one was open for 0% of the time, Pallas kernels for 14%

profile of v7, /device:TPU:0, one launch (start us, length us, event | category | flops | bytes accessed | tf_op | source)
XLA Modules:
  0.0 58.7 jit_solution(11617881517158654802)
XLA Ops:
  0.7 2.1 %pack_kernel.1 = bf16[2432,128]{1,0:T(8,128)(2,1)} custom-call(s32[1,256]{1,0:T(1,128)} %bitcast.12, bf16[256,384]{1,0:T(8,128)(2,1)} %feat_ref.1), custom_call_target="tpu_custom_call" | custom-call | flops 150994944 | bytes 820224 | tf_op jit(solution)/shard_map/pack_kernel/pallas_call | solution.py:23
  2.8 8.8 %all-to-all-start = ((bf16[16,152,128]{2,1,0:T(8,128)(2,1)}), bf16[16,152,128]{2,1,0:T(8,128)(2,1)S(1)}, u32[]{:S(2)}, u32[]{:S(2)}) async-start(bf16[16,152,128]{2,1,0:T(8,128)(2,1)} %bitcast.14), calls=%async_computation | async-start | bytes 1245184 | tf_op jit(solution)/shard_map/all_to_all | solution.py:97
  11.6 0.1 collective-permute-start
  11.7 0.1 reshape.36.neg_ref
  11.8 2.3 %split_kernel.1 = (s32[64,128]{1,0:T(8,128)S(1)}, f32[64,128]{1,0:T(8,128)S(1)}, f32[64,384]{1,0:T(8,128)S(1)}, bf16[1024,768]{1,0:T(8,128)(2,1)S(1)}, bf16[128,768]{1,0:T(8,128)(2,1)S(1)}) custom-call(s32[16,64]{1,0:T(8,128)S(1)} %reshape.36.neg_ref, f32[1,1024]{1,0:T(1,128)S(1)} %bitcast.11, f32[1024,384]{1,0:T(8,128)} %bank_ref.3), custom_call_target="tpu_custom_call" | custom-call | bytes 3514368 | tf_op jit(solution)/shard_map/split_kernel/pallas_call | solution.py:23
  14.1 12.2 %all-to-all-done = bf16[16,152,128]{2,1,0:T(8,128)(2,1)S(1)} async-done(((bf16[16,152,128]{2,1,0:T(8,128)(2,1)}), bf16[16,152,128]{2,1,0:T(8,128)(2,1)S(1)}, u32[]{:S(2)}, u32[]{:S(2)}) %all-to-all-start) | async-done | bytes 622624 | tf_op jit(solution)/shard_map/all_to_all | solution.py:97
  26.3 2.9 %mean_kernel.1 = (s32[1,768]{1,0:T(1,128)S(1)}, f32[768,384]{1,0:T(8,128)S(1)}, f32[72,384]{1,0:T(8,128)S(1)}, bf16[768,512]{1,0:T(8,128)(2,1)S(1)}, f32[768,128]{1,0:T(8,128)S(1)}, /*index=5*/f32[64,128]{1,0:T(8,128)S(1)}) custom-call(bf16[256,384]{1,0:T(8,128)(2,1)} %copy-done, s32[64,128]{1,0:T(8,128)S(1)} %get-tuple-element.34.neg_ref, ...), custom_call_target="tpu_custom_call" | custom-call | flops 2415919104 | bytes 5225472 | tf_op jit(solution)/shard_map/mean_kernel/pallas_call | solution.py:23
  29.2 0.1 collective-permute-start.1
  29.3 0.3 prepare_kernel.1
  29.6 1.0 %collective-permute-done.1.other_ref = f32[72,384]{1,0:T(8,128)S(1)} collective-permute-done((f32[72,384]{1,0:T(8,128)S(1)}, f32[72,384]{1,0:T(8,128)S(1)}, u32[]{:S(2)}, u32[]{:S(2)}) %collective-permute-start.1) | collective-permute-done | bytes 110624 | tf_op jit(solution)/shard_map/ppermute | solution.py:396
  30.6 1.6 %scale_kernel.1 = (bf16[64,768]{1,0:T(8,128)(2,1)}, bf16[32,768]{1,0:T(8,128)(2,1)}, f32[1,768]{1,0:T(1,128)S(1)}, bf16[768,384]{1,0:T(8,128)(2,1)}, bf16[32,768]{1,0:T(8,128)(2,1)S(1)}) custom-call(s32[1,768]{1,0:T(1,128)S(1)} %get-tuple-element.38.ids_ref, s32[64,128]{1,0:T(8,128)S(1)} %get-tuple-element.34.neg_ref, ...), custom_call_target="tpu_custom_call" | custom-call | bytes 2684928 | tf_op jit(solution)/shard_map/scale_kernel/pallas_call | solution.py:23
  32.1 0.2 collective-permute-start.3
  32.4 2.0 %collective-permute-start.4 = (bf16[32,768]{1,0:T(8,128)(2,1)}, bf16[32,768]{1,0:T(8,128)(2,1)S(1)}, u32[]{:S(2)}, u32[]{:S(2)}) collective-permute-start(bf16[32,768]{1,0:T(8,128)(2,1)} %get-tuple-element.55), channel_id=1, source_target_pairs={{0,24},{2,26},{4,28},{6,30},{8,16},{10,18},{12,20},{14,22},{16,8},... | collective-permute-start | bytes 147464 | tf_op jit(solution)/shard_map/ppermute | solution.py:400
  34.3 5.4 %all-to-all-start.1 = ((bf16[16,48,384]{2,1,0:T(8,128)(2,1)}), bf16[16,48,384]{2,1,0:T(8,128)(2,1)S(1)}, u32[]{:S(2)}, u32[]{:S(2)}) async-start(bf16[16,48,384]{2,1,0:T(8,128)(2,1)} %bitcast.15), calls=%async_computation.1 | async-start | bytes 1179648 | tf_op jit(solution)/shard_map/all_to_all | solution.py:97
  39.8 1.5 %collective-permute-start.5 = (bf16[128,768]{1,0:T(8,128)(2,1)S(1)}, bf16[128,768]{1,0:T(8,128)(2,1)S(1)}, u32[]{:S(2)}, u32[]{:S(2)}) collective-permute-start(bf16[128,768]{1,0:T(8,128)(2,1)S(1)} %join_kernel.1.refs_0_), channel_id=1, source_target_pairs={{0,2},{1,5},{2,0},{3,7},{4,6},{5,1},{6,4},{7,3},{8,10},{9,13},{10,... | collective-permute-start | bytes 589832 | tf_op jit(solution)/shard_map/ppermute | solution.py:404
  41.3 4.7 %owner_kernel.1 = (f32[1024,384]{1,0:T(8,128)}, f32[1,1024]{1,0:T(1,128)}) custom-call(s32[1,768]{1,0:T(1,128)S(1)} %get-tuple-element.38.ids_ref, f32[1,768]{1,0:T(1,128)S(1)} %get-tuple-element.45.dist_ref, bf16[768,512]{1,0:T(8,128)(2,1)S(1)} %copy-done.6, f32[1024,384]{1,0:T(8,128)} %bank_ref.3, f32[1,1024]{1,0:T(1,128)} %bitcast.10), custom_call_target="tpu_custom_call" | custom-call | flops 20000000000 | bytes 3145728 | tf_op jit(solution)/shard_map/owner_kernel/pallas_call | solution.py:310
  46.1 1.5 %collective-permute-start.6 = (bf16[128,768]{1,0:T(8,128)(2,1)S(1)}, bf16[128,768]{1,0:T(8,128)(2,1)S(1)}, u32[]{:S(2)}, u32[]{:S(2)}) collective-permute-start(bf16[128,768]{1,0:T(8,128)(2,1)S(1)} %join_kernel.1.refs_0_), channel_id=1, source_target_pairs={{0,4},{1,3},{2,6},{3,1},{4,0},{5,7},{6,2},{7,5},{8,12},{9,11},{10,... | collective-permute-start | bytes 589832 | tf_op jit(solution)/shard_map/ppermute | solution.py:404
  47.5 0.6 %collective-permute-done.5.value_ref = bf16[128,768]{1,0:T(8,128)(2,1)S(1)} collective-permute-done((bf16[128,768]{1,0:T(8,128)(2,1)S(1)}, bf16[128,768]{1,0:T(8,128)(2,1)S(1)}, u32[]{:S(2)}, u32[]{:S(2)}) %collective-permute-start.5) | collective-permute-done | bytes 196640 | tf_op jit(solution)/shard_map/ppermute | solution.py:404
  48.2 2.5 %collective-permute-start.7 = (bf16[128,768]{1,0:T(8,128)(2,1)S(1)}, bf16[128,768]{1,0:T(8,128)(2,1)S(1)}, u32[]{:S(2)}, u32[]{:S(2)}) collective-permute-start(bf16[128,768]{1,0:T(8,128)(2,1)S(1)} %again_kernel.1.refs_1_), channel_id=1, source_target_pairs={{0,4},{1,3},{2,6},{3,1},{4,0},{5,7},{6,2},{7,5},{8,12},{9,11},{10,... | collective-permute-start | bytes 589832 | tf_op jit(solution)/shard_map/ppermute | solution.py:404
  50.7 3.5 %all-to-all-done.1 = bf16[16,48,384]{2,1,0:T(8,128)(2,1)S(1)} async-done(((bf16[16,48,384]{2,1,0:T(8,128)(2,1)}), bf16[16,48,384]{2,1,0:T(8,128)(2,1)S(1)}, u32[]{:S(2)}, u32[]{:S(2)}) %all-to-all-start.1) | async-done | bytes 589856 | tf_op jit(solution)/shard_map/all_to_all | solution.py:97
  54.2 0.5 positive_kernel.1
  54.7 0.0 copy-done.1
  54.7 0.7 %logits_kernel.1 = (bf16[256,512]{1,0:T(8,128)(2,1)S(1)}, bf16[512,768]{1,0:T(8,128)(2,1)S(1)}, f32[8,256]{1,0:T(8,128)S(1)}) custom-call(f32[8,256]{1,0:T(8,128)S(1)} %get-tuple-element.52.after_ref.part_ref, bf16[256,384]{1,0:T(8,128)(2,1)S(1)} %get-tuple-element.50.query_ref.mine_ref, bf16[256,384]{1,0:T(8,128)(2,1)S(1)} %copy-done.1, ...), custom_call_target="tpu_custom_call" | custom-call | flops 201326592 | bytes 2244608 | tf_op jit(solution)/shard_map/logits_kernel/pallas_call | solution.py:23
  55.5 0.3 pull_kernel.1.after_ref
  55.8 0.1 collective-permute-start.9
  55.8 0.5 collective-permute-start.2
  56.3 0.1 collective-permute-start.8
  56.4 0.3 near_kernel.1.keep_ref
  56.7 0.8 %collective-permute-done.2.far_ref = f32[8,256]{1,0:T(8,128)S(1)} collective-permute-done((f32[8,256]{1,0:T(8,128)S(1)}, f32[8,256]{1,0:T(8,128)S(1)}, u32[]{:S(2)}, u32[]{:S(2)}) %collective-permute-start.2) | collective-permute-done | bytes 8224 | tf_op jit(solution)/shard_map/ppermute | solution.py:396
  57.6 0.0 collective-permute-done.8.there_ref
  57.6 0.2 factor_kernel.1
  57.8 0.9 %final_kernel.1 = (f32[256,384]{1,0:T(8,128)}, f32[1,256]{1,0:T(1,128)}) custom-call(f32[256,128]{1,0:T(8,128)S(1)} %get-tuple-element.57.factor_ref, bf16[256,384]{1,0:T(8,128)(2,1)S(1)} %get-tuple-element.58.rows_ref, f32[256,384]{1,0:T(8,128)S(1)} %near_kernel.1.keep_ref, f32[256,384]{1,0:T(8,128)S(1)} %collective-permute-done.9.sent_ref, ...), custom_call_target="tpu_custom_call" | custom-call | bytes 1510400 | tf_op jit(solution)/shard_map/final_kernel/pallas_call | solution.py:23
  (23 shorter events, 0.1 us)
Async XLA Ops:
  0.6 11.0 %copy-start.2 = (bf16[256,384]{1,0:T(8,128)(2,1)S(1)}, bf16[256,384]{1,0:T(8,128)(2,1)}, u32[]{:S(2)}) copy-start(bf16[256,384]{1,0:T(8,128)(2,1)} %query_ref.1) | copy-start | bytes 589828
  0.6 11.0 %copy-start.7 = (s32[1024]{0:T(1024)S(1)}, s32[1024]{0:T(1024)}, u32[]{:S(2)}) copy-start(s32[1024]{0:T(1024)} %param.11) | copy-start | bytes 12292
  0.7 11.1 %copy-start.3 = (f32[1024]{0:T(1024)S(1)}, f32[1024]{0:T(1024)}, u32[]{:S(2)}) copy-start(f32[1024]{0:T(1024)} %param.10) | copy-start | bytes 12292
  2.8 23.5 %all-to-all-start = ((bf16[16,152,128]{2,1,0:T(8,128)(2,1)}), bf16[16,152,128]{2,1,0:T(8,128)(2,1)S(1)}, u32[]{:S(2)}, u32[]{:S(2)}) async-start(bf16[16,152,128]{2,1,0:T(8,128)(2,1)} %bitcast.14), calls=%async_computation | async-start | bytes 1245184 | tf_op jit(solution)/shard_map/all_to_all | solution.py:97
  11.6 2.5 %collective-permute-start = (bf16[256,384]{1,0:T(8,128)(2,1)S(1)}, bf16[256,384]{1,0:T(8,128)(2,1)S(1)}, u32[]{:S(2)}, u32[]{:S(2)}) collective-permute-start(bf16[256,384]{1,0:T(8,128)(2,1)S(1)} %copy-done.2), channel_id=1, source_target_pairs={{0,1},{1,0},{2,3},{3,2},{4,5},{5,4},{6,7},{7,6},{8,9},{9,8},{10,11... | collective-permute-start | bytes 589832 | tf_op jit(solution)/shard_map/ppermute | solution.py:396
  14.1 12.2 %copy-start = (bf16[256,384]{1,0:T(8,128)(2,1)}, bf16[256,384]{1,0:T(8,128)(2,1)S(1)}, u32[]{:S(2)}) copy-start(bf16[256,384]{1,0:T(8,128)(2,1)S(1)} %collective-permute-done.after_ref.other_ref) | copy-start | bytes 589828
  26.3 2.9 %copy-start.4 = (s32[256]{0:T(256)S(1)}, s32[256]{0:T(256)}, u32[]{:S(2)}) copy-start(s32[256]{0:T(256)} %param.7) | copy-start | bytes 3076
  29.2 3.2 %copy-start.5 = (bf16[768,512]{1,0:T(8,128)(2,1)}, bf16[768,512]{1,0:T(8,128)(2,1)S(1)}, u32[]{:S(2)}) copy-start(bf16[768,512]{1,0:T(8,128)(2,1)S(1)} %get-tuple-element.46.got_ref) | copy-start | bytes 2359300
  29.2 1.4 %collective-permute-start.1 = (f32[72,384]{1,0:T(8,128)S(1)}, f32[72,384]{1,0:T(8,128)S(1)}, u32[]{:S(2)}, u32[]{:S(2)}) collective-permute-start(f32[72,384]{1,0:T(8,128)S(1)} %get-tuple-element.41.pack_ref), channel_id=1, source_target_pairs={{0,1},{1,0},{2,3},{3,2},{4,5},{5,4},{6,7},{7,6},{8,9},{9,8},{10,11... | collective-permute-start | bytes 331784 | tf_op jit(solution)/shard_map/ppermute | solution.py:396
  32.1 7.6 %collective-permute-start.3 = (bf16[64,768]{1,0:T(8,128)(2,1)}, bf16[64,768]{1,0:T(8,128)(2,1)S(1)}, u32[]{:S(2)}, u32[]{:S(2)}) collective-permute-start(bf16[64,768]{1,0:T(8,128)(2,1)} %get-tuple-element.54), channel_id=1, source_target_pairs={{0,8},{1,17},{2,10},{3,19},{4,12},{5,21},{6,14},{7,23},{8,0},{9,25... | collective-permute-start | bytes 294920 | tf_op jit(solution)/shard_map/ppermute | solution.py:404
  32.4 9.0 %copy-start.6 = (bf16[768,512]{1,0:T(8,128)(2,1)S(1)}, bf16[768,512]{1,0:T(8,128)(2,1)}, u32[]{:S(2)}) copy-start(bf16[768,512]{1,0:T(8,128)(2,1)} %copy-done.5) | copy-start | bytes 2359300
  32.4 7.4 %collective-permute-start.4 = (bf16[32,768]{1,0:T(8,128)(2,1)}, bf16[32,768]{1,0:T(8,128)(2,1)S(1)}, u32[]{:S(2)}, u32[]{:S(2)}) collective-permute-start(bf16[32,768]{1,0:T(8,128)(2,1)} %get-tuple-element.55), channel_id=1, source_target_pairs={{0,24},{2,26},{4,28},{6,30},{8,16},{10,18},{12,20},{14,22},{16,8},... | collective-permute-start | bytes 147464 | tf_op jit(solution)/shard_map/ppermute | solution.py:400
  34.3 19.8 %all-to-all-start.1 = ((bf16[16,48,384]{2,1,0:T(8,128)(2,1)}), bf16[16,48,384]{2,1,0:T(8,128)(2,1)S(1)}, u32[]{:S(2)}, u32[]{:S(2)}) async-start(bf16[16,48,384]{2,1,0:T(8,128)(2,1)} %bitcast.15), calls=%async_computation.1 | async-start | bytes 1179648 | tf_op jit(solution)/shard_map/all_to_all | solution.py:97
  39.8 8.3 %collective-permute-start.5 = (bf16[128,768]{1,0:T(8,128)(2,1)S(1)}, bf16[128,768]{1,0:T(8,128)(2,1)S(1)}, u32[]{:S(2)}, u32[]{:S(2)}) collective-permute-start(bf16[128,768]{1,0:T(8,128)(2,1)S(1)} %join_kernel.1.refs_0_), channel_id=1, source_target_pairs={{0,2},{1,5},{2,0},{3,7},{4,6},{5,1},{6,4},{7,3},{8,10},{9,13},{10,... | collective-permute-start | bytes 589832 | tf_op jit(solution)/shard_map/ppermute | solution.py:404
  41.3 13.4 %copy-start.1 = (bf16[256,384]{1,0:T(8,128)(2,1)S(1)}, bf16[256,384]{1,0:T(8,128)(2,1)}, u32[]{:S(2)}) copy-start(bf16[256,384]{1,0:T(8,128)(2,1)} %copy-done) | copy-start | bytes 589828
  46.1 8.7 %collective-permute-start.6 = (bf16[128,768]{1,0:T(8,128)(2,1)S(1)}, bf16[128,768]{1,0:T(8,128)(2,1)S(1)}, u32[]{:S(2)}, u32[]{:S(2)}) collective-permute-start(bf16[128,768]{1,0:T(8,128)(2,1)S(1)} %join_kernel.1.refs_0_), channel_id=1, source_target_pairs={{0,4},{1,3},{2,6},{3,1},{4,0},{5,7},{6,2},{7,5},{8,12},{9,11},{10,... | collective-permute-start | bytes 589832 | tf_op jit(solution)/shard_map/ppermute | solution.py:404
  48.2 6.6 %collective-permute-start.7 = (bf16[128,768]{1,0:T(8,128)(2,1)S(1)}, bf16[128,768]{1,0:T(8,128)(2,1)S(1)}, u32[]{:S(2)}, u32[]{:S(2)}) collective-permute-start(bf16[128,768]{1,0:T(8,128)(2,1)S(1)} %again_kernel.1.refs_1_), channel_id=1, source_target_pairs={{0,4},{1,3},{2,6},{3,1},{4,0},{5,7},{6,2},{7,5},{8,12},{9,11},{10,... | collective-permute-start | bytes 589832 | tf_op jit(solution)/shard_map/ppermute | solution.py:404
  55.8 2.0 %collective-permute-start.9 = (f32[256,384]{1,0:T(8,128)S(1)}, f32[256,384]{1,0:T(8,128)S(1)}, u32[]{:S(2)}, u32[]{:S(2)}) collective-permute-start(f32[256,384]{1,0:T(8,128)S(1)} %pull_kernel.1.after_ref), channel_id=1, source_target_pairs={{0,1},{1,0},{2,3},{3,2},{4,5},{5,4},{6,7},{7,6},{8,9},{9,8},{10,11... | collective-permute-start | bytes 1179656 | tf_op jit(solution)/shard_map/ppermute | solution.py:396
  55.8 1.7 %collective-permute-start.2 = (f32[8,256]{1,0:T(8,128)S(1)}, f32[8,256]{1,0:T(8,128)S(1)}, u32[]{:S(2)}, u32[]{:S(2)}) collective-permute-start(f32[8,256]{1,0:T(8,128)S(1)} %get-tuple-element.52.after_ref.part_ref), channel_id=1, source_target_pairs={{0,1},{1,0},{2,3},{3,2},{4,5},{5,4},{6,7},{7,6},{8,9},{9,8},{10,11... | collective-permute-start | bytes 24584 | tf_op jit(solution)/shard_map/ppermute | solution.py:396
  56.3 1.2 %collective-permute-start.8 = (f32[8,256]{1,0:T(8,128)S(1)}, f32[8,256]{1,0:T(8,128)S(1)}, u32[]{:S(2)}, u32[]{:S(2)}) collective-permute-start(f32[8,256]{1,0:T(8,128)S(1)} %get-tuple-element.56.here_ref), channel_id=1, source_target_pairs={{0,1},{1,0},{2,3},{3,2},{4,5},{5,4},{6,7},{7,6},{8,9},{9,8},{10,11... | collective-permute-start | bytes 24584 | tf_op jit(solution)/shard_map/ppermute | solution.py:396
